TPU v7x, 512 devices: a whole 4x8x8 slice. The times are simulated.
512 devices in a mesh: row: 16 (over z, core), col: 32 (over x, y).
Axes of the slice: x: 4, y: 8, z: 8, core: 2. Of those that a mesh axis runs over, the one named last changes fastest.
Arguments:
- iterate: bfloat16 [4608, 8192], P('row', 'col'), may hold values from -0.046875 to 0.046875
Outputs:
- update: bfloat16 [4608, 8192], P('row', 'col')
All inputs are finite; a program needn't handle non-finite values.
Results may differ from a plain program's by a relative error of at most 0.0061.
Values may be sent and summed in bfloat16 or wider, within the bound.
No kernel may reach another device: no remote copies, remote signals or barrier semaphores. Data moves between devices by JAX's collectives and lax.ppermute only.
A program may use at most 64 MiB of HBM per device.

v0:
```python
import math

import jax
import jax.numpy as jnp
from jax import lax
from jax.sharding import PartitionSpec as P

COLS = 8192


def spread(value, axis, source):
    kept = jnp.where(lax.axis_index(axis) == source, value, 0).astype(value.dtype)
    return lax.psum(kept, axis)


def times_transposed(left, right):
    return lax.dot_general(
        left, right, (((1,), (1,)), ((), ())), preferred_element_type=jnp.float32
    )


def on_device(iterate):
    rows_dev = iterate.shape[0]
    ratio = lax.axis_size("col") // lax.axis_size("row")
    col_index = lax.axis_index("col")
    half_rows = rows_dev // ratio
    row_panel = lax.all_gather(iterate, "col", axis=1, tiled=True)
    column_panel = lax.all_gather(iterate, "row", axis=0, tiled=True)
    own_rows = lax.dynamic_slice_in_dim(row_panel, col_index % ratio * half_rows, half_rows, 0)
    matched = spread(own_rows, "row", col_index // ratio)
    gram = times_transposed(row_panel, matched).astype(jnp.bfloat16)
    gram_panel = lax.all_gather(gram, "col", axis=1, tiled=True)
    gram_cols = lax.all_gather(gram, "row", axis=0, tiled=True)
    square = jnp.dot(gram_panel, gram_cols, preferred_element_type=jnp.float32)
    poly = (-4.775 * gram.astype(jnp.float32) + 2.0315 * square).astype(jnp.bfloat16)
    applied = jnp.dot(
        lax.all_gather(poly, "col", axis=1, tiled=True),
        column_panel,
        preferred_element_type=jnp.float32,
    )
    scale = math.sqrt(COLS)
    return (scale * (3.4445 * iterate.astype(jnp.float32) + applied)).astype(jnp.bfloat16)


def solution(mesh):
    placed = (P("row", "col"),)
    return jax.shard_map(
        on_device, mesh=mesh, in_specs=placed, out_specs=P("row", "col"), check_vma=False
    )
```

profile of v0, /device:TPU:1, one launch (start us, length us, event | category | flops | bytes accessed | tf_op | source)
XLA Modules:
  0.0 505.2 jit_solution(5886205332244965462)
XLA Ops:
  6.5 0.0 all-gather.7.cloned.1.call-start
  6.5 0.7 all-gather.7.cloned.1.call-update
  7.3 0.0 all-reduce.2.cloned.1.call-start
  7.3 96.2 %all-gather.7.cloned.1.call-done = bf16[288,8192]{1,0:T(8,128)(2,1)} async-done(((bf16[288,256]{1,0:T(8,128)(2,1)}), bf16[288,8192]{1,0:T(8,128)(2,1)}) %all-gather.7.cloned.1.call-update) | async-done | bytes 4718608 | tf_op jit(solution)/shard_map/all_gather | solution.py:27
  103.5 3.6 dynamic-slice_select_fusion
  107.1 0.0 all-reduce.2.cloned.1.call-update
  107.1 0.0 all-gather.15.cloned.1.call-start
  107.2 125.1 %all-reduce.2.cloned.1.call-done = bf16[144,8192]{1,0:T(8,128)(2,1)} async-done(((bf16[144,8192]{1,0:T(8,128)(2,1)}), bf16[144,8192]{1,0:T(8,128)(2,1)}) %all-reduce.2.cloned.1.call-update) | async-done | bytes 2359312 | tf_op jit(solution)/shard_map/psum | solution.py:13
  232.2 5.7 %convolution_convert_fusion = bf16[144,288]{1,0:T(8,128)(2,1)} fusion(bf16[144,8192]{1,0:T(8,128)(2,1)} %all-reduce.2.cloned.1.call-done, bf16[288,8192]{1,0:T(8,128)(2,1)} %all-gather.7.cloned.1.call-done), kind=kOutput, calls=%fused_computation.7 | convolution fusion | flops 679518720 | bytes 7160832 | tf_op jit(solution)/shard_map/dot_general | solution.py:17
  238.0 0.0 all-gather.15.cloned.1.call-update
  238.0 0.0 all-gather.9.cloned.1.call-start
  238.0 0.5 all-gather.9.cloned.1.call-update
  238.6 0.0 all-gather.13.cloned.1.call-start
  238.6 0.5 all-gather.13.cloned.1.call-update
  239.2 0.0 all-gather.11.cloned.1.call-start
  239.2 42.1 %all-gather.15.cloned.1.call-done = bf16[16,288,144]{1,2,0:T(8,128)(2,1)} async-done(((bf16[1,288,144]{1,2,0:T(8,128)(2,1)}), bf16[16,288,144]{1,2,0:T(8,128)(2,1)}) %all-gather.15.cloned.1.call-update) | async-done | bytes 1327120 | tf_op jit(solution)/shard_map/all_gather | solution.py:33
  281.3 1.9 copy.3
  283.2 0.0 copy-start
  283.2 1.9 reshape.1
  285.1 0.0 copy-start.1
  285.1 79.3 %all-gather.9.cloned.1.call-done = bf16[288,4608]{0,1:T(8,128)(2,1)} async-done(((bf16[288,144]{0,1:T(8,128)(2,1)}), bf16[288,4608]{0,1:T(8,128)(2,1)}) %all-gather.9.cloned.1.call-update) | async-done | bytes 2654224 | tf_op jit(solution)/shard_map/all_gather | solution.py:32
  364.3 0.0 copy-done
  364.3 3.5 fusion.3
  367.8 0.0 all-gather.11.cloned.1.call-update
  367.9 42.5 %all-gather.13.cloned.1.call-done = bf16[4608,256]{1,0:T(8,128)(2,1)} async-done(((bf16[288,256]{1,0:T(8,128)(2,1)}), bf16[4608,256]{1,0:T(8,128)(2,1)}) %all-gather.13.cloned.1.call-update) | async-done | bytes 2359312 | tf_op jit(solution)/shard_map/all_gather | solution.py:28
  410.3 83.5 %all-gather.11.cloned.1.call-done = bf16[288,4608]{0,1:T(8,128)(2,1)} async-done(((bf16[288,144]{0,1:T(8,128)(2,1)}), bf16[288,4608]{0,1:T(8,128)(2,1)}) %all-gather.11.cloned.1.call-update) | async-done | bytes 2654224 | tf_op jit(solution)/shard_map/all_gather | solution.py:37
  493.8 0.0 copy-done.1
  493.8 4.6 fusion.2
Async XLA Ops:
  6.5 97.0 %all-gather.7.cloned.1.call-start = ((), (), s32[]{:S(2)}) async-start(), calls=%async_computation | async-start | bytes 4866048 | tf_op jit(solution)/shard_map/all_gather | solution.py:27
  7.3 225.0 %all-reduce.2.cloned.1.call-start = ((), (), s32[]{:S(2)}) async-start(), calls=%async_computation.1 | async-start | bytes 4718592 | tf_op jit(solution)/shard_map/psum | solution.py:13
  107.1 174.2 %all-gather.15.cloned.1.call-start = ((), (), s32[]{:S(2)}) async-start(), calls=%async_computation.5 | async-start | bytes 1880064 | tf_op jit(solution)/shard_map/all_gather | solution.py:33
  238.0 126.3 %all-gather.9.cloned.1.call-start = ((), (), s32[]{:S(2)}) async-start(), calls=%async_computation.2 | async-start | bytes 3649536 | tf_op jit(solution)/shard_map/all_gather | solution.py:32
  238.6 171.7 %all-gather.13.cloned.1.call-start = ((), (), s32[]{:S(2)}) async-start(), calls=%async_computation.4 | async-start | bytes 2506752 | tf_op jit(solution)/shard_map/all_gather | solution.py:28
  239.2 254.6 %all-gather.11.cloned.1.call-start = ((), (), s32[]{:S(2)}) async-start(), calls=%async_computation.3 | async-start | bytes 3649536 | tf_op jit(solution)/shard_map/all_gather | solution.py:37
  283.2 81.2 %copy-start = (bf16[144,288]{1,0:T(8,128)(2,1)S(1)}, bf16[144,288]{1,0:T(8,128)(2,1)}, u32[]{:S(2)}) copy-start(bf16[144,288]{1,0:T(8,128)(2,1)} %convolution_convert_fusion) | copy-start | bytes 248836
  285.1 208.7 %copy-start.1 = (bf16[288,256]{1,0:T(8,128)(2,1)S(1)}, bf16[288,256]{1,0:T(8,128)(2,1)}, u32[]{:S(2)}) copy-start(bf16[288,256]{1,0:T(8,128)(2,1)} %param.1) | copy-start | bytes 442372
Sparse Core Ops, SparseCore 0:
  10.4 93.0 all-gather.6
  107.3 124.9 all-reduce.1
  238.1 43.1 all-gather.14
  284.3 79.9 all-gather.8
  366.3 43.9 all-gather.12
  413.3 80.3 all-gather.10
where the time goes:
time: 507 us; the launch traced here: 505 us
  waiting for transfers between devices  470 us (93%)
  matrix products  13.8 us (3%)
  between operations  13.5 us (3%)
    psum x1, waiting for transfers between devices, spread(): return lax.psum(kept, axis)  125 us
    all_gather x1, waiting for transfers between devices, on_device(): row_panel = lax.all_gather(iterate, 'col', axis=1, tiled=True)  96.2 us
    all_gather x1, waiting for transfers between devices, on_device(): lax.all_gather(poly, 'col', axis=1, tiled=True)  83.5 us
    all_gather x1, waiting for transfers between devices, on_device(): gram_panel = lax.all_gather(gram, 'col', axis=1, tiled=True)  79.3 us
    all_gather x1, waiting for transfers between devices, on_device(): column_panel = lax.all_gather(iterate, 'row', axis=0, tiled=True)  42.5 us
    all_gather x1, waiting for transfers between devices, on_device(): gram_cols = lax.all_gather(gram, 'row', axis=0, tiled=True)  42.1 us
  transfers between devices with their start and end apart: 6, of which 6 were waited for; matrix products, arithmetic and copies ran while one was open for 1% of the time, Pallas kernels for 0%

commit v1 on v0

v1 whole, which is shorter than its diff:
```python
import math

import jax
import jax.numpy as jnp
from jax import lax
from jax.sharding import Mesh, PartitionSpec as P

COLS = 8192
F32, BF16 = jnp.float32, jnp.bfloat16


def exchange(chunks, axis):
    return lax.all_to_all(chunks, axis, 0, 0)


def gather(block, axis):
    return exchange(jnp.broadcast_to(block, (lax.axis_size(axis), *block.shape)), axis)


def reduce_scatter(chunks, axis):
    return jnp.sum(exchange(chunks, axis).astype(F32), 0)


def swap_cores(block):
    return lax.ppermute(block, "core", [(0, 1), (1, 0)])


def on_device(own):
    rows, cols = own.shape
    nx, ny, nz = (lax.axis_size(a) for a in "xyz")
    quarter = rows // nx
    core = lax.axis_index("core")

    wide = gather(own, "x")
    wide_peer = swap_cores(wide)
    share = lax.dynamic_slice_in_dim(wide, lax.axis_index("x") * quarter, quarter, 1)
    panel = gather(share, "z")

    def gram_of(mine):
        return jnp.einsum("xrc,zxsc->rzs", mine, panel, preferred_element_type=F32)

    partial = jnp.concatenate([gram_of(wide), gram_of(wide_peer)], 0).astype(BF16)
    partial = partial.reshape(ny, 2 * rows // ny, nz * quarter)
    gram = gather(reduce_scatter(partial, "y").astype(BF16), "y")
    gram = gram.reshape(2, rows, nz, quarter)

    def applied(right):
        mine = jnp.einsum("rzs,zxsc->xrc", gram[0], right, preferred_element_type=F32)
        peer = jnp.einsum("rzs,zxsc->xrc", gram[1], right, preferred_element_type=F32)
        return mine + swap_cores(peer.astype(BF16)).astype(F32)

    first = applied(panel).reshape(nx, nx, quarter, cols).swapaxes(0, 1).astype(BF16)
    first = reduce_scatter(first, "x")
    inner = (-4.775 * share.astype(F32) + 2.0315 * first).astype(BF16)
    second = reduce_scatter(applied(gather(inner, "z")).astype(BF16), "x")
    scale = math.sqrt(COLS)
    return (scale * (3.4445 * own.astype(F32) + second)).astype(BF16)


def solution(mesh):
    fine = Mesh(mesh.devices.reshape(8, 2, 4, 8), ("z", "core", "x", "y"))
    placed = P(("z", "core"), ("x", "y"))
    return jax.shard_map(
        on_device, mesh=fine, in_specs=placed, out_specs=placed, check_vma=False
    )
```

time: 507 us -> 191 us (0.38)
  waiting for transfers between devices: 470 us -> 37 us
  blocking collectives: 0 us -> 106 us
  starting transfers between devices: 0.2 us -> 30.9 us
  between operations: 13.5 us -> 0.17 us
  matrix products: 13.8 us -> 6.31 us
    all_gather x5 -> x0, waiting for transfers between devices: 343 us -> none  [the longest x1 96.2 us: on_device(): row_panel = lax.all_gather(iterate, 'col', axis=1, tiled=True)]
    psum x1 -> x0, waiting for transfers between devices: 125 us -> none  [spread(): return lax.psum(kept, axis)]
    all_to_all x0 -> x5, blocking collectives: none -> 106 us  [exchange(): return lax.all_to_all(chunks, axis, 0, 0)]
    all_to_all x0 -> x2, waiting for transfers between devices: none -> 35.2 us  [exchange(): return lax.all_to_all(chunks, axis, 0, 0)]
    all_to_all x0 -> x2, starting transfers between devices: none -> 16.9 us  [exchange(): return lax.all_to_all(chunks, axis, 0, 0)]
    ppermute x0 -> x3, starting transfers between devices: none -> 14.1 us  [swap_cores(): return lax.ppermute(block, 'core', [(0, 1), (1, 0)])]
    dot_general x3 -> x6, matrix products: 13.8 us -> 6.31 us  [the longest x2 2.57 us: applied(): jnp.einsum('rzs,zxsc->xrc', gram[0], right, preferred_element_type=F32)]
  transfers between devices with their start and end apart: 6 -> 5, of which waited for: 6 -> 4; matrix products, arithmetic and copies ran while one was open for 1% -> 1% of each run, Pallas kernels for 0% -> 0%
where the time goes in v1:
time: 191 us; the launch traced here: 190 us
  blocking collectives  106 us (55%)
  waiting for transfers between devices  37 us (19%)
  starting transfers between devices  30.9 us (16%)
  local copies, waits for them, and re-layouts  8.69 us (5%)
  matrix products  6.31 us (3%)
    all_to_all x5, blocking collectives, exchange(): return lax.all_to_all(chunks, axis, 0, 0)  106 us
    all_to_all x2, waiting for transfers between devices, exchange(): return lax.all_to_all(chunks, axis, 0, 0)  35.2 us
    all_to_all x2, starting transfers between devices, exchange(): return lax.all_to_all(chunks, axis, 0, 0)  16.9 us
    ppermute x3, starting transfers between devices, swap_cores(): return lax.ppermute(block, 'core', [(0, 1), (1, 0)])  14.1 us
  transfers between devices with their start and end apart: 5, of which 4 were waited for; matrix products, arithmetic and copies ran while one was open for 1% of the time, Pallas kernels for 0%

profile of v1, /device:TPU:1, one launch (start us, length us, event | category | flops | bytes accessed | tf_op | source)
XLA Modules:
  0.0 190.3 jit_solution(2919595724809925280)
XLA Ops:
  0.0 1.8 broadcast_in_dim.12
  1.8 4.8 %all-to-all-start = ((bf16[4,288,256]{2,1,0:T(8,128)(2,1)}), bf16[4,288,256]{2,1,0:T(8,128)(2,1)S(1)}, u32[]{:S(2)}, u32[]{:S(2)}) async-start(bf16[4,288,256]{2,1,0:T(8,128)(2,1)} %broadcast_in_dim.12), calls=%async_computation | async-start | bytes 1179648 | tf_op jit(solution)/shard_map/all_to_all | solution.py:13
  6.6 7.3 %all-to-all-done = bf16[4,288,256]{2,1,0:T(8,128)(2,1)S(1)} async-done(((bf16[4,288,256]{2,1,0:T(8,128)(2,1)}), bf16[4,288,256]{2,1,0:T(8,128)(2,1)S(1)}, u32[]{:S(2)}, u32[]{:S(2)}) %all-to-all-start) | async-done | bytes 589856 | tf_op jit(solution)/shard_map/all_to_all | solution.py:13
  13.9 1.1 broadcast_in_dim.13
  15.0 12.0 %all-to-all-start.1 = ((bf16[8,4,72,256]{3,2,1,0:T(8,128)(2,1)}), bf16[8,4,72,256]{3,2,1,0:T(8,128)(2,1)S(1)}, u32[]{:S(2)}, u32[]{:S(2)}) async-start(bf16[8,4,72,256]{3,2,1,0:T(8,128)(2,1)} %broadcast_in_dim.13), calls=%async_computation.1 | async-start | bytes 2359296 | tf_op jit(solution)/shard_map/all_to_all | solution.py:13
  27.0 4.0 %collective-permute-start = (bf16[4,288,256]{2,1,0:T(8,128)(2,1)S(1)}, bf16[4,288,256]{2,1,0:T(8,128)(2,1)S(1)}, u32[]{:S(2)}, u32[]{:S(2)}) collective-permute-start(bf16[4,288,256]{2,1,0:T(8,128)(2,1)S(1)} %all-to-all-done), channel_id=1, source_target_pairs={{0,32},{32,0},{1,33},{33,1},{2,34},{34,2},{3,35},{35,3},{4,36},{36... | collective-permute-start | bytes 1769480 | tf_op jit(solution)/shard_map/ppermute | solution.py:25
  31.1 28.0 %all-to-all-done.1 = bf16[8,4,72,256]{3,2,1,0:T(8,128)(2,1)S(1)} async-done(((bf16[8,4,72,256]{3,2,1,0:T(8,128)(2,1)}), bf16[8,4,72,256]{3,2,1,0:T(8,128)(2,1)S(1)}, u32[]{:S(2)}, u32[]{:S(2)}) %all-to-all-start.1) | async-done | bytes 1179680 | tf_op jit(solution)/shard_map/all_to_all | solution.py:13
  59.0 0.8 fusion.7
  59.8 0.2 copy-done
  60.0 0.8 fusion.6
  60.8 0.2 pad_maximum_fusion
  61.1 1.1 reshape.22
  62.2 1.2 copy.27
  63.5 27.6 %all_to_all.35 = bf16[8,72,576]{2,1,0:T(8,128)(2,1)S(1)} all-to-all(bf16[8,72,576]{2,1,0:T(8,128)(2,1)S(1)} %copy.27), channel_id=1, replica_groups=mesh['z'=8,'core'=2,'x'=4,'y'=8] {'y'}, dimensions={0} | all-to-all | bytes 1327104 | tf_op jit(solution)/shard_map/all_to_all | solution.py:13
  91.3 21.8 %all_to_all.36 = bf16[8,72,576]{2,1,0:T(8,128)(2,1)S(1)} all-to-all(bf16[8,72,576]{2,1,0:T(8,128)(2,1)S(1)} %broadcast_in_dim.14), channel_id=1, replica_groups=mesh['z'=8,'core'=2,'x'=4,'y'=8] {'y'}, dimensions={0} | all-to-all | bytes 1327104 | tf_op jit(solution)/shard_map/all_to_all | solution.py:13
  113.1 0.6 squeeze.9
  113.7 0.4 copy.22
  114.1 0.2 copy-done.1
  114.4 1.5 fusion.5
  115.9 5.5 %collective-permute-start.1 = (bf16[4,288,256]{2,1,0:T(8,128)(2,1)}, bf16[4,288,256]{2,1,0:T(8,128)(2,1)}, u32[]{:S(2)}, u32[]{:S(2)}) collective-permute-start(bf16[4,288,256]{2,1,0:T(8,128)(2,1)} %fusion.5), channel_id=1, source_target_pairs={{0,32},{32,0},{1,33},{33,1},{2,34},{34,2},{3,35},{35,3},{4,36},{36... | collective-permute-start | bytes 1769480 | tf_op jit(solution)/shard_map/ppermute | solution.py:25
  121.4 0.6 squeeze.8
  122.0 1.2 copy.21
  123.2 0.2 collective-permute-done.1
  123.4 1.9 add_convert_fusion.1
  125.3 12.0 %all_to_all.37 = bf16[4,4,72,256]{3,2,1,0:T(8,128)(2,1)S(1)} all-to-all(bf16[4,4,72,256]{3,2,1,0:T(8,128)(2,1)S(1)} %bitcast.68), channel_id=1, replica_groups=mesh['z'=8,'core'=2,'x'=4,'y'=8] {'x'}, dimensions={0} | all-to-all | bytes 1179648 | tf_op jit(solution)/shard_map/all_to_all | solution.py:13
  137.6 32.3 %all_to_all.38 = bf16[8,4,72,256]{3,2,1,0:T(8,128)(2,1)S(1)} all-to-all(bf16[8,4,72,256]{3,2,1,0:T(8,128)(2,1)S(1)} %broadcast_in_dim.15), channel_id=1, replica_groups=mesh['z'=8,'core'=2,'x'=4,'y'=8] {'z'}, dimensions={0} | all-to-all | bytes 2359296 | tf_op jit(solution)/shard_map/all_to_all | solution.py:13
  169.9 0.7 fusion.4
  170.6 4.5 %collective-permute-start.2 = (bf16[4,288,256]{2,1,0:T(8,128)(2,1)S(1)}, bf16[4,288,256]{2,1,0:T(8,128)(2,1)S(1)}, u32[]{:S(2)}, u32[]{:S(2)}) collective-permute-start(bf16[4,288,256]{2,1,0:T(8,128)(2,1)S(1)} %fusion.4), channel_id=1, source_target_pairs={{0,32},{32,0},{1,33},{33,1},{2,34},{34,2},{3,35},{35,3},{4,36},{36... | collective-permute-start | bytes 1769480 | tf_op jit(solution)/shard_map/ppermute | solution.py:25
  175.0 1.6 collective-permute-done.2
  176.7 0.7 add_convert_fusion
  177.4 12.1 %all_to_all.39 = bf16[4,288,256]{2,1,0:T(8,128)(2,1)S(1)} all-to-all(bf16[4,288,256]{2,1,0:T(8,128)(2,1)S(1)} %add_convert_fusion), channel_id=1, replica_groups=mesh['z'=8,'core'=2,'x'=4,'y'=8] {'x'}, dimensions={0} | all-to-all | bytes 1179648 | tf_op jit(solution)/shard_map/all_to_all | solution.py:13
  189.6 0.7 multiply_convert_fusion
  (16 shorter events, 0.6 us)
Async XLA Ops:
  1.8 12.1 %all-to-all-start = ((bf16[4,288,256]{2,1,0:T(8,128)(2,1)}), bf16[4,288,256]{2,1,0:T(8,128)(2,1)S(1)}, u32[]{:S(2)}, u32[]{:S(2)}) async-start(bf16[4,288,256]{2,1,0:T(8,128)(2,1)} %broadcast_in_dim.12), calls=%async_computation | async-start | bytes 1179648 | tf_op jit(solution)/shard_map/all_to_all | solution.py:13
  15.0 44.0 %all-to-all-start.1 = ((bf16[8,4,72,256]{3,2,1,0:T(8,128)(2,1)}), bf16[8,4,72,256]{3,2,1,0:T(8,128)(2,1)S(1)}, u32[]{:S(2)}, u32[]{:S(2)}) async-start(bf16[8,4,72,256]{3,2,1,0:T(8,128)(2,1)} %broadcast_in_dim.13), calls=%async_computation.1 | async-start | bytes 2359296 | tf_op jit(solution)/shard_map/all_to_all | solution.py:13
  27.0 32.8 %collective-permute-start = (bf16[4,288,256]{2,1,0:T(8,128)(2,1)S(1)}, bf16[4,288,256]{2,1,0:T(8,128)(2,1)S(1)}, u32[]{:S(2)}, u32[]{:S(2)}) collective-permute-start(bf16[4,288,256]{2,1,0:T(8,128)(2,1)S(1)} %all-to-all-done), channel_id=1, source_target_pairs={{0,32},{32,0},{1,33},{33,1},{2,34},{34,2},{3,35},{35,3},{4,36},{36... | collective-permute-start | bytes 1769480 | tf_op jit(solution)/shard_map/ppermute | solution.py:25
  59.0 1.0 copy-start
  113.1 1.3 copy-start.1
  115.9 7.5 %collective-permute-start.1 = (bf16[4,288,256]{2,1,0:T(8,128)(2,1)}, bf16[4,288,256]{2,1,0:T(8,128)(2,1)}, u32[]{:S(2)}, u32[]{:S(2)}) collective-permute-start(bf16[4,288,256]{2,1,0:T(8,128)(2,1)} %fusion.5), channel_id=1, source_target_pairs={{0,32},{32,0},{1,33},{33,1},{2,34},{34,2},{3,35},{35,3},{4,36},{36... | collective-permute-start | bytes 1769480 | tf_op jit(solution)/shard_map/ppermute | solution.py:25
  169.9 6.8 %copy-start.3 = (bf16[288,8,72,1]{0,2,3,1:T(8,128)(2,1)S(1)}, bf16[288,8,72,1]{0,2,3,1:T(8,128)(2,1)}, u32[]{:S(2)}) copy-start(bf16[288,8,72,1]{0,2,3,1:T(8,128)(2,1)} %copy.21) | copy-start | bytes 995332
  170.6 6.1 %collective-permute-start.2 = (bf16[4,288,256]{2,1,0:T(8,128)(2,1)S(1)}, bf16[4,288,256]{2,1,0:T(8,128)(2,1)S(1)}, u32[]{:S(2)}, u32[]{:S(2)}) collective-permute-start(bf16[4,288,256]{2,1,0:T(8,128)(2,1)S(1)} %fusion.4), channel_id=1, source_target_pairs={{0,32},{32,0},{1,33},{33,1},{2,34},{34,2},{3,35},{35,3},{4,36},{36... | collective-permute-start | bytes 1769480 | tf_op jit(solution)/shard_map/ppermute | solution.py:25
  177.4 12.2 %copy-start.2 = (bf16[288,256]{1,0:T(8,128)(2,1)S(1)}, bf16[288,256]{1,0:T(8,128)(2,1)}, u32[]{:S(2)}) copy-start(bf16[288,256]{1,0:T(8,128)(2,1)} %param.1) | copy-start | bytes 442372

commit v2 on v1

v2 whole, which is shorter than its diff:
```python
import math

import jax
import jax.numpy as jnp
from jax import lax
from jax.sharding import Mesh, PartitionSpec as P

COLS = 8192
F32, BF16 = jnp.float32, jnp.bfloat16


def exchange(chunks, axis):
    return lax.all_to_all(chunks, axis, 0, 0)


def gather(block, axis):
    return exchange(jnp.broadcast_to(block, (lax.axis_size(axis), *block.shape)), axis)


def reduce_scatter(chunks, axis):
    parts = exchange(chunks, axis)
    return sum(parts[i].astype(F32) for i in range(parts.shape[0]))


def swap_cores(block):
    return lax.ppermute(block, "core", [(0, 1), (1, 0)])


def on_device(own):
    rows, cols = own.shape
    nx, ny, nz = (lax.axis_size(a) for a in "xyz")
    quarter = rows // nx

    split = own.reshape(1, nx, quarter, cols)
    spread = jnp.broadcast_to(split, (nz, nx, quarter, cols)).reshape(nz * nx, quarter, cols)
    panel = exchange(spread, ("z", "x")).reshape(nz, nx, quarter, cols)
    here = lax.axis_index("x")
    wide = jnp.zeros((nx, rows, cols), BF16)
    for hop in range(nx):
        moves = [(i, (i + hop) % nx) for i in range(nx)]
        block = lax.ppermute(own, "x", moves) if hop else own
        wide = lax.dynamic_update_index_in_dim(wide, block, lax.rem(here + (nx - hop), nx), 0)
    share = lax.dynamic_slice_in_dim(wide, here * quarter, quarter, 1)

    def both(mine):
        return mine, swap_cores(mine)

    panels = both(panel)
    partial = [
        jnp.einsum("xrc,zxsc->rzs", wide, p, preferred_element_type=F32)
        .astype(BF16)
        .reshape(rows, nz * quarter)
        for p in panels
    ]
    partial = jnp.concatenate(partial, 1).reshape(ny, rows // ny, 2 * nz * quarter)
    gram = gather(reduce_scatter(partial, "y").astype(BF16), "y")
    gram = gram.reshape(rows, 2, nz, quarter)

    def applied(right):
        return sum(
            jnp.einsum("rzs,zxsc->xrc", gram[:, i], p, preferred_element_type=F32)
            for i, p in enumerate(right)
        ).astype(BF16)

    first = applied(panels).reshape(nx, nx, quarter, cols).swapaxes(0, 1)
    first = reduce_scatter(first, "x")
    inner = (-4.775 * share.astype(F32) + 2.0315 * first).astype(BF16)
    second = reduce_scatter(applied(both(gather(inner, "z"))), "x")
    scale = math.sqrt(COLS)
    return (scale * (3.4445 * own.astype(F32) + second)).astype(BF16)


def solution(mesh):
    fine = Mesh(mesh.devices.reshape(8, 2, 4, 8), ("z", "core", "x", "y"))
    placed = P(("z", "core"), ("x", "y"))
    return jax.shard_map(
        on_device, mesh=fine, in_specs=placed, out_specs=placed, check_vma=False
    )
```

time: 191 us -> 179 us (0.937)
  blocking collectives: 106 us -> 90.7 us
  starting transfers between devices: 30.9 us -> 42.7 us
  waiting for transfers between devices: 37 us -> 27.1 us
    all_to_all x5 -> x4, blocking collectives: 106 us -> 90.7 us  [exchange(): return lax.all_to_all(chunks, axis, 0, 0)]
    ppermute x0 -> x3, starting transfers between devices: none -> 11.1 us  [on_device(): block = lax.ppermute(own, 'x', moves) if hop else own]
    all_to_all x2, waiting for transfers between devices: 35.2 us -> 24.7 us  [exchange(): return lax.all_to_all(chunks, axis, 0, 0)]
    reshape x0 -> x2, local copies, waits for them, and re-layouts: none -> 2.94 us  [the longest x1 2.09 us: on_device(): gram = gram.reshape(rows, 2, nz, quarter)]
    broadcast_in_dim x4 -> x2, local copies, waits for them, and re-layouts: 3 us -> 0.13 us  [gather(): jnp.broadcast_to(block, (lax.axis_size(axis), *block.shape))]
    squeeze x4 -> x0, local copies, waits for them, and re-layouts: 2.74 us -> none  [the longest x2 1.74 us: applied(): gram[0]]
    broadcast_in_dim x0 -> x2, local copies, waits for them, and re-layouts: none -> 2.05 us  [the longest x1 2.01 us: on_device(): jnp.broadcast_to(split, (nz, nx, quarter, cols))]
    ppermute x3 -> x2, starting transfers between devices: 14.1 us -> 13.5 us  [swap_cores(): return lax.ppermute(block, 'core', [(0, 1), (1, 0)])]
  transfers between devices with their start and end apart: 5 -> 7, of which waited for: 4 -> 4; matrix products, arithmetic and copies ran while one was open for 1% -> 1% of each run, Pallas kernels for 0% -> 0%
where the time goes in v2:
time: 179 us; the launch traced here: 178 us
  blocking collectives  90.7 us (51%)
  starting transfers between devices  42.7 us (24%)
  waiting for transfers between devices  27.1 us (15%)
  local copies, waits for them, and re-layouts  8.45 us (5%)
  matrix products  6.8 us (4%)
  other arithmetic  2.13 us (1%)
    all_to_all x4, blocking collectives, exchange(): return lax.all_to_all(chunks, axis, 0, 0)  90.7 us
    all_to_all x2, waiting for transfers between devices, exchange(): return lax.all_to_all(chunks, axis, 0, 0)  24.7 us
    all_to_all x2, starting transfers between devices, exchange(): return lax.all_to_all(chunks, axis, 0, 0)  18.1 us
    ppermute x2, starting transfers between devices, swap_cores(): return lax.ppermute(block, 'core', [(0, 1), (1, 0)])  13.5 us
    ppermute x3, starting transfers between devices, on_device(): block = lax.ppermute(own, 'x', moves) if hop else own  11.1 us
    dot_general x4, matrix products, applied(): jnp.einsum('rzs,zxsc->xrc', gram[:, i], p, preferred_element_type=F32)  3.94 us
  transfers between devices with their start and end apart: 7, of which 4 were waited for; matrix products, arithmetic and copies ran while one was open for 1% of the time, Pallas kernels for 0%

profile of v2, /device:TPU:1, one launch (start us, length us, event | category | flops | bytes accessed | tf_op | source)
XLA Modules:
  0.0 178.3 jit_solution(17282184825381418370)
XLA Ops:
  0.0 2.0 %broadcast_in_dim.35 = bf16[8,4,72,256]{3,2,1,0:T(8,128)(2,1)} broadcast(bf16[4,72,256]{2,1,0:T(8,128)(2,1)} %bitcast.95), dimensions={1,2,3} | broadcast | bytes 1327104 | tf_op jit(solution)/shard_map/broadcast_in_dim | solution.py:35
  2.0 13.8 %all-to-all-start = ((bf16[32,72,256]{2,1,0:T(8,128)(2,1)}), bf16[32,72,256]{2,1,0:T(8,128)(2,1)S(1)}, u32[]{:S(2)}, u32[]{:S(2)}) async-start(bf16[32,72,256]{2,1,0:T(8,128)(2,1)} %bitcast.6), calls=%async_computation | async-start | bytes 2359296 | tf_op jit(solution)/shard_map/all_to_all | solution.py:13
  15.9 4.6 %collective-permute-start.1 = (bf16[288,256]{1,0:T(8,128)(2,1)S(1)}, bf16[288,256]{1,0:T(8,128)(2,1)S(1)}, u32[]{:S(2)}, u32[]{:S(2)}) collective-permute-start(bf16[288,256]{1,0:T(8,128)(2,1)S(1)} %copy-done), channel_id=1, source_target_pairs={{0,16},{8,24},{16,0},{24,8},{1,17},{9,25},{17,1},{25,9},{2,18},{10... | collective-permute-start | bytes 442376 | tf_op jit(solution)/shard_map/ppermute | solution.py:41
  20.5 2.2 %collective-permute-start = (bf16[288,256]{1,0:T(8,128)(2,1)S(1)}, bf16[288,256]{1,0:T(8,128)(2,1)S(1)}, u32[]{:S(2)}, u32[]{:S(2)}) collective-permute-start(bf16[288,256]{1,0:T(8,128)(2,1)S(1)} %copy-done), channel_id=1, source_target_pairs={{0,8},{8,16},{16,24},{24,0},{1,9},{9,17},{17,25},{25,1},{2,10},{10... | collective-permute-start | bytes 442376 | tf_op jit(solution)/shard_map/ppermute | solution.py:41
  22.7 4.3 %collective-permute-start.2 = (bf16[288,256]{1,0:T(8,128)(2,1)S(1)}, bf16[288,256]{1,0:T(8,128)(2,1)S(1)}, u32[]{:S(2)}, u32[]{:S(2)}) collective-permute-start(bf16[288,256]{1,0:T(8,128)(2,1)S(1)} %copy-done), channel_id=1, source_target_pairs={{0,24},{8,0},{16,8},{24,16},{1,25},{9,1},{17,9},{25,17},{2,26},{10... | collective-permute-start | bytes 442376 | tf_op jit(solution)/shard_map/ppermute | solution.py:41
  27.1 17.4 %all-to-all-done = bf16[32,72,256]{2,1,0:T(8,128)(2,1)S(1)} async-done(((bf16[32,72,256]{2,1,0:T(8,128)(2,1)}), bf16[32,72,256]{2,1,0:T(8,128)(2,1)S(1)}, u32[]{:S(2)}, u32[]{:S(2)}) %all-to-all-start) | async-done | bytes 1179680 | tf_op jit(solution)/shard_map/all_to_all | solution.py:13
  44.5 5.0 %collective-permute-start.3 = (bf16[8,4,72,256]{3,2,1,0:T(8,128)(2,1)S(1)}, bf16[8,4,72,256]{3,2,1,0:T(8,128)(2,1)}, u32[]{:S(2)}, u32[]{:S(2)}) collective-permute-start(bf16[8,4,72,256]{3,2,1,0:T(8,128)(2,1)S(1)} %bitcast.96), channel_id=1, source_target_pairs={{0,32},{32,0},{1,33},{33,1},{2,34},{34,2},{3,35},{35,3},{4,36},{36... | collective-permute-start | bytes 3538952 | tf_op jit(solution)/shard_map/ppermute | solution.py:26
  49.7 0.8 fusion.4
  50.5 0.4 copy.12
  50.9 0.5 concatenate.8
  51.5 0.7 collective-permute-done.3
  52.1 2.1 %fusion.5 = bf16[288,8,72]{0,2,1:T(8,128)(2,1)S(1)} fusion(bf16[8,4,72,256]{3,2,1,0:T(8,128)(2,1)} %collective-permute-done.3, bf16[4,288,256]{2,1,0:T(8,128)(2,1)S(1)} %bitcast_dynamic-update-slice_fusion), kind=kOutput, calls=%fused_computation.11 | convolution fusion | flops 339904512 | bytes 2101248 | tf_op jit(solution)/shard_map/xrc,zxsc->rzs/dot_general | solution.py:50
  54.6 0.5 concatenate.9
  55.3 27.8 %all_to_all.30 = bf16[8,36,1152]{2,1,0:T(8,128)(2,1)S(1)} all-to-all(bf16[8,36,1152]{2,1,0:T(8,128)(2,1)S(1)} %pad_maximum_fusion), channel_id=1, replica_groups=mesh['z'=8,'core'=2,'x'=4,'y'=8] {'y'}, dimensions={0} | all-to-all | bytes 1327104 | tf_op jit(solution)/shard_map/all_to_all | solution.py:13
  83.3 22.2 %all_to_all.31 = bf16[8,36,1152]{2,1,0:T(8,128)(2,1)S(1)} all-to-all(bf16[8,36,1152]{2,1,0:T(8,128)(2,1)S(1)} %broadcast_in_dim.36), channel_id=1, replica_groups=mesh['z'=8,'core'=2,'x'=4,'y'=8] {'y'}, dimensions={0} | all-to-all | bytes 1327104 | tf_op jit(solution)/shard_map/all_to_all | solution.py:13
  105.5 2.1 %reshape.52 = bf16[288,2,8,72]{3,2,1,0:T(8,128)(2,1)S(1)} reshape(bf16[8,36,1152]{2,1,0:T(8,128)(2,1)S(1)} %all_to_all.31) | data formatting | bytes 1327104 | tf_op jit(solution)/shard_map/reshape | solution.py:57
  107.7 0.4 copy.29
  108.1 0.4 copy.28
  108.5 0.4 copy-done.2
  109.0 0.6 convolution_bitcast_fusion.1
  109.6 1.9 %fusion.2 = bf16[288,4,256]{2,0,1:T(8,128)(2,1)S(1)} fusion(f32[288,4,256]{2,0,1:T(8,128)S(1)} %convolution_bitcast_fusion.1, bf16[8,4,72,256]{3,2,1,0:T(8,128)(2,1)} %collective-permute-done.3, bf16[288,1,8,72]{0,3,2,1:T(8,128)(2,1)S(1)} %copy.29), kind=kOutput, calls=%fused_computation.6 | convolution fusion | flops 340328448 | bytes 3280896 | tf_op jit(solution)/shard_map/rzs,zxsc->xrc/dot_general | solution.py:61
  111.5 0.9 copy.31
  112.4 4.2 %all-to-all-start.3 = ((bf16[4,4,72,256]{3,2,1,0:T(8,128)(2,1)}), bf16[4,4,72,256]{3,2,1,0:T(8,128)(2,1)S(1)}, u32[]{:S(2)}, u32[]{:S(2)}) async-start(bf16[4,4,72,256]{3,2,1,0:T(8,128)(2,1)} %bitcast.94), calls=%async_computation.3 | async-start | bytes 1179648 | tf_op jit(solution)/shard_map/all_to_all | solution.py:13
  116.6 7.3 %all-to-all-done.3 = bf16[4,4,72,256]{3,2,1,0:T(8,128)(2,1)S(1)} async-done(((bf16[4,4,72,256]{3,2,1,0:T(8,128)(2,1)}), bf16[4,4,72,256]{3,2,1,0:T(8,128)(2,1)S(1)}, u32[]{:S(2)}, u32[]{:S(2)}) %all-to-all-start.3) | async-done | bytes 589856 | tf_op jit(solution)/shard_map/all_to_all | solution.py:13
  123.9 1.0 fusion.15
  125.0 28.7 %all_to_all.32 = bf16[8,4,72,256]{3,2,1,0:T(8,128)(2,1)S(1)} all-to-all(bf16[8,4,72,256]{3,2,1,0:T(8,128)(2,1)S(1)} %broadcast_in_dim.37), channel_id=1, replica_groups=mesh['z'=8,'core'=2,'x'=4,'y'=8] {'z'}, dimensions={0} | all-to-all | bytes 2359296 | tf_op jit(solution)/shard_map/all_to_all | solution.py:13
  153.8 8.5 %collective-permute-start.4 = (bf16[8,4,72,256]{3,2,0,1:T(8,128)(2,1)S(1)}, bf16[8,4,72,256]{3,2,0,1:T(8,128)(2,1)S(1)}, u32[]{:S(2)}, u32[]{:S(2)}) collective-permute-start(bf16[8,4,72,256]{3,2,0,1:T(8,128)(2,1)S(1)} %copy.20), channel_id=1, source_target_pairs={{0,32},{32,0},{1,33},{33,1},{2,34},{34,2},{3,35},{35,3},{4,36},{36... | collective-permute-start | bytes 3538952 | tf_op jit(solution)/shard_map/ppermute | solution.py:26
  162.3 0.7 convolution_bitcast_fusion.3
  163.0 1.8 collective-permute-done.4
  164.8 0.7 fusion.6
  165.5 12.0 %all_to_all.33 = bf16[4,288,256]{2,1,0:T(8,128)(2,1)S(1)} all-to-all(bf16[4,288,256]{2,1,0:T(8,128)(2,1)S(1)} %fusion.6), channel_id=1, replica_groups=mesh['z'=8,'core'=2,'x'=4,'y'=8] {'x'}, dimensions={0} | all-to-all | bytes 1179648 | tf_op jit(solution)/shard_map/all_to_all | solution.py:13
  177.5 0.8 fusion.14
  (22 shorter events, 1.1 us)
Async XLA Ops:
  2.0 13.9 %copy-start = (bf16[288,256]{1,0:T(8,128)(2,1)S(1)}, bf16[288,256]{1,0:T(8,128)(2,1)}, u32[]{:S(2)}) copy-start(bf16[288,256]{1,0:T(8,128)(2,1)} %param.1) | copy-start | bytes 442372
  2.0 42.5 %all-to-all-start = ((bf16[32,72,256]{2,1,0:T(8,128)(2,1)}), bf16[32,72,256]{2,1,0:T(8,128)(2,1)S(1)}, u32[]{:S(2)}, u32[]{:S(2)}) async-start(bf16[32,72,256]{2,1,0:T(8,128)(2,1)} %bitcast.6), calls=%async_computation | async-start | bytes 2359296 | tf_op jit(solution)/shard_map/all_to_all | solution.py:13
  15.9 33.8 %collective-permute-start.1 = (bf16[288,256]{1,0:T(8,128)(2,1)S(1)}, bf16[288,256]{1,0:T(8,128)(2,1)S(1)}, u32[]{:S(2)}, u32[]{:S(2)}) collective-permute-start(bf16[288,256]{1,0:T(8,128)(2,1)S(1)} %copy-done), channel_id=1, source_target_pairs={{0,16},{8,24},{16,0},{24,8},{1,17},{9,25},{17,1},{25,9},{2,18},{10... | collective-permute-start | bytes 442376 | tf_op jit(solution)/shard_map/ppermute | solution.py:41
  20.5 29.1 %collective-permute-start = (bf16[288,256]{1,0:T(8,128)(2,1)S(1)}, bf16[288,256]{1,0:T(8,128)(2,1)S(1)}, u32[]{:S(2)}, u32[]{:S(2)}) collective-permute-start(bf16[288,256]{1,0:T(8,128)(2,1)S(1)} %copy-done), channel_id=1, source_target_pairs={{0,8},{8,16},{16,24},{24,0},{1,9},{9,17},{17,25},{25,1},{2,10},{10... | collective-permute-start | bytes 442376 | tf_op jit(solution)/shard_map/ppermute | solution.py:41
  22.7 27.0 %collective-permute-start.2 = (bf16[288,256]{1,0:T(8,128)(2,1)S(1)}, bf16[288,256]{1,0:T(8,128)(2,1)S(1)}, u32[]{:S(2)}, u32[]{:S(2)}) collective-permute-start(bf16[288,256]{1,0:T(8,128)(2,1)S(1)} %copy-done), channel_id=1, source_target_pairs={{0,24},{8,0},{16,8},{24,16},{1,25},{9,1},{17,9},{25,17},{2,26},{10... | collective-permute-start | bytes 442376 | tf_op jit(solution)/shard_map/ppermute | solution.py:41
  44.5 6.0 %copy-start.1 = (bf16[32,72,256]{2,1,0:T(8,128)(2,1)}, bf16[32,72,256]{2,1,0:T(8,128)(2,1)S(1)}, u32[]{:S(2)}) copy-start(bf16[32,72,256]{2,1,0:T(8,128)(2,1)S(1)} %all-to-all-done) | copy-start | bytes 3538948
  44.5 7.6 %collective-permute-start.3 = (bf16[8,4,72,256]{3,2,1,0:T(8,128)(2,1)S(1)}, bf16[8,4,72,256]{3,2,1,0:T(8,128)(2,1)}, u32[]{:S(2)}, u32[]{:S(2)}) collective-permute-start(bf16[8,4,72,256]{3,2,1,0:T(8,128)(2,1)S(1)} %bitcast.96), channel_id=1, source_target_pairs={{0,32},{32,0},{1,33},{33,1},{2,34},{34,2},{3,35},{35,3},{4,36},{36... | collective-permute-start | bytes 3538952 | tf_op jit(solution)/shard_map/ppermute | solution.py:26
  49.7 2.4 %copy-start.3 = (bf16[4,288,256]{2,1,0:T(8,128)(2,1)}, bf16[4,288,256]{2,1,0:T(8,128)(2,1)S(1)}, u32[]{:S(2)}) copy-start(bf16[4,288,256]{2,1,0:T(8,128)(2,1)S(1)} %bitcast_dynamic-update-slice_fusion) | copy-start | bytes 1769476
  107.7 1.3 copy-start.2
  112.4 11.5 %all-to-all-start.3 = ((bf16[4,4,72,256]{3,2,1,0:T(8,128)(2,1)}), bf16[4,4,72,256]{3,2,1,0:T(8,128)(2,1)S(1)}, u32[]{:S(2)}, u32[]{:S(2)}) async-start(bf16[4,4,72,256]{3,2,1,0:T(8,128)(2,1)} %bitcast.94), calls=%async_computation.3 | async-start | bytes 1179648 | tf_op jit(solution)/shard_map/all_to_all | solution.py:13
  153.8 10.9 %collective-permute-start.4 = (bf16[8,4,72,256]{3,2,0,1:T(8,128)(2,1)S(1)}, bf16[8,4,72,256]{3,2,0,1:T(8,128)(2,1)S(1)}, u32[]{:S(2)}, u32[]{:S(2)}) collective-permute-start(bf16[8,4,72,256]{3,2,0,1:T(8,128)(2,1)S(1)} %copy.20), channel_id=1, source_target_pairs={{0,32},{32,0},{1,33},{33,1},{2,34},{34,2},{3,35},{35,3},{4,36},{36... | collective-permute-start | bytes 3538952 | tf_op jit(solution)/shard_map/ppermute | solution.py:26

commit v3 on v1

v3 whole, which is shorter than its diff:
```python
import math

import jax
import jax.numpy as jnp
from jax import lax
from jax.sharding import Mesh, PartitionSpec as P

COLS = 8192
SHIFT = 2.0
F32, BF16 = jnp.float32, jnp.bfloat16


def exchange(chunks, axis):
    return lax.all_to_all(chunks, axis, 0, 0)


def gather(block, axis):
    return exchange(jnp.broadcast_to(block, (lax.axis_size(axis), *block.shape)), axis)


def reduce_scatter(chunks, axis):
    parts = exchange(chunks, axis)
    return sum(parts[i].astype(F32) for i in range(parts.shape[0]))


def swap_cores(block):
    return lax.ppermute(block, "core", [(0, 1), (1, 0)])


def in_columns(block, parts):
    return block.reshape(block.shape[0], parts, -1).swapaxes(0, 1)


def on_device(own):
    rows, cols = own.shape
    nx, ny, nz = (lax.axis_size(a) for a in "xyz")
    quarter = rows // nx
    depth = nz * quarter
    here = lax.axis_index("x")

    split = own.reshape(1, nx, quarter, cols)
    spread = jnp.broadcast_to(split, (nz, nx, quarter, cols)).reshape(nz * nx, quarter, cols)
    panel = exchange(spread, ("z", "x")).reshape(nz, nx, quarter, cols)
    panel = jnp.concatenate([panel[:, x].reshape(depth, cols) for x in range(nx)], 1)
    blocks = [own]
    for hop in range(1, nx):
        blocks.append(lax.ppermute(own, "x", [(i, (i + hop) % nx) for i in range(nx)]))
    order = [lax.rem(here + (nx - x), nx) for x in range(nx)]
    wide = jnp.concatenate([lax.select_n(hop, *blocks) for hop in order], 1)
    share = lax.dynamic_slice_in_dim(wide, here * quarter, quarter, 0)

    left = jnp.concatenate([wide, swap_cores(wide)], 0)
    partial = lax.dot_general(left, panel, (((1,), (1,)), ((), ())), preferred_element_type=F32)
    partial = partial.astype(BF16).reshape(ny, 2 * rows // ny, depth)
    gram = gather(reduce_scatter(partial, "y").astype(BF16), "y").reshape(2 * rows, depth)

    def applied(right):
        peer = jnp.dot(gram[rows:], right, preferred_element_type=F32).astype(BF16)
        mine = jnp.dot(gram[:rows], right, preferred_element_type=F32)
        return mine + swap_cores(peer).astype(F32)

    first = reduce_scatter(applied(panel).astype(BF16).reshape(nx, quarter, nx * cols), "x")
    inner = (-4.775 * share.astype(F32) + 2.0315 * first).astype(BF16)
    right = gather(inner, "z").reshape(depth, nx * cols)
    mask = jnp.where(jnp.arange(nx) == here, SHIFT, 0.0)
    known = (mask[:, None, None] * share.astype(F32)).reshape(rows, nx * cols)
    second = reduce_scatter(in_columns((applied(right) + known).astype(BF16), nx), "x")
    scale = math.sqrt(COLS)
    return (scale * ((3.4445 - SHIFT) * own.astype(F32) + second)).astype(BF16)


def solution(mesh):
    fine = Mesh(mesh.devices.reshape(8, 2, 4, 8), ("z", "core", "x", "y"))
    placed = P(("z", "core"), ("x", "y"))
    return jax.shard_map(
        on_device, mesh=fine, in_specs=placed, out_specs=placed, check_vma=False
    )
```

time: 191 us -> 172 us (0.901)
  blocking collectives: 106 us -> 89.9 us
  starting transfers between devices: 30.9 us -> 45.5 us
  waiting for transfers between devices: 37 us -> 28 us
  local copies, waits for them, and re-layouts: 8.69 us -> 2.55 us
    all_to_all x2, waiting for transfers between devices: 35.2 us -> 15.7 us  [exchange(): return lax.all_to_all(chunks, axis, 0, 0)]
    all_to_all x5 -> x4, blocking collectives: 106 us -> 89.9 us  [exchange(): return lax.all_to_all(chunks, axis, 0, 0)]
    ppermute x0 -> x3, starting transfers between devices: none -> 10.5 us  [on_device(): lax.ppermute(own, 'x', [(i, (i + hop) % nx) for i in range(nx)])]
    ppermute x0 -> x3, waiting for transfers between devices: none -> 9.28 us  [on_device(): lax.ppermute(own, 'x', [(i, (i + hop) % nx) for i in range(nx)])]
    all_to_all x2, starting transfers between devices: 16.9 us -> 19.8 us  [exchange(): return lax.all_to_all(chunks, axis, 0, 0)]
    broadcast_in_dim x4 -> x2, local copies, waits for them, and re-layouts: 3 us -> 0.19 us  [gather(): jnp.broadcast_to(block, (lax.axis_size(axis), *block.shape))]
    squeeze x4 -> x0, local copies, waits for them, and re-layouts: 2.74 us -> none  [the longest x2 1.74 us: applied(): gram[0]]
    convert_element_type x3 -> x0, local copies, waits for them, and re-layouts: 2.41 us -> none  [the longest x2 2.37 us: on_device(): jnp.concatenate([gram_of(wide), gram_of(wide_peer)], 0).astype(BF16)]
  transfers between devices with their start and end apart: 5 -> 8, of which waited for: 4 -> 6; matrix products, arithmetic and copies ran while one was open for 1% -> 0% of each run, Pallas kernels for 0% -> 0%
where the time goes in v3:
time: 172 us
  blocking collectives  89.9 us (52%)
  starting transfers between devices  45.5 us (26%)
  waiting for transfers between devices  28 us (16%)
  matrix products  4.5 us (3%)
  local copies, waits for them, and re-layouts  2.55 us (1%)
    all_to_all x4, blocking collectives, exchange(): return lax.all_to_all(chunks, axis, 0, 0)  89.9 us
    all_to_all x2, starting transfers between devices, exchange(): return lax.all_to_all(chunks, axis, 0, 0)  19.8 us
    all_to_all x2, waiting for transfers between devices, exchange(): return lax.all_to_all(chunks, axis, 0, 0)  15.7 us
    ppermute x3, starting transfers between devices, swap_cores(): return lax.ppermute(block, 'core', [(0, 1), (1, 0)])  15.2 us
    ppermute x3, starting transfers between devices, on_device(): lax.ppermute(own, 'x', [(i, (i + hop) % nx) for i in range(nx)])  10.5 us
    ppermute x3, waiting for transfers between devices, on_device(): lax.ppermute(own, 'x', [(i, (i + hop) % nx) for i in range(nx)])  9.28 us
  transfers between devices with their start and end apart: 8, of which 6 were waited for; matrix products, arithmetic and copies ran while one was open for 0% of the time, Pallas kernels for 0%

profile of v3, /device:TPU:1, one launch (start us, length us, event | category | flops | bytes accessed | tf_op | source)
XLA Modules:
  0.0 171.8 jit_solution(8138980188552081311)
XLA Ops:
  0.0 2.0 %broadcast_in_dim.24 = bf16[8,4,72,256]{3,2,1,0:T(8,128)(2,1)} broadcast(bf16[4,72,256]{2,1,0:T(8,128)(2,1)} %bitcast.50), dimensions={1,2,3} | broadcast | bytes 1327104 | tf_op jit(solution)/shard_map/broadcast_in_dim | solution.py:42
  2.0 13.8 %all-to-all-start = ((bf16[32,72,256]{2,1,0:T(8,128)(2,1)}), bf16[32,72,256]{2,1,0:T(8,128)(2,1)S(1)}, u32[]{:S(2)}, u32[]{:S(2)}) async-start(bf16[32,72,256]{2,1,0:T(8,128)(2,1)} %bitcast.1), calls=%async_computation | async-start | bytes 2359296 | tf_op jit(solution)/shard_map/all_to_all | solution.py:14
  15.9 3.1 %collective-permute-start = (bf16[288,256]{1,0:T(8,128)(2,1)S(1)}, bf16[288,256]{1,0:T(8,128)(2,1)S(1)}, u32[]{:S(2)}, u32[]{:S(2)}) collective-permute-start(bf16[288,256]{1,0:T(8,128)(2,1)S(1)} %copy-done), channel_id=1, source_target_pairs={{0,8},{8,16},{16,24},{24,0},{1,9},{9,17},{17,25},{25,1},{2,10},{10... | collective-permute-start | bytes 442376 | tf_op jit(solution)/shard_map/ppermute | solution.py:47
  19.0 4.3 %collective-permute-start.1 = (bf16[288,256]{1,0:T(8,128)(2,1)S(1)}, bf16[288,256]{1,0:T(8,128)(2,1)S(1)}, u32[]{:S(2)}, u32[]{:S(2)}) collective-permute-start(bf16[288,256]{1,0:T(8,128)(2,1)S(1)} %copy-done), channel_id=1, source_target_pairs={{0,16},{8,24},{16,0},{24,8},{1,17},{9,25},{17,1},{25,9},{2,18},{10... | collective-permute-start | bytes 442376 | tf_op jit(solution)/shard_map/ppermute | solution.py:47
  23.3 3.1 %collective-permute-start.2 = (bf16[288,256]{1,0:T(8,128)(2,1)S(1)}, bf16[288,256]{1,0:T(8,128)(2,1)S(1)}, u32[]{:S(2)}, u32[]{:S(2)}) collective-permute-start(bf16[288,256]{1,0:T(8,128)(2,1)S(1)} %copy-done), channel_id=1, source_target_pairs={{0,24},{8,0},{16,8},{24,16},{1,25},{9,1},{17,9},{25,17},{2,26},{10... | collective-permute-start | bytes 442376 | tf_op jit(solution)/shard_map/ppermute | solution.py:47
  26.5 4.8 %collective-permute-done.1 = bf16[288,256]{1,0:T(8,128)(2,1)S(1)} collective-permute-done((bf16[288,256]{1,0:T(8,128)(2,1)S(1)}, bf16[288,256]{1,0:T(8,128)(2,1)S(1)}, u32[]{:S(2)}, u32[]{:S(2)}) %collective-permute-start.1) | collective-permute-done | bytes 147488 | tf_op jit(solution)/shard_map/ppermute | solution.py:47
  31.3 4.5 %collective-permute-done.2 = bf16[288,256]{1,0:T(8,128)(2,1)S(1)} collective-permute-done((bf16[288,256]{1,0:T(8,128)(2,1)S(1)}, bf16[288,256]{1,0:T(8,128)(2,1)S(1)}, u32[]{:S(2)}, u32[]{:S(2)}) %collective-permute-start.2) | collective-permute-done | bytes 147488 | tf_op jit(solution)/shard_map/ppermute | solution.py:47
  35.7 0.1 select_select_fusion.3
  35.9 2.5 %collective-permute-start.3 = (bf16[288,1024]{1,0:T(8,128)(2,1)S(1)}, bf16[288,1024]{1,0:T(8,128)(2,1)S(1)}, u32[]{:S(2)}, u32[]{:S(2)}) collective-permute-start(bf16[288,1024]{1,0:T(8,128)(2,1)S(1)} %pad_maximum_fusion.1), channel_id=1, source_target_pairs={{0,32},{32,0},{1,33},{33,1},{2,34},{34,2},{3,35},{35,3},{4,36},{36... | collective-permute-start | bytes 1769480 | tf_op jit(solution)/shard_map/ppermute | solution.py:27
  38.4 6.1 %all-to-all-done = bf16[32,72,256]{2,1,0:T(8,128)(2,1)S(1)} async-done(((bf16[32,72,256]{2,1,0:T(8,128)(2,1)}), bf16[32,72,256]{2,1,0:T(8,128)(2,1)S(1)}, u32[]{:S(2)}, u32[]{:S(2)}) %all-to-all-start) | async-done | bytes 1179680 | tf_op jit(solution)/shard_map/all_to_all | solution.py:14
  44.5 0.1 fusion.17
  44.6 1.1 convolution_convert_fusion
  45.7 24.3 %all_to_all.30 = bf16[8,72,576]{2,1,0:T(8,128)(2,1)S(1)} all-to-all(bf16[8,72,576]{2,1,0:T(8,128)(2,1)S(1)} %bitcast.51), channel_id=1, replica_groups=mesh['z'=8,'core'=2,'x'=4,'y'=8] {'y'}, dimensions={0} | all-to-all | bytes 1327104 | tf_op jit(solution)/shard_map/all_to_all | solution.py:14
  70.0 0.1 fusion.14
  70.2 20.6 %all_to_all.31 = bf16[8,72,576]{2,1,0:T(8,128)(2,1)S(1)} all-to-all(bf16[8,72,576]{2,1,0:T(8,128)(2,1)S(1)} %broadcast_in_dim.25), channel_id=1, replica_groups=mesh['z'=8,'core'=2,'x'=4,'y'=8] {'y'}, dimensions={0} | all-to-all | bytes 1327104 | tf_op jit(solution)/shard_map/all_to_all | solution.py:14
  90.8 0.6 convolution_convert_fusion.2
  91.4 7.7 %collective-permute-start.4 = (bf16[288,1024]{1,0:T(8,128)(2,1)S(1)}, bf16[288,1024]{1,0:T(8,128)(2,1)S(1)}, u32[]{:S(2)}, u32[]{:S(2)}) collective-permute-start(bf16[288,1024]{1,0:T(8,128)(2,1)S(1)} %convolution_convert_fusion.2), channel_id=1, source_target_pairs={{0,32},{32,0},{1,33},{33,1},{2,34},{34,2},{3,35},{35,3},{4,36},{36... | collective-permute-start | bytes 1769480 | tf_op jit(solution)/shard_map/ppermute | solution.py:27
  99.2 1.6 collective-permute-done.4
  100.8 1.5 add_convert_fusion
  102.2 6.0 %all-to-all-start.3 = ((bf16[4,72,1024]{2,1,0:T(8,128)(2,1)}), bf16[4,72,1024]{2,1,0:T(8,128)(2,1)S(1)}, u32[]{:S(2)}, u32[]{:S(2)}) async-start(bf16[4,72,1024]{2,1,0:T(8,128)(2,1)} %bitcast.11), calls=%async_computation.3 | async-start | bytes 1179648 | tf_op jit(solution)/shard_map/all_to_all | solution.py:14
  108.2 9.6 %all-to-all-done.3 = bf16[4,72,1024]{2,1,0:T(8,128)(2,1)S(1)} async-done(((bf16[4,72,1024]{2,1,0:T(8,128)(2,1)}), bf16[4,72,1024]{2,1,0:T(8,128)(2,1)S(1)}, u32[]{:S(2)}, u32[]{:S(2)}) %all-to-all-start.3) | async-done | bytes 589856 | tf_op jit(solution)/shard_map/all_to_all | solution.py:14
  117.8 0.1 fusion.13
  117.9 0.1 broadcast_in_dim.26
  118.1 33.0 %all_to_all.32 = bf16[8,72,1024]{2,1,0:T(8,128)(2,1)S(1)} all-to-all(bf16[8,72,1024]{2,1,0:T(8,128)(2,1)S(1)} %broadcast_in_dim.26), channel_id=1, replica_groups=mesh['z'=8,'core'=2,'x'=4,'y'=8] {'z'}, dimensions={0} | all-to-all | bytes 2359296 | tf_op jit(solution)/shard_map/all_to_all | solution.py:14
  151.0 0.6 convolution_convert_fusion.1
  151.7 5.0 %collective-permute-start.5 = (bf16[288,1024]{1,0:T(8,128)(2,1)S(1)}, bf16[288,1024]{1,0:T(8,128)(2,1)S(1)}, u32[]{:S(2)}, u32[]{:S(2)}) collective-permute-start(bf16[288,1024]{1,0:T(8,128)(2,1)S(1)} %convolution_convert_fusion.1), channel_id=1, source_target_pairs={{0,32},{32,0},{1,33},{33,1},{2,34},{34,2},{3,35},{35,3},{4,36},{36... | collective-permute-start | bytes 1769480 | tf_op jit(solution)/shard_map/ppermute | solution.py:27
  156.7 0.1 mul.54
  156.8 0.1 mul.55
  156.9 1.4 collective-permute-done.5
  158.3 0.7 fusion.10
  159.0 12.1 %all_to_all.33 = bf16[4,288,256]{2,1,0:T(8,128)(2,1)S(1)} all-to-all(bf16[4,288,256]{2,1,0:T(8,128)(2,1)S(1)} %bitcast.47), channel_id=1, replica_groups=mesh['z'=8,'core'=2,'x'=4,'y'=8] {'x'}, dimensions={0} | all-to-all | bytes 1179648 | tf_op jit(solution)/shard_map/all_to_all | solution.py:14
  171.1 0.8 fusion.12
  (10 shorter events, 0.3 us)
Async XLA Ops:
  2.0 13.9 %copy-start = (bf16[288,256]{1,0:T(8,128)(2,1)S(1)}, bf16[288,256]{1,0:T(8,128)(2,1)}, u32[]{:S(2)}) copy-start(bf16[288,256]{1,0:T(8,128)(2,1)} %param.1) | copy-start | bytes 442372
  2.0 42.5 %all-to-all-start = ((bf16[32,72,256]{2,1,0:T(8,128)(2,1)}), bf16[32,72,256]{2,1,0:T(8,128)(2,1)S(1)}, u32[]{:S(2)}, u32[]{:S(2)}) async-start(bf16[32,72,256]{2,1,0:T(8,128)(2,1)} %bitcast.1), calls=%async_computation | async-start | bytes 2359296 | tf_op jit(solution)/shard_map/all_to_all | solution.py:14
  15.9 10.6 %collective-permute-start = (bf16[288,256]{1,0:T(8,128)(2,1)S(1)}, bf16[288,256]{1,0:T(8,128)(2,1)S(1)}, u32[]{:S(2)}, u32[]{:S(2)}) collective-permute-start(bf16[288,256]{1,0:T(8,128)(2,1)S(1)} %copy-done), channel_id=1, source_target_pairs={{0,8},{8,16},{16,24},{24,0},{1,9},{9,17},{17,25},{25,1},{2,10},{10... | collective-permute-start | bytes 442376 | tf_op jit(solution)/shard_map/ppermute | solution.py:47
  19.0 12.2 %collective-permute-start.1 = (bf16[288,256]{1,0:T(8,128)(2,1)S(1)}, bf16[288,256]{1,0:T(8,128)(2,1)S(1)}, u32[]{:S(2)}, u32[]{:S(2)}) collective-permute-start(bf16[288,256]{1,0:T(8,128)(2,1)S(1)} %copy-done), channel_id=1, source_target_pairs={{0,16},{8,24},{16,0},{24,8},{1,17},{9,25},{17,1},{25,9},{2,18},{10... | collective-permute-start | bytes 442376 | tf_op jit(solution)/shard_map/ppermute | solution.py:47
  23.3 12.4 %collective-permute-start.2 = (bf16[288,256]{1,0:T(8,128)(2,1)S(1)}, bf16[288,256]{1,0:T(8,128)(2,1)S(1)}, u32[]{:S(2)}, u32[]{:S(2)}) collective-permute-start(bf16[288,256]{1,0:T(8,128)(2,1)S(1)} %copy-done), channel_id=1, source_target_pairs={{0,24},{8,0},{16,8},{24,16},{1,25},{9,1},{17,9},{25,17},{2,26},{10... | collective-permute-start | bytes 442376 | tf_op jit(solution)/shard_map/ppermute | solution.py:47
  35.9 8.7 %collective-permute-start.3 = (bf16[288,1024]{1,0:T(8,128)(2,1)S(1)}, bf16[288,1024]{1,0:T(8,128)(2,1)S(1)}, u32[]{:S(2)}, u32[]{:S(2)}) collective-permute-start(bf16[288,1024]{1,0:T(8,128)(2,1)S(1)} %pad_maximum_fusion.1), channel_id=1, source_target_pairs={{0,32},{32,0},{1,33},{33,1},{2,34},{34,2},{3,35},{35,3},{4,36},{36... | collective-permute-start | bytes 1769480 | tf_op jit(solution)/shard_map/ppermute | solution.py:27
  91.4 9.3 %collective-permute-start.4 = (bf16[288,1024]{1,0:T(8,128)(2,1)S(1)}, bf16[288,1024]{1,0:T(8,128)(2,1)S(1)}, u32[]{:S(2)}, u32[]{:S(2)}) collective-permute-start(bf16[288,1024]{1,0:T(8,128)(2,1)S(1)} %convolution_convert_fusion.2), channel_id=1, source_target_pairs={{0,32},{32,0},{1,33},{33,1},{2,34},{34,2},{3,35},{35,3},{4,36},{36... | collective-permute-start | bytes 1769480 | tf_op jit(solution)/shard_map/ppermute | solution.py:27
  102.2 15.6 %all-to-all-start.3 = ((bf16[4,72,1024]{2,1,0:T(8,128)(2,1)}), bf16[4,72,1024]{2,1,0:T(8,128)(2,1)S(1)}, u32[]{:S(2)}, u32[]{:S(2)}) async-start(bf16[4,72,1024]{2,1,0:T(8,128)(2,1)} %bitcast.11), calls=%async_computation.3 | async-start | bytes 1179648 | tf_op jit(solution)/shard_map/all_to_all | solution.py:14
  151.7 6.6 %collective-permute-start.5 = (bf16[288,1024]{1,0:T(8,128)(2,1)S(1)}, bf16[288,1024]{1,0:T(8,128)(2,1)S(1)}, u32[]{:S(2)}, u32[]{:S(2)}) collective-permute-start(bf16[288,1024]{1,0:T(8,128)(2,1)S(1)} %convolution_convert_fusion.1), channel_id=1, source_target_pairs={{0,32},{32,0},{1,33},{33,1},{2,34},{34,2},{3,35},{35,3},{4,36},{36... | collective-permute-start | bytes 1769480 | tf_op jit(solution)/shard_map/ppermute | solution.py:27

commit v4 on v3

v4 whole, which is shorter than its diff:
```python
import math

import jax
import jax.numpy as jnp
from jax import lax
from jax.sharding import Mesh, PartitionSpec as P

COLS = 8192
SHIFT = 2.0
F32, BF16 = jnp.float32, jnp.bfloat16


def exchange(chunks, axis):
    return lax.all_to_all(chunks, axis, 0, 0)


def gather(block, axis):
    return exchange(jnp.broadcast_to(block, (lax.axis_size(axis), *block.shape)), axis)


def reduce_scatter(chunks, axis):
    parts = exchange(chunks, axis)
    return sum(parts[i].astype(F32) for i in range(parts.shape[0]))


def swap_cores(block):
    return lax.ppermute(block, "core", [(0, 1), (1, 0)])


def by_column(blocks):
    n, nx, rows, cols = blocks.shape
    return blocks.swapaxes(0, 1).reshape(nx, n * rows, cols)


def on_device(own):
    rows, cols = own.shape
    nx, ny, nz = (lax.axis_size(a) for a in "xyz")
    quarter = rows // nx
    depth = nz * quarter
    here = lax.axis_index("x")

    split = own.reshape(1, nx, quarter, cols)
    spread = jnp.broadcast_to(split, (nz, nx, quarter, cols)).reshape(nz * nx, quarter, cols)
    panel = by_column(exchange(spread, ("z", "x")).reshape(nz, nx, quarter, cols))
    blocks = [own]
    for hop in range(1, nx):
        blocks.append(lax.ppermute(own, "x", [(i, (i + hop) % nx) for i in range(nx)]))
    order = [lax.rem(here + (nx - x), nx) for x in range(nx)]
    wide = jnp.stack([lax.select_n(hop, *blocks) for hop in order])
    share = lax.dynamic_slice_in_dim(wide, here * quarter, quarter, 1)

    left = jnp.concatenate([wide, swap_cores(wide)], 1)
    partial = jnp.einsum("xrc,xjc->rj", left, panel, preferred_element_type=F32)
    partial = partial.astype(BF16).reshape(ny, 2 * rows // ny, depth)
    partial, share = lax.optimization_barrier((partial, share))
    gram = gather(reduce_scatter(partial, "y").astype(BF16), "y").reshape(2 * rows, depth)

    def times(left, right):
        return jnp.einsum("rj,xjc->xrc", left, right, preferred_element_type=F32)

    def applied(right):
        peer = swap_cores(times(gram[rows:], right).astype(BF16))
        return lax.optimization_barrier(times(gram[:rows], right)) + peer.astype(F32)

    first = applied(panel).astype(BF16).reshape(nx, nx, quarter, cols).swapaxes(0, 1)
    first = reduce_scatter(first, "x")
    inner = (-4.775 * share.astype(F32) + 2.0315 * first).astype(BF16)
    right = by_column(gather(inner, "z"))
    mask = jnp.where(jnp.arange(nx) == here, SHIFT, 0.0)[:, None, None]
    known = (mask * share[:, None].astype(F32)).reshape(nx, rows, cols)
    second = reduce_scatter((applied(right) + known).astype(BF16), "x")
    scale = math.sqrt(COLS)
    return (scale * ((3.4445 - SHIFT) * own.astype(F32) + second)).astype(BF16)


def solution(mesh):
    fine = Mesh(mesh.devices.reshape(8, 2, 4, 8), ("z", "core", "x", "y"))
    placed = P(("z", "core"), ("x", "y"))
    return jax.shard_map(
        on_device, mesh=fine, in_specs=placed, out_specs=placed, check_vma=False
    )
```

time: 172 us -> 170 us (0.988)
  blocking collectives: 89.9 us -> 105 us
  waiting for transfers between devices: 28 us -> 16.6 us
  starting transfers between devices: 45.5 us -> 40.3 us
    all_to_all x4 -> x5, blocking collectives: 89.9 us -> 105 us  [exchange(): return lax.all_to_all(chunks, axis, 0, 0)]
    all_to_all x2 -> x1, waiting for transfers between devices: 15.7 us -> 7.16 us  [exchange(): return lax.all_to_all(chunks, axis, 0, 0)]
    all_to_all x2 -> x1, starting transfers between devices: 19.8 us -> 13.8 us  [exchange(): return lax.all_to_all(chunks, axis, 0, 0)]
  transfers between devices with their start and end apart: 8 -> 7, of which waited for: 6 -> 4; matrix products, arithmetic and copies ran while one was open for 0% -> 1% of each run, Pallas kernels for 0% -> 0%
where the time goes in v4:
time: 170 us
  blocking collectives  105 us (62%)
  starting transfers between devices  40.3 us (24%)
  waiting for transfers between devices  16.6 us (10%)
  matrix products  3.61 us (2%)
  local copies, waits for them, and re-layouts  2.58 us (2%)
    all_to_all x5, blocking collectives, exchange(): return lax.all_to_all(chunks, axis, 0, 0)  105 us
    ppermute x3, starting transfers between devices, swap_cores(): return lax.ppermute(block, 'core', [(0, 1), (1, 0)])  16.5 us
    all_to_all x1, starting transfers between devices, exchange(): return lax.all_to_all(chunks, axis, 0, 0)  13.8 us
    ppermute x3, starting transfers between devices, on_device(): lax.ppermute(own, 'x', [(i, (i + hop) % nx) for i in range(nx)])  9.93 us
    ppermute x3, waiting for transfers between devices, on_device(): lax.ppermute(own, 'x', [(i, (i + hop) % nx) for i in range(nx)])  7.71 us
    all_to_all x1, waiting for transfers between devices, exchange(): return lax.all_to_all(chunks, axis, 0, 0)  7.16 us
  transfers between devices with their start and end apart: 7, of which 4 were waited for; matrix products, arithmetic and copies ran while one was open for 1% of the time, Pallas kernels for 0%

profile of v4, /device:TPU:1, one launch (start us, length us, event | category | flops | bytes accessed | tf_op | source)
XLA Modules:
  0.0 169.7 jit_solution(3911394844035104251)
XLA Ops:
  0.0 2.0 %broadcast_in_dim.23 = bf16[8,4,72,256]{3,2,1,0:T(8,128)(2,1)} broadcast(bf16[4,72,256]{2,1,0:T(8,128)(2,1)} %bitcast.75), dimensions={1,2,3} | broadcast | bytes 1327104 | tf_op jit(solution)/shard_map/broadcast_in_dim | solution.py:43
  2.0 13.8 %all-to-all-start = ((bf16[32,72,256]{2,1,0:T(8,128)(2,1)}), bf16[32,72,256]{2,1,0:T(8,128)(2,1)S(1)}, u32[]{:S(2)}, u32[]{:S(2)}) async-start(bf16[32,72,256]{2,1,0:T(8,128)(2,1)} %bitcast.5), calls=%async_computation | async-start | bytes 2359296 | tf_op jit(solution)/shard_map/all_to_all | solution.py:14
  15.9 4.6 %collective-permute-start.1 = (bf16[288,256]{1,0:T(8,128)(2,1)S(1)}, bf16[288,256]{1,0:T(8,128)(2,1)S(1)}, u32[]{:S(2)}, u32[]{:S(2)}) collective-permute-start(bf16[288,256]{1,0:T(8,128)(2,1)S(1)} %copy-done), channel_id=1, source_target_pairs={{0,16},{8,24},{16,0},{24,8},{1,17},{9,25},{17,1},{25,9},{2,18},{10... | collective-permute-start | bytes 442376 | tf_op jit(solution)/shard_map/ppermute | solution.py:47
  20.5 2.8 %collective-permute-start.2 = (bf16[288,256]{1,0:T(8,128)(2,1)S(1)}, bf16[288,256]{1,0:T(8,128)(2,1)S(1)}, u32[]{:S(2)}, u32[]{:S(2)}) collective-permute-start(bf16[288,256]{1,0:T(8,128)(2,1)S(1)} %copy-done), channel_id=1, source_target_pairs={{0,24},{8,0},{16,8},{24,16},{1,25},{9,1},{17,9},{25,17},{2,26},{10... | collective-permute-start | bytes 442376 | tf_op jit(solution)/shard_map/ppermute | solution.py:47
  23.3 2.5 %collective-permute-start = (bf16[288,256]{1,0:T(8,128)(2,1)S(1)}, bf16[288,256]{1,0:T(8,128)(2,1)S(1)}, u32[]{:S(2)}, u32[]{:S(2)}) collective-permute-start(bf16[288,256]{1,0:T(8,128)(2,1)S(1)} %copy-done), channel_id=1, source_target_pairs={{0,8},{8,16},{16,24},{24,0},{1,9},{9,17},{17,25},{25,1},{2,10},{10... | collective-permute-start | bytes 442376 | tf_op jit(solution)/shard_map/ppermute | solution.py:47
  25.9 7.7 %collective-permute-done.2 = bf16[288,256]{1,0:T(8,128)(2,1)S(1)} collective-permute-done((bf16[288,256]{1,0:T(8,128)(2,1)S(1)}, bf16[288,256]{1,0:T(8,128)(2,1)S(1)}, u32[]{:S(2)}, u32[]{:S(2)}) %collective-permute-start.2) | collective-permute-done | bytes 147488 | tf_op jit(solution)/shard_map/ppermute | solution.py:47
  33.7 0.1 pad_maximum_fusion
  33.7 3.6 %collective-permute-start.3 = (bf16[4,288,256]{2,1,0:T(8,128)(2,1)S(1)}, bf16[4,288,256]{2,1,0:T(8,128)(2,1)S(1)}, u32[]{:S(2)}, u32[]{:S(2)}) collective-permute-start(bf16[4,288,256]{2,1,0:T(8,128)(2,1)S(1)} %pad_maximum_fusion), channel_id=1, source_target_pairs={{0,32},{32,0},{1,33},{33,1},{2,34},{34,2},{3,35},{35,3},{4,36},{36... | collective-permute-start | bytes 1769480 | tf_op jit(solution)/shard_map/ppermute | solution.py:27
  37.3 7.2 %all-to-all-done = bf16[32,72,256]{2,1,0:T(8,128)(2,1)S(1)} async-done(((bf16[32,72,256]{2,1,0:T(8,128)(2,1)}), bf16[32,72,256]{2,1,0:T(8,128)(2,1)S(1)}, u32[]{:S(2)}, u32[]{:S(2)}) %all-to-all-start) | async-done | bytes 1179680 | tf_op jit(solution)/shard_map/all_to_all | solution.py:14
  44.5 0.1 copy.4
  44.6 1.1 bitcast_convert_fusion
  45.7 24.3 %all_to_all.30 = bf16[8,72,576]{2,1,0:T(8,128)(2,1)S(1)} all-to-all(bf16[8,72,576]{2,1,0:T(8,128)(2,1)S(1)} %bitcast.76), channel_id=1, replica_groups=mesh['z'=8,'core'=2,'x'=4,'y'=8] {'y'}, dimensions={0} | all-to-all | bytes 1327104 | tf_op jit(solution)/shard_map/all_to_all | solution.py:14
  70.0 0.1 fusion.16
  70.2 20.6 %all_to_all.31 = bf16[8,72,576]{2,1,0:T(8,128)(2,1)S(1)} all-to-all(bf16[8,72,576]{2,1,0:T(8,128)(2,1)S(1)} %broadcast_in_dim.24), channel_id=1, replica_groups=mesh['z'=8,'core'=2,'x'=4,'y'=8] {'y'}, dimensions={0} | all-to-all | bytes 1327104 | tf_op jit(solution)/shard_map/all_to_all | solution.py:14
  90.8 0.6 fusion
  91.4 7.7 %collective-permute-start.4 = (bf16[4,288,256]{2,1,0:T(8,128)(2,1)S(1)}, bf16[4,288,256]{2,1,0:T(8,128)(2,1)S(1)}, u32[]{:S(2)}, u32[]{:S(2)}) collective-permute-start(bf16[4,288,256]{2,1,0:T(8,128)(2,1)S(1)} %fusion), channel_id=1, source_target_pairs={{0,32},{32,0},{1,33},{33,1},{2,34},{34,2},{3,35},{35,3},{4,36},{36... | collective-permute-start | bytes 1769480 | tf_op jit(solution)/shard_map/ppermute | solution.py:27
  99.2 0.6 convolution_bitcast_fusion.1
  99.8 1.0 collective-permute-done.4
  100.8 0.1 add_convert_fusion
  101.0 15.4 %all_to_all.32 = bf16[4,4,72,256]{3,2,1,0:T(8,128)(2,1)S(1)} all-to-all(bf16[4,4,72,256]{3,2,1,0:T(8,128)(2,1)S(1)} %bitcast.73), channel_id=1, replica_groups=mesh['z'=8,'core'=2,'x'=4,'y'=8] {'x'}, dimensions={0} | all-to-all | bytes 1179648 | tf_op jit(solution)/shard_map/all_to_all | solution.py:14
  116.3 0.1 fusion.15
  116.5 0.1 broadcast_in_dim.25
  116.5 32.5 %all_to_all.33 = bf16[8,4,72,256]{3,2,1,0:T(8,128)(2,1)S(1)} all-to-all(bf16[8,4,72,256]{3,2,1,0:T(8,128)(2,1)S(1)} %broadcast_in_dim.25), channel_id=1, replica_groups=mesh['z'=8,'core'=2,'x'=4,'y'=8] {'z'}, dimensions={0} | all-to-all | bytes 2359296 | tf_op jit(solution)/shard_map/all_to_all | solution.py:14
  149.0 0.1 copy.6
  149.1 0.6 fusion.1
  149.7 5.2 %collective-permute-start.5 = (bf16[4,288,256]{2,1,0:T(8,128)(2,1)S(1)}, bf16[4,288,256]{2,1,0:T(8,128)(2,1)S(1)}, u32[]{:S(2)}, u32[]{:S(2)}) collective-permute-start(bf16[4,288,256]{2,1,0:T(8,128)(2,1)S(1)} %fusion.1), channel_id=1, source_target_pairs={{0,32},{32,0},{1,33},{33,1},{2,34},{34,2},{3,35},{35,3},{4,36},{36... | collective-permute-start | bytes 1769480 | tf_op jit(solution)/shard_map/ppermute | solution.py:27
  155.1 0.1 mul.55
  155.2 0.6 convolution_bitcast_fusion
  155.8 0.8 collective-permute-done.5
  156.6 0.3 fusion.12
  156.9 12.0 %all_to_all.34 = bf16[4,288,256]{2,1,0:T(8,128)(2,1)S(1)} all-to-all(bf16[4,288,256]{2,1,0:T(8,128)(2,1)S(1)} %fusion.12), channel_id=1, replica_groups=mesh['z'=8,'core'=2,'x'=4,'y'=8] {'x'}, dimensions={0} | all-to-all | bytes 1179648 | tf_op jit(solution)/shard_map/all_to_all | solution.py:14
  168.9 0.8 fusion.14
  (13 shorter events, 0.4 us)
Async XLA Ops:
  2.0 13.9 %copy-start = (bf16[288,256]{1,0:T(8,128)(2,1)S(1)}, bf16[288,256]{1,0:T(8,128)(2,1)}, u32[]{:S(2)}) copy-start(bf16[288,256]{1,0:T(8,128)(2,1)} %param.1) | copy-start | bytes 442372
  2.0 42.5 %all-to-all-start = ((bf16[32,72,256]{2,1,0:T(8,128)(2,1)}), bf16[32,72,256]{2,1,0:T(8,128)(2,1)S(1)}, u32[]{:S(2)}, u32[]{:S(2)}) async-start(bf16[32,72,256]{2,1,0:T(8,128)(2,1)} %bitcast.5), calls=%async_computation | async-start | bytes 2359296 | tf_op jit(solution)/shard_map/all_to_all | solution.py:14
  15.9 10.0 %collective-permute-start.1 = (bf16[288,256]{1,0:T(8,128)(2,1)S(1)}, bf16[288,256]{1,0:T(8,128)(2,1)S(1)}, u32[]{:S(2)}, u32[]{:S(2)}) collective-permute-start(bf16[288,256]{1,0:T(8,128)(2,1)S(1)} %copy-done), channel_id=1, source_target_pairs={{0,16},{8,24},{16,0},{24,8},{1,17},{9,25},{17,1},{25,9},{2,18},{10... | collective-permute-start | bytes 442376 | tf_op jit(solution)/shard_map/ppermute | solution.py:47
  20.5 13.0 %collective-permute-start.2 = (bf16[288,256]{1,0:T(8,128)(2,1)S(1)}, bf16[288,256]{1,0:T(8,128)(2,1)S(1)}, u32[]{:S(2)}, u32[]{:S(2)}) collective-permute-start(bf16[288,256]{1,0:T(8,128)(2,1)S(1)} %copy-done), channel_id=1, source_target_pairs={{0,24},{8,0},{16,8},{24,16},{1,25},{9,1},{17,9},{25,17},{2,26},{10... | collective-permute-start | bytes 442376 | tf_op jit(solution)/shard_map/ppermute | solution.py:47
  23.3 10.2 %collective-permute-start = (bf16[288,256]{1,0:T(8,128)(2,1)S(1)}, bf16[288,256]{1,0:T(8,128)(2,1)S(1)}, u32[]{:S(2)}, u32[]{:S(2)}) collective-permute-start(bf16[288,256]{1,0:T(8,128)(2,1)S(1)} %copy-done), channel_id=1, source_target_pairs={{0,8},{8,16},{16,24},{24,0},{1,9},{9,17},{17,25},{25,1},{2,10},{10... | collective-permute-start | bytes 442376 | tf_op jit(solution)/shard_map/ppermute | solution.py:47
  33.7 10.8 %collective-permute-start.3 = (bf16[4,288,256]{2,1,0:T(8,128)(2,1)S(1)}, bf16[4,288,256]{2,1,0:T(8,128)(2,1)S(1)}, u32[]{:S(2)}, u32[]{:S(2)}) collective-permute-start(bf16[4,288,256]{2,1,0:T(8,128)(2,1)S(1)} %pad_maximum_fusion), channel_id=1, source_target_pairs={{0,32},{32,0},{1,33},{33,1},{2,34},{34,2},{3,35},{35,3},{4,36},{36... | collective-permute-start | bytes 1769480 | tf_op jit(solution)/shard_map/ppermute | solution.py:27
  91.4 9.3 %collective-permute-start.4 = (bf16[4,288,256]{2,1,0:T(8,128)(2,1)S(1)}, bf16[4,288,256]{2,1,0:T(8,128)(2,1)S(1)}, u32[]{:S(2)}, u32[]{:S(2)}) collective-permute-start(bf16[4,288,256]{2,1,0:T(8,128)(2,1)S(1)} %fusion), channel_id=1, source_target_pairs={{0,32},{32,0},{1,33},{33,1},{2,34},{34,2},{3,35},{35,3},{4,36},{36... | collective-permute-start | bytes 1769480 | tf_op jit(solution)/shard_map/ppermute | solution.py:27
  149.7 6.9 %collective-permute-start.5 = (bf16[4,288,256]{2,1,0:T(8,128)(2,1)S(1)}, bf16[4,288,256]{2,1,0:T(8,128)(2,1)S(1)}, u32[]{:S(2)}, u32[]{:S(2)}) collective-permute-start(bf16[4,288,256]{2,1,0:T(8,128)(2,1)S(1)} %fusion.1), channel_id=1, source_target_pairs={{0,32},{32,0},{1,33},{33,1},{2,34},{34,2},{3,35},{35,3},{4,36},{36... | collective-permute-start | bytes 1769480 | tf_op jit(solution)/shard_map/ppermute | solution.py:27

commit v5 on v4

v5 whole, which is shorter than its diff:
```python
import math

import jax
import jax.numpy as jnp
from jax import lax
from jax.sharding import Mesh, PartitionSpec as P

COLS = 8192
F32, BF16 = jnp.float32, jnp.bfloat16


def exchange(chunks, axis):
    return lax.all_to_all(chunks, axis, 0, 0)


def gather(block, axis):
    return exchange(jnp.broadcast_to(block, (lax.axis_size(axis), *block.shape)), axis)


def reduce_scatter(chunks, axis):
    parts = exchange(chunks, axis)
    return sum(parts[i].astype(F32) for i in range(parts.shape[0]))


def swap_cores(block):
    return lax.ppermute(block, "core", [(0, 1), (1, 0)])


def by_column(blocks):
    n, nx, rows, cols = blocks.shape
    return blocks.swapaxes(0, 1).reshape(nx, n * rows, cols)


def on_device(own):
    rows, cols = own.shape
    nx, ny, nz = (lax.axis_size(a) for a in "xyz")
    quarter = rows // nx
    depth = nz * quarter
    here = lax.axis_index("x")

    def shift_x(block, hop):
        return lax.ppermute(block, "x", [(i, (i + hop) % nx) for i in range(nx)])

    chunks = jnp.broadcast_to(own.reshape(nx, quarter, cols), (nz, nx, quarter, cols))
    chunks = exchange(chunks.reshape(nz * nx, quarter, cols), ("z", "x"))
    panel = by_column(chunks.reshape(nz, nx, quarter, cols))
    blocks = [own] + [shift_x(own, hop) for hop in range(1, nx)]
    order = [lax.rem(here + (nx - x), nx) for x in range(nx)]
    wide = jnp.stack([lax.select_n(hop, *blocks) for hop in order])

    left = jnp.concatenate([wide, swap_cores(wide)], 1)
    partial = jnp.einsum("xrc,xjc->rj", left, panel, preferred_element_type=F32)
    partial = partial.astype(BF16).reshape(ny, 2 * rows // ny, depth)
    gram = gather(reduce_scatter(partial, "y").astype(BF16), "y").reshape(2 * rows, depth)

    def times(left, right):
        return jnp.einsum("rj,xjc->xrc", left, right, preferred_element_type=F32)

    def applied(right):
        peer = swap_cores(times(gram[rows:], right).astype(BF16))
        return lax.optimization_barrier(times(gram[:rows], right)) + peer.astype(F32)

    first = reduce_scatter(applied(panel).astype(BF16), "x")
    inner = (-4.775 * own.astype(F32) + 2.0315 * first).astype(BF16).reshape(nx, quarter, cols)
    inner, gram = lax.optimization_barrier((inner, gram))
    right = by_column(gather(inner, "z"))
    top, bottom = gram[:rows], gram[rows:]
    above_top, below_bottom = shift_x(top, -1), shift_x(bottom, 1)
    above_bottom, below_top = shift_x(bottom, -1), shift_x(top, 1)
    far_top, far_bottom = shift_x(above_top, -1), shift_x(below_bottom, 1)
    tops = jnp.stack([lax.select_n(hop, top, below_top, far_top, above_top) for hop in order])
    bottoms = jnp.stack([lax.select_n(hop, bottom, below_bottom, far_bottom, above_bottom) for hop in order])

    def with_all(left):
        return jnp.einsum("xrj,xjc->rc", left, right, preferred_element_type=F32)

    other = swap_cores(with_all(bottoms))
    second = lax.optimization_barrier(with_all(tops)) + other
    scale = math.sqrt(COLS)
    return (scale * (3.4445 * own.astype(F32) + second)).astype(BF16)


def solution(mesh):
    fine = Mesh(mesh.devices.reshape(8, 2, 4, 8), ("z", "core", "x", "y"))
    placed = P(("z", "core"), ("x", "y"))
    return jax.shard_map(
        on_device, mesh=fine, in_specs=placed, out_specs=placed, check_vma=False
    )
```

time: 170 us -> 162 us (0.953)
  blocking collectives: 105 us -> 60.3 us
  starting transfers between devices: 40.3 us -> 59.4 us
  waiting for transfers between devices: 16.6 us -> 29.9 us
  local copies, waits for them, and re-layouts: 2.58 us -> 4.72 us
    all_to_all x5 -> x3, blocking collectives: 105 us -> 60.3 us  [exchange(): return lax.all_to_all(chunks, axis, 0, 0)]
    ppermute x3 -> x9, starting transfers between devices: 9.93 us -> 26.7 us  [shift_x(): return lax.ppermute(block, 'x', [(i, (i + hop) % nx) for i in range(nx)])]
    ppermute x3 -> x9, waiting for transfers between devices: 7.71 us -> 20.6 us  [shift_x(): return lax.ppermute(block, 'x', [(i, (i + hop) % nx) for i in range(nx)])]
    all_to_all x1 -> x2, starting transfers between devices: 13.8 us -> 17.4 us  [exchange(): return lax.all_to_all(chunks, axis, 0, 0)]
    all_to_all x1 -> x2, waiting for transfers between devices: 7.16 us -> 7.8 us  [exchange(): return lax.all_to_all(chunks, axis, 0, 0)]
  transfers between devices with their start and end apart: 7 -> 14, of which waited for: 4 -> 9; matrix products, arithmetic and copies ran while one was open for 1% -> 2% of each run, Pallas kernels for 0% -> 0%
where the time goes in v5:
time: 162 us; the launch traced here: 161 us
  blocking collectives  60.3 us (37%)
  starting transfers between devices  59.4 us (37%)
  waiting for transfers between devices  29.9 us (18%)
  local copies, waits for them, and re-layouts  4.72 us (3%)
  matrix products  3.73 us (2%)
  other arithmetic  2.74 us (2%)
    all_to_all x3, blocking collectives, exchange(): return lax.all_to_all(chunks, axis, 0, 0)  60.3 us
    ppermute x9, starting transfers between devices, shift_x(): return lax.ppermute(block, 'x', [(i, (i + hop) % nx) for i in range(nx)])  26.7 us
    ppermute x9, waiting for transfers between devices, shift_x(): return lax.ppermute(block, 'x', [(i, (i + hop) % nx) for i in range(nx)])  20.6 us
    all_to_all x2, starting transfers between devices, exchange(): return lax.all_to_all(chunks, axis, 0, 0)  17.4 us
    ppermute x3, starting transfers between devices, swap_cores(): return lax.ppermute(block, 'core', [(0, 1), (1, 0)])  15.3 us
    all_to_all x2, waiting for transfers between devices, exchange(): return lax.all_to_all(chunks, axis, 0, 0)  7.8 us
  transfers between devices with their start and end apart: 14, of which 9 were waited for; matrix products, arithmetic and copies ran while one was open for 2% of the time, Pallas kernels for 0%

profile of v5, /device:TPU:1, one launch (start us, length us, event | category | flops | bytes accessed | tf_op | source)
XLA Modules:
  0.0 161.0 jit_solution(1270783791162294895)
XLA Ops:
  0.0 2.0 %broadcast_in_dim.9 = bf16[8,4,72,256]{3,2,1,0:T(8,128)(2,1)} broadcast(bf16[4,72,256]{2,1,0:T(8,128)(2,1)} %bitcast.70), dimensions={1,2,3} | broadcast | bytes 1327104 | tf_op jit(solution)/shard_map/broadcast_in_dim | solution.py:44
  2.0 13.8 %all-to-all-start = ((bf16[32,72,256]{2,1,0:T(8,128)(2,1)}), bf16[32,72,256]{2,1,0:T(8,128)(2,1)S(1)}, u32[]{:S(2)}, u32[]{:S(2)}) async-start(bf16[32,72,256]{2,1,0:T(8,128)(2,1)} %bitcast.5), calls=%async_computation | async-start | bytes 2359296 | tf_op jit(solution)/shard_map/all_to_all | solution.py:13
  15.9 4.6 %collective-permute-start.1 = (bf16[288,256]{1,0:T(8,128)(2,1)S(1)}, bf16[288,256]{1,0:T(8,128)(2,1)S(1)}, u32[]{:S(2)}, u32[]{:S(2)}) collective-permute-start(bf16[288,256]{1,0:T(8,128)(2,1)S(1)} %copy-done), channel_id=1, source_target_pairs={{0,16},{8,24},{16,0},{24,8},{1,17},{9,25},{17,1},{25,9},{2,18},{10... | collective-permute-start | bytes 442376 | tf_op jit(solution)/shard_map/ppermute | solution.py:42
  20.5 2.8 %collective-permute-start.2 = (bf16[288,256]{1,0:T(8,128)(2,1)S(1)}, bf16[288,256]{1,0:T(8,128)(2,1)S(1)}, u32[]{:S(2)}, u32[]{:S(2)}) collective-permute-start(bf16[288,256]{1,0:T(8,128)(2,1)S(1)} %copy-done), channel_id=1, source_target_pairs={{0,24},{8,0},{16,8},{24,16},{1,25},{9,1},{17,9},{25,17},{2,26},{10... | collective-permute-start | bytes 442376 | tf_op jit(solution)/shard_map/ppermute | solution.py:42
  23.3 2.5 %collective-permute-start = (bf16[288,256]{1,0:T(8,128)(2,1)S(1)}, bf16[288,256]{1,0:T(8,128)(2,1)S(1)}, u32[]{:S(2)}, u32[]{:S(2)}) collective-permute-start(bf16[288,256]{1,0:T(8,128)(2,1)S(1)} %copy-done), channel_id=1, source_target_pairs={{0,8},{8,16},{16,24},{24,0},{1,9},{9,17},{17,25},{25,1},{2,10},{10... | collective-permute-start | bytes 442376 | tf_op jit(solution)/shard_map/ppermute | solution.py:42
  25.9 7.7 %collective-permute-done.2 = bf16[288,256]{1,0:T(8,128)(2,1)S(1)} collective-permute-done((bf16[288,256]{1,0:T(8,128)(2,1)S(1)}, bf16[288,256]{1,0:T(8,128)(2,1)S(1)}, u32[]{:S(2)}, u32[]{:S(2)}) %collective-permute-start.2) | collective-permute-done | bytes 147488 | tf_op jit(solution)/shard_map/ppermute | solution.py:42
  33.8 3.6 %collective-permute-start.3 = (bf16[4,288,256]{2,1,0:T(8,128)(2,1)S(1)}, bf16[4,288,256]{2,1,0:T(8,128)(2,1)S(1)}, u32[]{:S(2)}, u32[]{:S(2)}) collective-permute-start(bf16[4,288,256]{2,1,0:T(8,128)(2,1)S(1)} %pad_maximum_fusion), channel_id=1, source_target_pairs={{0,32},{32,0},{1,33},{33,1},{2,34},{34,2},{3,35},{35,3},{4,36},{36... | collective-permute-start | bytes 1769480 | tf_op jit(solution)/shard_map/ppermute | solution.py:26
  37.3 7.2 %all-to-all-done = bf16[32,72,256]{2,1,0:T(8,128)(2,1)S(1)} async-done(((bf16[32,72,256]{2,1,0:T(8,128)(2,1)}), bf16[32,72,256]{2,1,0:T(8,128)(2,1)S(1)}, u32[]{:S(2)}, u32[]{:S(2)}) %all-to-all-start) | async-done | bytes 1179680 | tf_op jit(solution)/shard_map/all_to_all | solution.py:13
  44.6 1.1 bitcast_convert_fusion
  45.7 24.3 %all_to_all.25 = bf16[8,72,576]{2,1,0:T(8,128)(2,1)S(1)} all-to-all(bf16[8,72,576]{2,1,0:T(8,128)(2,1)S(1)} %bitcast.74), channel_id=1, replica_groups=mesh['z'=8,'core'=2,'x'=4,'y'=8] {'y'}, dimensions={0} | all-to-all | bytes 1327104 | tf_op jit(solution)/shard_map/all_to_all | solution.py:13
  70.2 20.6 %all_to_all.26 = bf16[8,72,576]{2,1,0:T(8,128)(2,1)S(1)} all-to-all(bf16[8,72,576]{2,1,0:T(8,128)(2,1)S(1)} %broadcast_in_dim.10), channel_id=1, replica_groups=mesh['z'=8,'core'=2,'x'=4,'y'=8] {'y'}, dimensions={0} | all-to-all | bytes 1327104 | tf_op jit(solution)/shard_map/all_to_all | solution.py:13
  91.5 7.7 %collective-permute-start.4 = (bf16[4,288,256]{2,1,0:T(8,128)(2,1)S(1)}, bf16[4,288,256]{2,1,0:T(8,128)(2,1)S(1)}, u32[]{:S(2)}, u32[]{:S(2)}) collective-permute-start(bf16[4,288,256]{2,1,0:T(8,128)(2,1)S(1)} %fusion.16), channel_id=1, source_target_pairs={{0,32},{32,0},{1,33},{33,1},{2,34},{34,2},{3,35},{35,3},{4,36},{36... | collective-permute-start | bytes 1769480 | tf_op jit(solution)/shard_map/ppermute | solution.py:26
  99.8 1.0 collective-permute-done.4
  100.9 15.4 %all_to_all.27 = bf16[4,288,256]{2,1,0:T(8,128)(2,1)S(1)} all-to-all(bf16[4,288,256]{2,1,0:T(8,128)(2,1)S(1)} %add_convert_fusion), channel_id=1, replica_groups=mesh['z'=8,'core'=2,'x'=4,'y'=8] {'x'}, dimensions={0} | all-to-all | bytes 1179648 | tf_op jit(solution)/shard_map/all_to_all | solution.py:13
  116.4 1.1 broadcast_in_dim.11
  117.5 3.6 %all-to-all-start.4 = ((bf16[8,4,72,256]{3,2,1,0:T(8,128)(2,1)}), bf16[8,4,72,256]{3,2,1,0:T(8,128)(2,1)S(1)}, u32[]{:S(2)}, u32[]{:S(2)}) async-start(bf16[8,4,72,256]{3,2,1,0:T(8,128)(2,1)} %broadcast_in_dim.11), calls=%async_computation.4 | async-start | bytes 2359296 | tf_op jit(solution)/shard_map/all_to_all | solution.py:13
  121.2 2.8 %collective-permute-start.6 = (bf16[288,576]{1,0:T(8,128)(2,1)S(1)}, bf16[288,576]{1,0:T(8,128)(2,1)S(1)}, u32[]{:S(2)}, u32[]{:S(2)}) collective-permute-start(bf16[288,576]{1,0:T(8,128)(2,1)S(1)} %get-tuple-element.18), channel_id=1, source_target_pairs={{0,24},{8,0},{16,8},{24,16},{1,25},{9,1},{17,9},{25,17},{2,26},{10... | collective-permute-start | bytes 995336 | tf_op jit(solution)/shard_map/ppermute | solution.py:42
  124.0 2.5 %collective-permute-start.8 = (bf16[288,576]{1,0:T(8,128)(2,1)S(1)}, bf16[288,576]{1,0:T(8,128)(2,1)S(1)}, u32[]{:S(2)}, u32[]{:S(2)}) collective-permute-start(bf16[288,576]{1,0:T(8,128)(2,1)S(1)} %get-tuple-element.17), channel_id=1, source_target_pairs={{0,8},{8,16},{16,24},{24,0},{1,9},{9,17},{17,25},{25,1},{2,10},{10... | collective-permute-start | bytes 995336 | tf_op jit(solution)/shard_map/ppermute | solution.py:42
  126.5 2.2 %collective-permute-start.5 = (bf16[288,576]{1,0:T(8,128)(2,1)S(1)}, bf16[288,576]{1,0:T(8,128)(2,1)S(1)}, u32[]{:S(2)}, u32[]{:S(2)}) collective-permute-start(bf16[288,576]{1,0:T(8,128)(2,1)S(1)} %get-tuple-element.18), channel_id=1, source_target_pairs={{0,8},{8,16},{16,24},{24,0},{1,9},{9,17},{17,25},{25,1},{2,10},{10... | collective-permute-start | bytes 995336 | tf_op jit(solution)/shard_map/ppermute | solution.py:42
  128.7 2.7 %collective-permute-done.6 = bf16[288,576]{1,0:T(8,128)(2,1)S(1)} collective-permute-done((bf16[288,576]{1,0:T(8,128)(2,1)S(1)}, bf16[288,576]{1,0:T(8,128)(2,1)S(1)}, u32[]{:S(2)}, u32[]{:S(2)}) %collective-permute-start.6) | collective-permute-done | bytes 331808 | tf_op jit(solution)/shard_map/ppermute | solution.py:42
  131.4 4.0 %collective-permute-start.7 = (bf16[288,576]{1,0:T(8,128)(2,1)S(1)}, bf16[288,576]{1,0:T(8,128)(2,1)S(1)}, u32[]{:S(2)}, u32[]{:S(2)}) collective-permute-start(bf16[288,576]{1,0:T(8,128)(2,1)S(1)} %collective-permute-done.6), channel_id=1, source_target_pairs={{0,24},{8,0},{16,8},{24,16},{1,25},{9,1},{17,9},{25,17},{2,26},{10... | collective-permute-start | bytes 995336 | tf_op jit(solution)/shard_map/ppermute | solution.py:42
  135.4 1.9 %collective-permute-start.10 = (bf16[288,576]{1,0:T(8,128)(2,1)S(1)}, bf16[288,576]{1,0:T(8,128)(2,1)S(1)}, u32[]{:S(2)}, u32[]{:S(2)}) collective-permute-start(bf16[288,576]{1,0:T(8,128)(2,1)S(1)} %get-tuple-element.17), channel_id=1, source_target_pairs={{0,24},{8,0},{16,8},{24,16},{1,25},{9,1},{17,9},{25,17},{2,26},{10... | collective-permute-start | bytes 995336 | tf_op jit(solution)/shard_map/ppermute | solution.py:42
  137.4 3.4 %collective-permute-start.9 = (bf16[288,576]{1,0:T(8,128)(2,1)S(1)}, bf16[288,576]{1,0:T(8,128)(2,1)S(1)}, u32[]{:S(2)}, u32[]{:S(2)}) collective-permute-start(bf16[288,576]{1,0:T(8,128)(2,1)S(1)} %collective-permute-done.8), channel_id=1, source_target_pairs={{0,8},{8,16},{16,24},{24,0},{1,9},{9,17},{17,25},{25,1},{2,10},{10... | collective-permute-start | bytes 995336 | tf_op jit(solution)/shard_map/ppermute | solution.py:42
  140.7 2.3 %collective-permute-done.5 = bf16[288,576]{1,0:T(8,128)(2,1)S(1)} collective-permute-done((bf16[288,576]{1,0:T(8,128)(2,1)S(1)}, bf16[288,576]{1,0:T(8,128)(2,1)S(1)}, u32[]{:S(2)}, u32[]{:S(2)}) %collective-permute-start.5) | collective-permute-done | bytes 331808 | tf_op jit(solution)/shard_map/ppermute | solution.py:42
  143.3 5.3 %collective-permute-done.10 = bf16[288,576]{1,0:T(8,128)(2,1)S(1)} collective-permute-done((bf16[288,576]{1,0:T(8,128)(2,1)S(1)}, bf16[288,576]{1,0:T(8,128)(2,1)S(1)}, u32[]{:S(2)}, u32[]{:S(2)}) %collective-permute-start.10) | collective-permute-done | bytes 331808 | tf_op jit(solution)/shard_map/ppermute | solution.py:42
  148.6 2.5 %collective-permute-done.9 = bf16[288,576]{1,0:T(8,128)(2,1)S(1)} collective-permute-done((bf16[288,576]{1,0:T(8,128)(2,1)S(1)}, bf16[288,576]{1,0:T(8,128)(2,1)S(1)}, u32[]{:S(2)}, u32[]{:S(2)}) %collective-permute-start.9) | collective-permute-done | bytes 331808 | tf_op jit(solution)/shard_map/ppermute | solution.py:42
  151.2 1.3 select_bitcast_fusion.3
  153.1 0.9 copy-done.1
  154.4 0.7 fusion.26
  155.1 4.0 %collective-permute-start.11 = (f32[288,256]{1,0:T(8,128)S(1)}, f32[288,256]{1,0:T(8,128)S(1)}, u32[]{:S(2)}, u32[]{:S(2)}) collective-permute-start(f32[288,256]{1,0:T(8,128)S(1)} %fusion.26), channel_id=1, source_target_pairs={{0,32},{32,0},{1,33},{33,1},{2,34},{34,2},{3,35},{35,3},{4,36},{36... | collective-permute-start | bytes 884744 | tf_op jit(solution)/shard_map/ppermute | solution.py:26
  159.1 0.7 fusion.29
  160.3 0.7 fusion.34
  (29 shorter events, 3.8 us)
Async XLA Ops:
  2.0 13.9 %copy-start = (bf16[288,256]{1,0:T(8,128)(2,1)S(1)}, bf16[288,256]{1,0:T(8,128)(2,1)}, u32[]{:S(2)}) copy-start(bf16[288,256]{1,0:T(8,128)(2,1)} %param.1) | copy-start | bytes 442372
  2.0 42.5 %all-to-all-start = ((bf16[32,72,256]{2,1,0:T(8,128)(2,1)}), bf16[32,72,256]{2,1,0:T(8,128)(2,1)S(1)}, u32[]{:S(2)}, u32[]{:S(2)}) async-start(bf16[32,72,256]{2,1,0:T(8,128)(2,1)} %bitcast.5), calls=%async_computation | async-start | bytes 2359296 | tf_op jit(solution)/shard_map/all_to_all | solution.py:13
  15.9 10.0 %collective-permute-start.1 = (bf16[288,256]{1,0:T(8,128)(2,1)S(1)}, bf16[288,256]{1,0:T(8,128)(2,1)S(1)}, u32[]{:S(2)}, u32[]{:S(2)}) collective-permute-start(bf16[288,256]{1,0:T(8,128)(2,1)S(1)} %copy-done), channel_id=1, source_target_pairs={{0,16},{8,24},{16,0},{24,8},{1,17},{9,25},{17,1},{25,9},{2,18},{10... | collective-permute-start | bytes 442376 | tf_op jit(solution)/shard_map/ppermute | solution.py:42
  20.5 13.0 %collective-permute-start.2 = (bf16[288,256]{1,0:T(8,128)(2,1)S(1)}, bf16[288,256]{1,0:T(8,128)(2,1)S(1)}, u32[]{:S(2)}, u32[]{:S(2)}) collective-permute-start(bf16[288,256]{1,0:T(8,128)(2,1)S(1)} %copy-done), channel_id=1, source_target_pairs={{0,24},{8,0},{16,8},{24,16},{1,25},{9,1},{17,9},{25,17},{2,26},{10... | collective-permute-start | bytes 442376 | tf_op jit(solution)/shard_map/ppermute | solution.py:42
  23.3 10.2 %collective-permute-start = (bf16[288,256]{1,0:T(8,128)(2,1)S(1)}, bf16[288,256]{1,0:T(8,128)(2,1)S(1)}, u32[]{:S(2)}, u32[]{:S(2)}) collective-permute-start(bf16[288,256]{1,0:T(8,128)(2,1)S(1)} %copy-done), channel_id=1, source_target_pairs={{0,8},{8,16},{16,24},{24,0},{1,9},{9,17},{17,25},{25,1},{2,10},{10... | collective-permute-start | bytes 442376 | tf_op jit(solution)/shard_map/ppermute | solution.py:42
  33.8 10.8 %collective-permute-start.3 = (bf16[4,288,256]{2,1,0:T(8,128)(2,1)S(1)}, bf16[4,288,256]{2,1,0:T(8,128)(2,1)S(1)}, u32[]{:S(2)}, u32[]{:S(2)}) collective-permute-start(bf16[4,288,256]{2,1,0:T(8,128)(2,1)S(1)} %pad_maximum_fusion), channel_id=1, source_target_pairs={{0,32},{32,0},{1,33},{33,1},{2,34},{34,2},{3,35},{35,3},{4,36},{36... | collective-permute-start | bytes 1769480 | tf_op jit(solution)/shard_map/ppermute | solution.py:26
  91.5 9.3 %collective-permute-start.4 = (bf16[4,288,256]{2,1,0:T(8,128)(2,1)S(1)}, bf16[4,288,256]{2,1,0:T(8,128)(2,1)S(1)}, u32[]{:S(2)}, u32[]{:S(2)}) collective-permute-start(bf16[4,288,256]{2,1,0:T(8,128)(2,1)S(1)} %fusion.16), channel_id=1, source_target_pairs={{0,32},{32,0},{1,33},{33,1},{2,34},{34,2},{3,35},{35,3},{4,36},{36... | collective-permute-start | bytes 1769480 | tf_op jit(solution)/shard_map/ppermute | solution.py:26
  117.5 35.5 %all-to-all-start.4 = ((bf16[8,4,72,256]{3,2,1,0:T(8,128)(2,1)}), bf16[8,4,72,256]{3,2,1,0:T(8,128)(2,1)S(1)}, u32[]{:S(2)}, u32[]{:S(2)}) async-start(bf16[8,4,72,256]{3,2,1,0:T(8,128)(2,1)} %broadcast_in_dim.11), calls=%async_computation.4 | async-start | bytes 2359296 | tf_op jit(solution)/shard_map/all_to_all | solution.py:13
  121.2 10.2 %collective-permute-start.6 = (bf16[288,576]{1,0:T(8,128)(2,1)S(1)}, bf16[288,576]{1,0:T(8,128)(2,1)S(1)}, u32[]{:S(2)}, u32[]{:S(2)}) collective-permute-start(bf16[288,576]{1,0:T(8,128)(2,1)S(1)} %get-tuple-element.18), channel_id=1, source_target_pairs={{0,24},{8,0},{16,8},{24,16},{1,25},{9,1},{17,9},{25,17},{2,26},{10... | collective-permute-start | bytes 995336 | tf_op jit(solution)/shard_map/ppermute | solution.py:42
  124.0 13.4 %collective-permute-start.8 = (bf16[288,576]{1,0:T(8,128)(2,1)S(1)}, bf16[288,576]{1,0:T(8,128)(2,1)S(1)}, u32[]{:S(2)}, u32[]{:S(2)}) collective-permute-start(bf16[288,576]{1,0:T(8,128)(2,1)S(1)} %get-tuple-element.17), channel_id=1, source_target_pairs={{0,8},{8,16},{16,24},{24,0},{1,9},{9,17},{17,25},{25,1},{2,10},{10... | collective-permute-start | bytes 995336 | tf_op jit(solution)/shard_map/ppermute | solution.py:42
  126.5 16.6 %collective-permute-start.5 = (bf16[288,576]{1,0:T(8,128)(2,1)S(1)}, bf16[288,576]{1,0:T(8,128)(2,1)S(1)}, u32[]{:S(2)}, u32[]{:S(2)}) collective-permute-start(bf16[288,576]{1,0:T(8,128)(2,1)S(1)} %get-tuple-element.18), channel_id=1, source_target_pairs={{0,8},{8,16},{16,24},{24,0},{1,9},{9,17},{17,25},{25,1},{2,10},{10... | collective-permute-start | bytes 995336 | tf_op jit(solution)/shard_map/ppermute | solution.py:42
  131.4 11.6 %collective-permute-start.7 = (bf16[288,576]{1,0:T(8,128)(2,1)S(1)}, bf16[288,576]{1,0:T(8,128)(2,1)S(1)}, u32[]{:S(2)}, u32[]{:S(2)}) collective-permute-start(bf16[288,576]{1,0:T(8,128)(2,1)S(1)} %collective-permute-done.6), channel_id=1, source_target_pairs={{0,24},{8,0},{16,8},{24,16},{1,25},{9,1},{17,9},{25,17},{2,26},{10... | collective-permute-start | bytes 995336 | tf_op jit(solution)/shard_map/ppermute | solution.py:42
  135.4 13.2 %collective-permute-start.10 = (bf16[288,576]{1,0:T(8,128)(2,1)S(1)}, bf16[288,576]{1,0:T(8,128)(2,1)S(1)}, u32[]{:S(2)}, u32[]{:S(2)}) collective-permute-start(bf16[288,576]{1,0:T(8,128)(2,1)S(1)} %get-tuple-element.17), channel_id=1, source_target_pairs={{0,24},{8,0},{16,8},{24,16},{1,25},{9,1},{17,9},{25,17},{2,26},{10... | collective-permute-start | bytes 995336 | tf_op jit(solution)/shard_map/ppermute | solution.py:42
  137.4 13.8 %collective-permute-start.9 = (bf16[288,576]{1,0:T(8,128)(2,1)S(1)}, bf16[288,576]{1,0:T(8,128)(2,1)S(1)}, u32[]{:S(2)}, u32[]{:S(2)}) collective-permute-start(bf16[288,576]{1,0:T(8,128)(2,1)S(1)} %collective-permute-done.8), channel_id=1, source_target_pairs={{0,8},{8,16},{16,24},{24,0},{1,9},{9,17},{17,25},{25,1},{2,10},{10... | collective-permute-start | bytes 995336 | tf_op jit(solution)/shard_map/ppermute | solution.py:42
  153.0 1.0 copy-start.1
  153.1 1.1 copy-start.2
  153.1 1.2 copy-start.3
  153.1 1.3 copy-start.4
  155.1 5.2 %collective-permute-start.11 = (f32[288,256]{1,0:T(8,128)S(1)}, f32[288,256]{1,0:T(8,128)S(1)}, u32[]{:S(2)}, u32[]{:S(2)}) collective-permute-start(f32[288,256]{1,0:T(8,128)S(1)} %fusion.26), channel_id=1, source_target_pairs={{0,32},{32,0},{1,33},{33,1},{2,34},{34,2},{3,35},{35,3},{4,36},{36... | collective-permute-start | bytes 884744 | tf_op jit(solution)/shard_map/ppermute | solution.py:26

commit v6 on v5

--- a/solution.py
+++ b/solution.py
@@ -3,6 +3,8 @@
 import jax
 import jax.numpy as jnp
 from jax import lax
+from jax.experimental import pallas as pl
+from jax.experimental.pallas import tpu as pltpu
 from jax.sharding import Mesh, PartitionSpec as P
 
 COLS = 8192
@@ -31,6 +33,31 @@
     return blocks.swapaxes(0, 1).reshape(nx, n * rows, cols)
 
 
+def product_kernel(right, *refs):
+    *blocks, out = refs
+    nx = right.shape[0]
+    here = lax.axis_index("x")
+    out[...] = sum(
+        jnp.dot(block[...], right[lax.rem(here + (nx - hop), nx)], preferred_element_type=F32)
+        for hop, block in enumerate(blocks)
+    )
+
+
+def product(right, *blocks):
+    rows, depth = blocks[0].shape
+    cols = right.shape[2]
+    size = 2 * rows * depth * cols * len(blocks)
+    moved = 2 * right.size + 2 * rows * depth * len(blocks) + 4 * rows * cols
+    return pl.pallas_call(
+        product_kernel,
+        out_shape=jax.ShapeDtypeStruct((rows, cols), F32),
+        in_specs=[pl.BlockSpec(memory_space=pltpu.VMEM)] * (1 + len(blocks)),
+        out_specs=pl.BlockSpec(memory_space=pltpu.VMEM),
+        compiler_params=pltpu.CompilerParams(vmem_limit_bytes=16 << 20),
+        cost_estimate=pl.CostEstimate(flops=size, bytes_accessed=moved, transcendentals=0),
+    )(right, *blocks)
+
+
 def on_device(own):
     rows, cols = own.shape
     nx, ny, nz = (lax.axis_size(a) for a in "xyz")
@@ -45,7 +72,7 @@
     chunks = exchange(chunks.reshape(nz * nx, quarter, cols), ("z", "x"))
     panel = by_column(chunks.reshape(nz, nx, quarter, cols))
     blocks = [own] + [shift_x(own, hop) for hop in range(1, nx)]
-    order = [lax.rem(here + (nx - x), nx) for x in range(nx)]
+    order = [lax.rem(here + (nx - hop), nx) for hop in range(nx)]
     wide = jnp.stack([lax.select_n(hop, *blocks) for hop in order])
 
     left = jnp.concatenate([wide, swap_cores(wide)], 1)
@@ -68,14 +95,8 @@
     above_top, below_bottom = shift_x(top, -1), shift_x(bottom, 1)
     above_bottom, below_top = shift_x(bottom, -1), shift_x(top, 1)
     far_top, far_bottom = shift_x(above_top, -1), shift_x(below_bottom, 1)
-    tops = jnp.stack([lax.select_n(hop, top, below_top, far_top, above_top) for hop in order])
-    bottoms = jnp.stack([lax.select_n(hop, bottom, below_bottom, far_bottom, above_bottom) for hop in order])
-
-    def with_all(left):
-        return jnp.einsum("xrj,xjc->rc", left, right, preferred_element_type=F32)
-
-    other = swap_cores(with_all(bottoms))
-    second = lax.optimization_barrier(with_all(tops)) + other
+    other = swap_cores(product(right, bottom, below_bottom, far_bottom, above_bottom))
+    second = product(right, top, below_top, far_top, above_top) + other
     scale = math.sqrt(COLS)
     return (scale * (3.4445 * own.astype(F32) + second)).astype(BF16)
 

time: 162 us -> 161 us (level)
    ppermute x9, waiting for transfers between devices: 20.6 us -> 12.6 us  [shift_x(): return lax.ppermute(block, 'x', [(i, (i + hop) % nx) for i in range(nx)])]
    all_to_all x2, waiting for transfers between devices: 7.8 us -> 15.7 us  [exchange(): return lax.all_to_all(chunks, axis, 0, 0)]
  transfers between devices with their start and end apart: 14 -> 14, of which waited for: 9 -> 7; matrix products, arithmetic and copies ran while one was open for 2% -> 1% of each run, Pallas kernels for 0% -> 1%
where the time goes in v6:
time: 161 us; the launch traced here: 160 us
  starting transfers between devices  60.2 us (37%)
  blocking collectives  60.2 us (37%)
  waiting for transfers between devices  29.8 us (19%)
  local copies, waits for them, and re-layouts  4.73 us (3%)
  matrix products  2.37 us (1%)
    all_to_all x3, blocking collectives, exchange(): return lax.all_to_all(chunks, axis, 0, 0)  60.2 us
    ppermute x9, starting transfers between devices, shift_x(): return lax.ppermute(block, 'x', [(i, (i + hop) % nx) for i in range(nx)])  27.3 us
    all_to_all x2, starting transfers between devices, exchange(): return lax.all_to_all(chunks, axis, 0, 0)  18.1 us
    all_to_all x2, waiting for transfers between devices, exchange(): return lax.all_to_all(chunks, axis, 0, 0)  15.7 us
    ppermute x3, starting transfers between devices, swap_cores(): return lax.ppermute(block, 'core', [(0, 1), (1, 0)])  14.7 us
    ppermute x9, waiting for transfers between devices, shift_x(): return lax.ppermute(block, 'x', [(i, (i + hop) % nx) for i in range(nx)])  12.6 us
  transfers between devices with their start and end apart: 14, of which 7 were waited for; matrix products, arithmetic and copies ran while one was open for 1% of the time, Pallas kernels for 1%

profile of v6, /device:TPU:1, one launch (start us, length us, event | category | flops | bytes accessed | tf_op | source)
XLA Modules:
  0.0 160.1 jit_solution(956522665315397348)
XLA Ops:
  0.0 2.0 %broadcast_in_dim.9 = bf16[8,4,72,256]{3,2,1,0:T(8,128)(2,1)} broadcast(bf16[4,72,256]{2,1,0:T(8,128)(2,1)} %bitcast.47), dimensions={1,2,3} | broadcast | bytes 1327104 | tf_op jit(solution)/shard_map/broadcast_in_dim | solution.py:71
  2.0 13.8 %all-to-all-start = ((bf16[32,72,256]{2,1,0:T(8,128)(2,1)}), bf16[32,72,256]{2,1,0:T(8,128)(2,1)S(1)}, u32[]{:S(2)}, u32[]{:S(2)}) async-start(bf16[32,72,256]{2,1,0:T(8,128)(2,1)} %bitcast.5), calls=%async_computation | async-start | bytes 2359296 | tf_op jit(solution)/shard_map/all_to_all | solution.py:15
  15.9 3.1 %collective-permute-start = (bf16[288,256]{1,0:T(8,128)(2,1)S(1)}, bf16[288,256]{1,0:T(8,128)(2,1)S(1)}, u32[]{:S(2)}, u32[]{:S(2)}) collective-permute-start(bf16[288,256]{1,0:T(8,128)(2,1)S(1)} %copy-done), channel_id=1, source_target_pairs={{0,8},{8,16},{16,24},{24,0},{1,9},{9,17},{17,25},{25,1},{2,10},{10... | collective-permute-start | bytes 442376 | tf_op jit(solution)/shard_map/ppermute | solution.py:69
  19.0 4.3 %collective-permute-start.1 = (bf16[288,256]{1,0:T(8,128)(2,1)S(1)}, bf16[288,256]{1,0:T(8,128)(2,1)S(1)}, u32[]{:S(2)}, u32[]{:S(2)}) collective-permute-start(bf16[288,256]{1,0:T(8,128)(2,1)S(1)} %copy-done), channel_id=1, source_target_pairs={{0,16},{8,24},{16,0},{24,8},{1,17},{9,25},{17,1},{25,9},{2,18},{10... | collective-permute-start | bytes 442376 | tf_op jit(solution)/shard_map/ppermute | solution.py:69
  23.4 3.1 %collective-permute-start.2 = (bf16[288,256]{1,0:T(8,128)(2,1)S(1)}, bf16[288,256]{1,0:T(8,128)(2,1)S(1)}, u32[]{:S(2)}, u32[]{:S(2)}) collective-permute-start(bf16[288,256]{1,0:T(8,128)(2,1)S(1)} %copy-done), channel_id=1, source_target_pairs={{0,24},{8,0},{16,8},{24,16},{1,25},{9,1},{17,9},{25,17},{2,26},{10... | collective-permute-start | bytes 442376 | tf_op jit(solution)/shard_map/ppermute | solution.py:69
  26.5 4.8 %collective-permute-done.1 = bf16[288,256]{1,0:T(8,128)(2,1)S(1)} collective-permute-done((bf16[288,256]{1,0:T(8,128)(2,1)S(1)}, bf16[288,256]{1,0:T(8,128)(2,1)S(1)}, u32[]{:S(2)}, u32[]{:S(2)}) %collective-permute-start.1) | collective-permute-done | bytes 147488 | tf_op jit(solution)/shard_map/ppermute | solution.py:69
  31.3 4.5 %collective-permute-done.2 = bf16[288,256]{1,0:T(8,128)(2,1)S(1)} collective-permute-done((bf16[288,256]{1,0:T(8,128)(2,1)S(1)}, bf16[288,256]{1,0:T(8,128)(2,1)S(1)}, u32[]{:S(2)}, u32[]{:S(2)}) %collective-permute-start.2) | collective-permute-done | bytes 147488 | tf_op jit(solution)/shard_map/ppermute | solution.py:69
  35.9 2.5 %collective-permute-start.3 = (bf16[4,288,256]{2,1,0:T(8,128)(2,1)S(1)}, bf16[4,288,256]{2,1,0:T(8,128)(2,1)S(1)}, u32[]{:S(2)}, u32[]{:S(2)}) collective-permute-start(bf16[4,288,256]{2,1,0:T(8,128)(2,1)S(1)} %pad_maximum_fusion), channel_id=1, source_target_pairs={{0,32},{32,0},{1,33},{33,1},{2,34},{34,2},{3,35},{35,3},{4,36},{36... | collective-permute-start | bytes 1769480 | tf_op jit(solution)/shard_map/ppermute | solution.py:28
  38.4 6.1 %all-to-all-done = bf16[32,72,256]{2,1,0:T(8,128)(2,1)S(1)} async-done(((bf16[32,72,256]{2,1,0:T(8,128)(2,1)}), bf16[32,72,256]{2,1,0:T(8,128)(2,1)S(1)}, u32[]{:S(2)}, u32[]{:S(2)}) %all-to-all-start) | async-done | bytes 1179680 | tf_op jit(solution)/shard_map/all_to_all | solution.py:15
  44.6 1.1 bitcast_convert_fusion
  45.7 24.3 %all_to_all.25 = bf16[8,72,576]{2,1,0:T(8,128)(2,1)S(1)} all-to-all(bf16[8,72,576]{2,1,0:T(8,128)(2,1)S(1)} %bitcast.49), channel_id=1, replica_groups=mesh['z'=8,'core'=2,'x'=4,'y'=8] {'y'}, dimensions={0} | all-to-all | bytes 1327104 | tf_op jit(solution)/shard_map/all_to_all | solution.py:15
  70.2 20.6 %all_to_all.26 = bf16[8,72,576]{2,1,0:T(8,128)(2,1)S(1)} all-to-all(bf16[8,72,576]{2,1,0:T(8,128)(2,1)S(1)} %broadcast_in_dim.10), channel_id=1, replica_groups=mesh['z'=8,'core'=2,'x'=4,'y'=8] {'y'}, dimensions={0} | all-to-all | bytes 1327104 | tf_op jit(solution)/shard_map/all_to_all | solution.py:15
  90.8 0.6 fusion
  91.5 7.7 %collective-permute-start.4 = (bf16[4,288,256]{2,1,0:T(8,128)(2,1)S(1)}, bf16[4,288,256]{2,1,0:T(8,128)(2,1)S(1)}, u32[]{:S(2)}, u32[]{:S(2)}) collective-permute-start(bf16[4,288,256]{2,1,0:T(8,128)(2,1)S(1)} %fusion), channel_id=1, source_target_pairs={{0,32},{32,0},{1,33},{33,1},{2,34},{34,2},{3,35},{35,3},{4,36},{36... | collective-permute-start | bytes 1769480 | tf_op jit(solution)/shard_map/ppermute | solution.py:28
  99.2 0.6 convolution_bitcast_fusion
  99.8 1.0 collective-permute-done.4
  100.9 15.4 %all_to_all.27 = bf16[4,288,256]{2,1,0:T(8,128)(2,1)S(1)} all-to-all(bf16[4,288,256]{2,1,0:T(8,128)(2,1)S(1)} %add_convert_fusion), channel_id=1, replica_groups=mesh['z'=8,'core'=2,'x'=4,'y'=8] {'x'}, dimensions={0} | all-to-all | bytes 1179648 | tf_op jit(solution)/shard_map/all_to_all | solution.py:15
  116.4 1.1 broadcast_in_dim.11
  117.5 4.3 %all-to-all-start.4 = ((bf16[8,4,72,256]{3,2,1,0:T(8,128)(2,1)}), bf16[8,4,72,256]{3,2,1,0:T(8,128)(2,1)}, u32[]{:S(2)}, u32[]{:S(2)}) async-start(bf16[8,4,72,256]{3,2,1,0:T(8,128)(2,1)} %broadcast_in_dim.11), calls=%async_computation.4 | async-start | bytes 2359296 | tf_op jit(solution)/shard_map/all_to_all | solution.py:15
  121.8 2.2 %collective-permute-start.8 = (bf16[288,576]{1,0:T(8,128)(2,1)S(1)}, bf16[288,576]{1,0:T(8,128)(2,1)S(1)}, u32[]{:S(2)}, u32[]{:S(2)}) collective-permute-start(bf16[288,576]{1,0:T(8,128)(2,1)S(1)} %get-tuple-element.9.refs_0_), channel_id=1, source_target_pairs={{0,8},{8,16},{16,24},{24,0},{1,9},{9,17},{17,25},{25,1},{2,10},{10... | collective-permute-start | bytes 995336 | tf_op jit(solution)/shard_map/ppermute | solution.py:69
  124.0 4.3 %collective-permute-start.6 = (bf16[288,576]{1,0:T(8,128)(2,1)S(1)}, bf16[288,576]{1,0:T(8,128)(2,1)S(1)}, u32[]{:S(2)}, u32[]{:S(2)}) collective-permute-start(bf16[288,576]{1,0:T(8,128)(2,1)S(1)} %get-tuple-element.10.refs_0_), channel_id=1, source_target_pairs={{0,24},{8,0},{16,8},{24,16},{1,25},{9,1},{17,9},{25,17},{2,26},{10... | collective-permute-start | bytes 995336 | tf_op jit(solution)/shard_map/ppermute | solution.py:69
  128.3 1.9 %collective-permute-start.10 = (bf16[288,576]{1,0:T(8,128)(2,1)S(1)}, bf16[288,576]{1,0:T(8,128)(2,1)S(1)}, u32[]{:S(2)}, u32[]{:S(2)}) collective-permute-start(bf16[288,576]{1,0:T(8,128)(2,1)S(1)} %get-tuple-element.9.refs_0_), channel_id=1, source_target_pairs={{0,24},{8,0},{16,8},{24,16},{1,25},{9,1},{17,9},{25,17},{2,26},{10... | collective-permute-start | bytes 995336 | tf_op jit(solution)/shard_map/ppermute | solution.py:69
  130.3 3.3 %collective-permute-done.8.refs_1_ = bf16[288,576]{1,0:T(8,128)(2,1)S(1)} collective-permute-done((bf16[288,576]{1,0:T(8,128)(2,1)S(1)}, bf16[288,576]{1,0:T(8,128)(2,1)S(1)}, u32[]{:S(2)}, u32[]{:S(2)}) %collective-permute-start.8) | collective-permute-done | bytes 331808 | tf_op jit(solution)/shard_map/ppermute | solution.py:69
  133.6 1.9 %collective-permute-start.9 = (bf16[288,576]{1,0:T(8,128)(2,1)S(1)}, bf16[288,576]{1,0:T(8,128)(2,1)S(1)}, u32[]{:S(2)}, u32[]{:S(2)}) collective-permute-start(bf16[288,576]{1,0:T(8,128)(2,1)S(1)} %collective-permute-done.8.refs_1_), channel_id=1, source_target_pairs={{0,8},{8,16},{16,24},{24,0},{1,9},{9,17},{17,25},{25,1},{2,10},{10... | collective-permute-start | bytes 995336 | tf_op jit(solution)/shard_map/ppermute | solution.py:69
  135.5 1.9 %collective-permute-start.5 = (bf16[288,576]{1,0:T(8,128)(2,1)S(1)}, bf16[288,576]{1,0:T(8,128)(2,1)S(1)}, u32[]{:S(2)}, u32[]{:S(2)}) collective-permute-start(bf16[288,576]{1,0:T(8,128)(2,1)S(1)} %get-tuple-element.10.refs_0_), channel_id=1, source_target_pairs={{0,8},{8,16},{16,24},{24,0},{1,9},{9,17},{17,25},{25,1},{2,10},{10... | collective-permute-start | bytes 995336 | tf_op jit(solution)/shard_map/ppermute | solution.py:69
  137.5 4.6 %collective-permute-start.7 = (bf16[288,576]{1,0:T(8,128)(2,1)S(1)}, bf16[288,576]{1,0:T(8,128)(2,1)S(1)}, u32[]{:S(2)}, u32[]{:S(2)}) collective-permute-start(bf16[288,576]{1,0:T(8,128)(2,1)S(1)} %collective-permute-done.6.refs_3_), channel_id=1, source_target_pairs={{0,24},{8,0},{16,8},{24,16},{1,25},{9,1},{17,9},{25,17},{2,26},{10... | collective-permute-start | bytes 995336 | tf_op jit(solution)/shard_map/ppermute | solution.py:69
  142.0 9.6 %all-to-all-done.4 = bf16[8,4,72,256]{3,2,1,0:T(8,128)(2,1)} async-done(((bf16[8,4,72,256]{3,2,1,0:T(8,128)(2,1)}), bf16[8,4,72,256]{3,2,1,0:T(8,128)(2,1)}, u32[]{:S(2)}, u32[]{:S(2)}) %all-to-all-start.4) | async-done | bytes 1179680 | tf_op jit(solution)/shard_map/all_to_all | solution.py:15
  151.6 1.3 copy.4
  153.0 0.6 shard_map.18
  153.6 4.6 %collective-permute-start.11 = (f32[288,256]{1,0:T(8,128)S(1)}, f32[288,256]{1,0:T(8,128)S(1)}, u32[]{:S(2)}, u32[]{:S(2)}) collective-permute-start(f32[288,256]{1,0:T(8,128)S(1)} %shard_map.18), channel_id=1, source_target_pairs={{0,32},{32,0},{1,33},{33,1},{2,34},{34,2},{3,35},{35,3},{4,36},{36... | collective-permute-start | bytes 884744 | tf_op jit(solution)/shard_map/ppermute | solution.py:28
  158.2 0.6 shard_map.17
  159.3 0.7 fusion.12
  (19 shorter events, 1.3 us)
Async XLA Ops:
  2.0 13.9 %copy-start = (bf16[288,256]{1,0:T(8,128)(2,1)S(1)}, bf16[288,256]{1,0:T(8,128)(2,1)}, u32[]{:S(2)}) copy-start(bf16[288,256]{1,0:T(8,128)(2,1)} %param.1) | copy-start | bytes 442372
  2.0 42.5 %all-to-all-start = ((bf16[32,72,256]{2,1,0:T(8,128)(2,1)}), bf16[32,72,256]{2,1,0:T(8,128)(2,1)S(1)}, u32[]{:S(2)}, u32[]{:S(2)}) async-start(bf16[32,72,256]{2,1,0:T(8,128)(2,1)} %bitcast.5), calls=%async_computation | async-start | bytes 2359296 | tf_op jit(solution)/shard_map/all_to_all | solution.py:15
  15.9 10.6 %collective-permute-start = (bf16[288,256]{1,0:T(8,128)(2,1)S(1)}, bf16[288,256]{1,0:T(8,128)(2,1)S(1)}, u32[]{:S(2)}, u32[]{:S(2)}) collective-permute-start(bf16[288,256]{1,0:T(8,128)(2,1)S(1)} %copy-done), channel_id=1, source_target_pairs={{0,8},{8,16},{16,24},{24,0},{1,9},{9,17},{17,25},{25,1},{2,10},{10... | collective-permute-start | bytes 442376 | tf_op jit(solution)/shard_map/ppermute | solution.py:69
  19.0 12.2 %collective-permute-start.1 = (bf16[288,256]{1,0:T(8,128)(2,1)S(1)}, bf16[288,256]{1,0:T(8,128)(2,1)S(1)}, u32[]{:S(2)}, u32[]{:S(2)}) collective-permute-start(bf16[288,256]{1,0:T(8,128)(2,1)S(1)} %copy-done), channel_id=1, source_target_pairs={{0,16},{8,24},{16,0},{24,8},{1,17},{9,25},{17,1},{25,9},{2,18},{10... | collective-permute-start | bytes 442376 | tf_op jit(solution)/shard_map/ppermute | solution.py:69
  23.4 12.4 %collective-permute-start.2 = (bf16[288,256]{1,0:T(8,128)(2,1)S(1)}, bf16[288,256]{1,0:T(8,128)(2,1)S(1)}, u32[]{:S(2)}, u32[]{:S(2)}) collective-permute-start(bf16[288,256]{1,0:T(8,128)(2,1)S(1)} %copy-done), channel_id=1, source_target_pairs={{0,24},{8,0},{16,8},{24,16},{1,25},{9,1},{17,9},{25,17},{2,26},{10... | collective-permute-start | bytes 442376 | tf_op jit(solution)/shard_map/ppermute | solution.py:69
  35.9 8.7 %collective-permute-start.3 = (bf16[4,288,256]{2,1,0:T(8,128)(2,1)S(1)}, bf16[4,288,256]{2,1,0:T(8,128)(2,1)S(1)}, u32[]{:S(2)}, u32[]{:S(2)}) collective-permute-start(bf16[4,288,256]{2,1,0:T(8,128)(2,1)S(1)} %pad_maximum_fusion), channel_id=1, source_target_pairs={{0,32},{32,0},{1,33},{33,1},{2,34},{34,2},{3,35},{35,3},{4,36},{36... | collective-permute-start | bytes 1769480 | tf_op jit(solution)/shard_map/ppermute | solution.py:28
  91.5 9.3 %collective-permute-start.4 = (bf16[4,288,256]{2,1,0:T(8,128)(2,1)S(1)}, bf16[4,288,256]{2,1,0:T(8,128)(2,1)S(1)}, u32[]{:S(2)}, u32[]{:S(2)}) collective-permute-start(bf16[4,288,256]{2,1,0:T(8,128)(2,1)S(1)} %fusion), channel_id=1, source_target_pairs={{0,32},{32,0},{1,33},{33,1},{2,34},{34,2},{3,35},{35,3},{4,36},{36... | collective-permute-start | bytes 1769480 | tf_op jit(solution)/shard_map/ppermute | solution.py:28
  117.5 34.1 %all-to-all-start.4 = ((bf16[8,4,72,256]{3,2,1,0:T(8,128)(2,1)}), bf16[8,4,72,256]{3,2,1,0:T(8,128)(2,1)}, u32[]{:S(2)}, u32[]{:S(2)}) async-start(bf16[8,4,72,256]{3,2,1,0:T(8,128)(2,1)} %broadcast_in_dim.11), calls=%async_computation.4 | async-start | bytes 2359296 | tf_op jit(solution)/shard_map/all_to_all | solution.py:15
  121.8 11.8 %collective-permute-start.8 = (bf16[288,576]{1,0:T(8,128)(2,1)S(1)}, bf16[288,576]{1,0:T(8,128)(2,1)S(1)}, u32[]{:S(2)}, u32[]{:S(2)}) collective-permute-start(bf16[288,576]{1,0:T(8,128)(2,1)S(1)} %get-tuple-element.9.refs_0_), channel_id=1, source_target_pairs={{0,8},{8,16},{16,24},{24,0},{1,9},{9,17},{17,25},{25,1},{2,10},{10... | collective-permute-start | bytes 995336 | tf_op jit(solution)/shard_map/ppermute | solution.py:69
  124.0 13.4 %collective-permute-start.6 = (bf16[288,576]{1,0:T(8,128)(2,1)S(1)}, bf16[288,576]{1,0:T(8,128)(2,1)S(1)}, u32[]{:S(2)}, u32[]{:S(2)}) collective-permute-start(bf16[288,576]{1,0:T(8,128)(2,1)S(1)} %get-tuple-element.10.refs_0_), channel_id=1, source_target_pairs={{0,24},{8,0},{16,8},{24,16},{1,25},{9,1},{17,9},{25,17},{2,26},{10... | collective-permute-start | bytes 995336 | tf_op jit(solution)/shard_map/ppermute | solution.py:69
  128.3 24.6 %collective-permute-start.10 = (bf16[288,576]{1,0:T(8,128)(2,1)S(1)}, bf16[288,576]{1,0:T(8,128)(2,1)S(1)}, u32[]{:S(2)}, u32[]{:S(2)}) collective-permute-start(bf16[288,576]{1,0:T(8,128)(2,1)S(1)} %get-tuple-element.9.refs_0_), channel_id=1, source_target_pairs={{0,24},{8,0},{16,8},{24,16},{1,25},{9,1},{17,9},{25,17},{2,26},{10... | collective-permute-start | bytes 995336 | tf_op jit(solution)/shard_map/ppermute | solution.py:69
  133.6 19.4 %collective-permute-start.9 = (bf16[288,576]{1,0:T(8,128)(2,1)S(1)}, bf16[288,576]{1,0:T(8,128)(2,1)S(1)}, u32[]{:S(2)}, u32[]{:S(2)}) collective-permute-start(bf16[288,576]{1,0:T(8,128)(2,1)S(1)} %collective-permute-done.8.refs_1_), channel_id=1, source_target_pairs={{0,8},{8,16},{16,24},{24,0},{1,9},{9,17},{17,25},{25,1},{2,10},{10... | collective-permute-start | bytes 995336 | tf_op jit(solution)/shard_map/ppermute | solution.py:69
  135.5 22.6 %collective-permute-start.5 = (bf16[288,576]{1,0:T(8,128)(2,1)S(1)}, bf16[288,576]{1,0:T(8,128)(2,1)S(1)}, u32[]{:S(2)}, u32[]{:S(2)}) collective-permute-start(bf16[288,576]{1,0:T(8,128)(2,1)S(1)} %get-tuple-element.10.refs_0_), channel_id=1, source_target_pairs={{0,8},{8,16},{16,24},{24,0},{1,9},{9,17},{17,25},{25,1},{2,10},{10... | collective-permute-start | bytes 995336 | tf_op jit(solution)/shard_map/ppermute | solution.py:69
  137.5 20.7 %collective-permute-start.7 = (bf16[288,576]{1,0:T(8,128)(2,1)S(1)}, bf16[288,576]{1,0:T(8,128)(2,1)S(1)}, u32[]{:S(2)}, u32[]{:S(2)}) collective-permute-start(bf16[288,576]{1,0:T(8,128)(2,1)S(1)} %collective-permute-done.6.refs_3_), channel_id=1, source_target_pairs={{0,24},{8,0},{16,8},{24,16},{1,25},{9,1},{17,9},{25,17},{2,26},{10... | collective-permute-start | bytes 995336 | tf_op jit(solution)/shard_map/ppermute | solution.py:69
  153.6 5.8 %collective-permute-start.11 = (f32[288,256]{1,0:T(8,128)S(1)}, f32[288,256]{1,0:T(8,128)S(1)}, u32[]{:S(2)}, u32[]{:S(2)}) collective-permute-start(f32[288,256]{1,0:T(8,128)S(1)} %shard_map.18), channel_id=1, source_target_pairs={{0,32},{32,0},{1,33},{33,1},{2,34},{34,2},{3,35},{35,3},{4,36},{36... | collective-permute-start | bytes 884744 | tf_op jit(solution)/shard_map/ppermute | solution.py:28

commit v7 on v6

--- a/solution.py
+++ b/solution.py
@@ -79,19 +79,19 @@
     partial = jnp.einsum("xrc,xjc->rj", left, panel, preferred_element_type=F32)
     partial = partial.astype(BF16).reshape(ny, 2 * rows // ny, depth)
     gram = gather(reduce_scatter(partial, "y").astype(BF16), "y").reshape(2 * rows, depth)
+    top, bottom = gram[:rows], gram[rows:]
 
     def times(left, right):
         return jnp.einsum("rj,xjc->xrc", left, right, preferred_element_type=F32)
 
     def applied(right):
-        peer = swap_cores(times(gram[rows:], right).astype(BF16))
-        return lax.optimization_barrier(times(gram[:rows], right)) + peer.astype(F32)
+        peer = swap_cores(times(bottom, right).astype(BF16))
+        return lax.optimization_barrier(times(top, right)) + peer.astype(F32)
 
     first = reduce_scatter(applied(panel).astype(BF16), "x")
     inner = (-4.775 * own.astype(F32) + 2.0315 * first).astype(BF16).reshape(nx, quarter, cols)
-    inner, gram = lax.optimization_barrier((inner, gram))
+    inner, top, bottom = lax.optimization_barrier((inner, top, bottom))
     right = by_column(gather(inner, "z"))
-    top, bottom = gram[:rows], gram[rows:]
     above_top, below_bottom = shift_x(top, -1), shift_x(bottom, 1)
     above_bottom, below_top = shift_x(bottom, -1), shift_x(top, 1)
     far_top, far_bottom = shift_x(above_top, -1), shift_x(below_bottom, 1)

time: 161 us -> 161 us (level)
  no operation moved by 1% of the time
where the time goes in v7:
time: 161 us; the launch traced here: 160 us
  starting transfers between devices  60.2 us (37%)
  blocking collectives  60.2 us (37%)
  waiting for transfers between devices  29.9 us (19%)
  local copies, waits for them, and re-layouts  4.69 us (3%)
  matrix products  2.37 us (1%)
    all_to_all x3, blocking collectives, exchange(): return lax.all_to_all(chunks, axis, 0, 0)  60.2 us
    ppermute x9, starting transfers between devices, shift_x(): return lax.ppermute(block, 'x', [(i, (i + hop) % nx) for i in range(nx)])  27.3 us
    all_to_all x2, starting transfers between devices, exchange(): return lax.all_to_all(chunks, axis, 0, 0)  18.1 us
    all_to_all x2, waiting for transfers between devices, exchange(): return lax.all_to_all(chunks, axis, 0, 0)  15.7 us
    ppermute x3, starting transfers between devices, swap_cores(): return lax.ppermute(block, 'core', [(0, 1), (1, 0)])  14.7 us
    ppermute x9, waiting for transfers between devices, shift_x(): return lax.ppermute(block, 'x', [(i, (i + hop) % nx) for i in range(nx)])  12.6 us
  transfers between devices with their start and end apart: 14, of which 7 were waited for; matrix products, arithmetic and copies ran while one was open for 1% of the time, Pallas kernels for 1%

profile of v7, /device:TPU:1, one launch (start us, length us, event | category | flops | bytes accessed | tf_op | source)
XLA Modules:
  0.0 160.1 jit_solution(2066038251309428662)
XLA Ops:
  0.0 2.0 %broadcast_in_dim.9 = bf16[8,4,72,256]{3,2,1,0:T(8,128)(2,1)} broadcast(bf16[4,72,256]{2,1,0:T(8,128)(2,1)} %bitcast.53), dimensions={1,2,3} | broadcast | bytes 1327104 | tf_op jit(solution)/shard_map/broadcast_in_dim | solution.py:71
  2.0 13.8 %all-to-all-start = ((bf16[32,72,256]{2,1,0:T(8,128)(2,1)}), bf16[32,72,256]{2,1,0:T(8,128)(2,1)S(1)}, u32[]{:S(2)}, u32[]{:S(2)}) async-start(bf16[32,72,256]{2,1,0:T(8,128)(2,1)} %bitcast.5), calls=%async_computation | async-start | bytes 2359296 | tf_op jit(solution)/shard_map/all_to_all | solution.py:15
  15.9 3.1 %collective-permute-start = (bf16[288,256]{1,0:T(8,128)(2,1)S(1)}, bf16[288,256]{1,0:T(8,128)(2,1)S(1)}, u32[]{:S(2)}, u32[]{:S(2)}) collective-permute-start(bf16[288,256]{1,0:T(8,128)(2,1)S(1)} %copy-done), channel_id=1, source_target_pairs={{0,8},{8,16},{16,24},{24,0},{1,9},{9,17},{17,25},{25,1},{2,10},{10... | collective-permute-start | bytes 442376 | tf_op jit(solution)/shard_map/ppermute | solution.py:69
  19.1 4.3 %collective-permute-start.1 = (bf16[288,256]{1,0:T(8,128)(2,1)S(1)}, bf16[288,256]{1,0:T(8,128)(2,1)S(1)}, u32[]{:S(2)}, u32[]{:S(2)}) collective-permute-start(bf16[288,256]{1,0:T(8,128)(2,1)S(1)} %copy-done), channel_id=1, source_target_pairs={{0,16},{8,24},{16,0},{24,8},{1,17},{9,25},{17,1},{25,9},{2,18},{10... | collective-permute-start | bytes 442376 | tf_op jit(solution)/shard_map/ppermute | solution.py:69
  23.4 3.1 %collective-permute-start.2 = (bf16[288,256]{1,0:T(8,128)(2,1)S(1)}, bf16[288,256]{1,0:T(8,128)(2,1)S(1)}, u32[]{:S(2)}, u32[]{:S(2)}) collective-permute-start(bf16[288,256]{1,0:T(8,128)(2,1)S(1)} %copy-done), channel_id=1, source_target_pairs={{0,24},{8,0},{16,8},{24,16},{1,25},{9,1},{17,9},{25,17},{2,26},{10... | collective-permute-start | bytes 442376 | tf_op jit(solution)/shard_map/ppermute | solution.py:69
  26.5 4.8 %collective-permute-done.1 = bf16[288,256]{1,0:T(8,128)(2,1)S(1)} collective-permute-done((bf16[288,256]{1,0:T(8,128)(2,1)S(1)}, bf16[288,256]{1,0:T(8,128)(2,1)S(1)}, u32[]{:S(2)}, u32[]{:S(2)}) %collective-permute-start.1) | collective-permute-done | bytes 147488 | tf_op jit(solution)/shard_map/ppermute | solution.py:69
  31.3 4.5 %collective-permute-done.2 = bf16[288,256]{1,0:T(8,128)(2,1)S(1)} collective-permute-done((bf16[288,256]{1,0:T(8,128)(2,1)S(1)}, bf16[288,256]{1,0:T(8,128)(2,1)S(1)}, u32[]{:S(2)}, u32[]{:S(2)}) %collective-permute-start.2) | collective-permute-done | bytes 147488 | tf_op jit(solution)/shard_map/ppermute | solution.py:69
  35.9 2.5 %collective-permute-start.3 = (bf16[4,288,256]{2,1,0:T(8,128)(2,1)S(1)}, bf16[4,288,256]{2,1,0:T(8,128)(2,1)S(1)}, u32[]{:S(2)}, u32[]{:S(2)}) collective-permute-start(bf16[4,288,256]{2,1,0:T(8,128)(2,1)S(1)} %pad_maximum_fusion), channel_id=1, source_target_pairs={{0,32},{32,0},{1,33},{33,1},{2,34},{34,2},{3,35},{35,3},{4,36},{36... | collective-permute-start | bytes 1769480 | tf_op jit(solution)/shard_map/ppermute | solution.py:28
  38.4 6.1 %all-to-all-done = bf16[32,72,256]{2,1,0:T(8,128)(2,1)S(1)} async-done(((bf16[32,72,256]{2,1,0:T(8,128)(2,1)}), bf16[32,72,256]{2,1,0:T(8,128)(2,1)S(1)}, u32[]{:S(2)}, u32[]{:S(2)}) %all-to-all-start) | async-done | bytes 1179680 | tf_op jit(solution)/shard_map/all_to_all | solution.py:15
  44.6 1.1 bitcast_convert_fusion
  45.7 24.3 %all_to_all.25 = bf16[8,72,576]{2,1,0:T(8,128)(2,1)S(1)} all-to-all(bf16[8,72,576]{2,1,0:T(8,128)(2,1)S(1)} %bitcast.54), channel_id=1, replica_groups=mesh['z'=8,'core'=2,'x'=4,'y'=8] {'y'}, dimensions={0} | all-to-all | bytes 1327104 | tf_op jit(solution)/shard_map/all_to_all | solution.py:15
  70.2 20.6 %all_to_all.26 = bf16[8,72,576]{2,1,0:T(8,128)(2,1)S(1)} all-to-all(bf16[8,72,576]{2,1,0:T(8,128)(2,1)S(1)} %broadcast_in_dim.10), channel_id=1, replica_groups=mesh['z'=8,'core'=2,'x'=4,'y'=8] {'y'}, dimensions={0} | all-to-all | bytes 1327104 | tf_op jit(solution)/shard_map/all_to_all | solution.py:15
  90.8 0.6 fusion
  91.5 7.7 %collective-permute-start.4 = (bf16[4,288,256]{2,1,0:T(8,128)(2,1)S(1)}, bf16[4,288,256]{2,1,0:T(8,128)(2,1)S(1)}, u32[]{:S(2)}, u32[]{:S(2)}) collective-permute-start(bf16[4,288,256]{2,1,0:T(8,128)(2,1)S(1)} %fusion), channel_id=1, source_target_pairs={{0,32},{32,0},{1,33},{33,1},{2,34},{34,2},{3,35},{35,3},{4,36},{36... | collective-permute-start | bytes 1769480 | tf_op jit(solution)/shard_map/ppermute | solution.py:28
  99.2 0.6 convolution_bitcast_fusion
  99.8 1.0 collective-permute-done.4
  100.9 15.4 %all_to_all.27 = bf16[4,288,256]{2,1,0:T(8,128)(2,1)S(1)} all-to-all(bf16[4,288,256]{2,1,0:T(8,128)(2,1)S(1)} %add_convert_fusion), channel_id=1, replica_groups=mesh['z'=8,'core'=2,'x'=4,'y'=8] {'x'}, dimensions={0} | all-to-all | bytes 1179648 | tf_op jit(solution)/shard_map/all_to_all | solution.py:15
  116.4 1.1 broadcast_in_dim.11
  117.5 4.3 %all-to-all-start.4 = ((bf16[8,4,72,256]{3,2,1,0:T(8,128)(2,1)}), bf16[8,4,72,256]{3,2,1,0:T(8,128)(2,1)}, u32[]{:S(2)}, u32[]{:S(2)}) async-start(bf16[8,4,72,256]{3,2,1,0:T(8,128)(2,1)} %broadcast_in_dim.11), calls=%async_computation.4 | async-start | bytes 2359296 | tf_op jit(solution)/shard_map/all_to_all | solution.py:15
  121.8 2.2 %collective-permute-start.8 = (bf16[288,576]{1,0:T(8,128)(2,1)S(1)}, bf16[288,576]{1,0:T(8,128)(2,1)S(1)}, u32[]{:S(2)}, u32[]{:S(2)}) collective-permute-start(bf16[288,576]{1,0:T(8,128)(2,1)S(1)} %bitcast.46), channel_id=1, source_target_pairs={{0,8},{8,16},{16,24},{24,0},{1,9},{9,17},{17,25},{25,1},{2,10},{10... | collective-permute-start | bytes 995336 | tf_op jit(solution)/shard_map/ppermute | solution.py:69
  124.0 4.3 %collective-permute-start.6 = (bf16[288,576]{1,0:T(8,128)(2,1)S(1)}, bf16[288,576]{1,0:T(8,128)(2,1)S(1)}, u32[]{:S(2)}, u32[]{:S(2)}) collective-permute-start(bf16[288,576]{1,0:T(8,128)(2,1)S(1)} %bitcast.42), channel_id=1, source_target_pairs={{0,24},{8,0},{16,8},{24,16},{1,25},{9,1},{17,9},{25,17},{2,26},{10... | collective-permute-start | bytes 995336 | tf_op jit(solution)/shard_map/ppermute | solution.py:69
  128.3 1.9 %collective-permute-start.10 = (bf16[288,576]{1,0:T(8,128)(2,1)S(1)}, bf16[288,576]{1,0:T(8,128)(2,1)S(1)}, u32[]{:S(2)}, u32[]{:S(2)}) collective-permute-start(bf16[288,576]{1,0:T(8,128)(2,1)S(1)} %bitcast.47), channel_id=1, source_target_pairs={{0,24},{8,0},{16,8},{24,16},{1,25},{9,1},{17,9},{25,17},{2,26},{10... | collective-permute-start | bytes 995336 | tf_op jit(solution)/shard_map/ppermute | solution.py:69
  130.2 3.3 %collective-permute-done.8.refs_1_ = bf16[288,576]{1,0:T(8,128)(2,1)S(1)} collective-permute-done((bf16[288,576]{1,0:T(8,128)(2,1)S(1)}, bf16[288,576]{1,0:T(8,128)(2,1)S(1)}, u32[]{:S(2)}, u32[]{:S(2)}) %collective-permute-start.8) | collective-permute-done | bytes 331808 | tf_op jit(solution)/shard_map/ppermute | solution.py:69
  133.6 1.9 %collective-permute-start.9 = (bf16[288,576]{1,0:T(8,128)(2,1)S(1)}, bf16[288,576]{1,0:T(8,128)(2,1)S(1)}, u32[]{:S(2)}, u32[]{:S(2)}) collective-permute-start(bf16[288,576]{1,0:T(8,128)(2,1)S(1)} %collective-permute-done.8.refs_1_), channel_id=1, source_target_pairs={{0,8},{8,16},{16,24},{24,0},{1,9},{9,17},{17,25},{25,1},{2,10},{10... | collective-permute-start | bytes 995336 | tf_op jit(solution)/shard_map/ppermute | solution.py:69
  135.5 1.9 %collective-permute-start.5 = (bf16[288,576]{1,0:T(8,128)(2,1)S(1)}, bf16[288,576]{1,0:T(8,128)(2,1)S(1)}, u32[]{:S(2)}, u32[]{:S(2)}) collective-permute-start(bf16[288,576]{1,0:T(8,128)(2,1)S(1)} %bitcast.43), channel_id=1, source_target_pairs={{0,8},{8,16},{16,24},{24,0},{1,9},{9,17},{17,25},{25,1},{2,10},{10... | collective-permute-start | bytes 995336 | tf_op jit(solution)/shard_map/ppermute | solution.py:69
  137.4 4.6 %collective-permute-start.7 = (bf16[288,576]{1,0:T(8,128)(2,1)S(1)}, bf16[288,576]{1,0:T(8,128)(2,1)S(1)}, u32[]{:S(2)}, u32[]{:S(2)}) collective-permute-start(bf16[288,576]{1,0:T(8,128)(2,1)S(1)} %collective-permute-done.6.refs_3_), channel_id=1, source_target_pairs={{0,24},{8,0},{16,8},{24,16},{1,25},{9,1},{17,9},{25,17},{2,26},{10... | collective-permute-start | bytes 995336 | tf_op jit(solution)/shard_map/ppermute | solution.py:69
  142.0 9.6 %all-to-all-done.4 = bf16[8,4,72,256]{3,2,1,0:T(8,128)(2,1)} async-done(((bf16[8,4,72,256]{3,2,1,0:T(8,128)(2,1)}), bf16[8,4,72,256]{3,2,1,0:T(8,128)(2,1)}, u32[]{:S(2)}, u32[]{:S(2)}) %all-to-all-start.4) | async-done | bytes 1179680 | tf_op jit(solution)/shard_map/all_to_all | solution.py:15
  151.6 1.3 copy.4
  153.0 0.6 shard_map.18
  153.6 4.6 %collective-permute-start.11 = (f32[288,256]{1,0:T(8,128)S(1)}, f32[288,256]{1,0:T(8,128)S(1)}, u32[]{:S(2)}, u32[]{:S(2)}) collective-permute-start(f32[288,256]{1,0:T(8,128)S(1)} %shard_map.18), channel_id=1, source_target_pairs={{0,32},{32,0},{1,33},{33,1},{2,34},{34,2},{3,35},{35,3},{4,36},{36... | collective-permute-start | bytes 884744 | tf_op jit(solution)/shard_map/ppermute | solution.py:28
  158.2 0.6 shard_map.17
  159.4 0.7 fusion.12
  (18 shorter events, 1.3 us)
Async XLA Ops:
  2.0 13.9 %copy-start = (bf16[288,256]{1,0:T(8,128)(2,1)S(1)}, bf16[288,256]{1,0:T(8,128)(2,1)}, u32[]{:S(2)}) copy-start(bf16[288,256]{1,0:T(8,128)(2,1)} %param.1) | copy-start | bytes 442372
  2.0 42.5 %all-to-all-start = ((bf16[32,72,256]{2,1,0:T(8,128)(2,1)}), bf16[32,72,256]{2,1,0:T(8,128)(2,1)S(1)}, u32[]{:S(2)}, u32[]{:S(2)}) async-start(bf16[32,72,256]{2,1,0:T(8,128)(2,1)} %bitcast.5), calls=%async_computation | async-start | bytes 2359296 | tf_op jit(solution)/shard_map/all_to_all | solution.py:15
  15.9 10.6 %collective-permute-start = (bf16[288,256]{1,0:T(8,128)(2,1)S(1)}, bf16[288,256]{1,0:T(8,128)(2,1)S(1)}, u32[]{:S(2)}, u32[]{:S(2)}) collective-permute-start(bf16[288,256]{1,0:T(8,128)(2,1)S(1)} %copy-done), channel_id=1, source_target_pairs={{0,8},{8,16},{16,24},{24,0},{1,9},{9,17},{17,25},{25,1},{2,10},{10... | collective-permute-start | bytes 442376 | tf_op jit(solution)/shard_map/ppermute | solution.py:69
  19.1 12.2 %collective-permute-start.1 = (bf16[288,256]{1,0:T(8,128)(2,1)S(1)}, bf16[288,256]{1,0:T(8,128)(2,1)S(1)}, u32[]{:S(2)}, u32[]{:S(2)}) collective-permute-start(bf16[288,256]{1,0:T(8,128)(2,1)S(1)} %copy-done), channel_id=1, source_target_pairs={{0,16},{8,24},{16,0},{24,8},{1,17},{9,25},{17,1},{25,9},{2,18},{10... | collective-permute-start | bytes 442376 | tf_op jit(solution)/shard_map/ppermute | solution.py:69
  23.4 12.4 %collective-permute-start.2 = (bf16[288,256]{1,0:T(8,128)(2,1)S(1)}, bf16[288,256]{1,0:T(8,128)(2,1)S(1)}, u32[]{:S(2)}, u32[]{:S(2)}) collective-permute-start(bf16[288,256]{1,0:T(8,128)(2,1)S(1)} %copy-done), channel_id=1, source_target_pairs={{0,24},{8,0},{16,8},{24,16},{1,25},{9,1},{17,9},{25,17},{2,26},{10... | collective-permute-start | bytes 442376 | tf_op jit(solution)/shard_map/ppermute | solution.py:69
  35.9 8.7 %collective-permute-start.3 = (bf16[4,288,256]{2,1,0:T(8,128)(2,1)S(1)}, bf16[4,288,256]{2,1,0:T(8,128)(2,1)S(1)}, u32[]{:S(2)}, u32[]{:S(2)}) collective-permute-start(bf16[4,288,256]{2,1,0:T(8,128)(2,1)S(1)} %pad_maximum_fusion), channel_id=1, source_target_pairs={{0,32},{32,0},{1,33},{33,1},{2,34},{34,2},{3,35},{35,3},{4,36},{36... | collective-permute-start | bytes 1769480 | tf_op jit(solution)/shard_map/ppermute | solution.py:28
  91.5 9.3 %collective-permute-start.4 = (bf16[4,288,256]{2,1,0:T(8,128)(2,1)S(1)}, bf16[4,288,256]{2,1,0:T(8,128)(2,1)S(1)}, u32[]{:S(2)}, u32[]{:S(2)}) collective-permute-start(bf16[4,288,256]{2,1,0:T(8,128)(2,1)S(1)} %fusion), channel_id=1, source_target_pairs={{0,32},{32,0},{1,33},{33,1},{2,34},{34,2},{3,35},{35,3},{4,36},{36... | collective-permute-start | bytes 1769480 | tf_op jit(solution)/shard_map/ppermute | solution.py:28
  117.5 34.1 %all-to-all-start.4 = ((bf16[8,4,72,256]{3,2,1,0:T(8,128)(2,1)}), bf16[8,4,72,256]{3,2,1,0:T(8,128)(2,1)}, u32[]{:S(2)}, u32[]{:S(2)}) async-start(bf16[8,4,72,256]{3,2,1,0:T(8,128)(2,1)} %broadcast_in_dim.11), calls=%async_computation.4 | async-start | bytes 2359296 | tf_op jit(solution)/shard_map/all_to_all | solution.py:15
  121.8 11.8 %collective-permute-start.8 = (bf16[288,576]{1,0:T(8,128)(2,1)S(1)}, bf16[288,576]{1,0:T(8,128)(2,1)S(1)}, u32[]{:S(2)}, u32[]{:S(2)}) collective-permute-start(bf16[288,576]{1,0:T(8,128)(2,1)S(1)} %bitcast.46), channel_id=1, source_target_pairs={{0,8},{8,16},{16,24},{24,0},{1,9},{9,17},{17,25},{25,1},{2,10},{10... | collective-permute-start | bytes 995336 | tf_op jit(solution)/shard_map/ppermute | solution.py:69
  124.0 13.4 %collective-permute-start.6 = (bf16[288,576]{1,0:T(8,128)(2,1)S(1)}, bf16[288,576]{1,0:T(8,128)(2,1)S(1)}, u32[]{:S(2)}, u32[]{:S(2)}) collective-permute-start(bf16[288,576]{1,0:T(8,128)(2,1)S(1)} %bitcast.42), channel_id=1, source_target_pairs={{0,24},{8,0},{16,8},{24,16},{1,25},{9,1},{17,9},{25,17},{2,26},{10... | collective-permute-start | bytes 995336 | tf_op jit(solution)/shard_map/ppermute | solution.py:69
  128.3 24.7 %collective-permute-start.10 = (bf16[288,576]{1,0:T(8,128)(2,1)S(1)}, bf16[288,576]{1,0:T(8,128)(2,1)S(1)}, u32[]{:S(2)}, u32[]{:S(2)}) collective-permute-start(bf16[288,576]{1,0:T(8,128)(2,1)S(1)} %bitcast.47), channel_id=1, source_target_pairs={{0,24},{8,0},{16,8},{24,16},{1,25},{9,1},{17,9},{25,17},{2,26},{10... | collective-permute-start | bytes 995336 | tf_op jit(solution)/shard_map/ppermute | solution.py:69
  133.6 19.4 %collective-permute-start.9 = (bf16[288,576]{1,0:T(8,128)(2,1)S(1)}, bf16[288,576]{1,0:T(8,128)(2,1)S(1)}, u32[]{:S(2)}, u32[]{:S(2)}) collective-permute-start(bf16[288,576]{1,0:T(8,128)(2,1)S(1)} %collective-permute-done.8.refs_1_), channel_id=1, source_target_pairs={{0,8},{8,16},{16,24},{24,0},{1,9},{9,17},{17,25},{25,1},{2,10},{10... | collective-permute-start | bytes 995336 | tf_op jit(solution)/shard_map/ppermute | solution.py:69
  135.5 22.7 %collective-permute-start.5 = (bf16[288,576]{1,0:T(8,128)(2,1)S(1)}, bf16[288,576]{1,0:T(8,128)(2,1)S(1)}, u32[]{:S(2)}, u32[]{:S(2)}) collective-permute-start(bf16[288,576]{1,0:T(8,128)(2,1)S(1)} %bitcast.43), channel_id=1, source_target_pairs={{0,8},{8,16},{16,24},{24,0},{1,9},{9,17},{17,25},{25,1},{2,10},{10... | collective-permute-start | bytes 995336 | tf_op jit(solution)/shard_map/ppermute | solution.py:69
  137.4 20.8 %collective-permute-start.7 = (bf16[288,576]{1,0:T(8,128)(2,1)S(1)}, bf16[288,576]{1,0:T(8,128)(2,1)S(1)}, u32[]{:S(2)}, u32[]{:S(2)}) collective-permute-start(bf16[288,576]{1,0:T(8,128)(2,1)S(1)} %collective-permute-done.6.refs_3_), channel_id=1, source_target_pairs={{0,24},{8,0},{16,8},{24,16},{1,25},{9,1},{17,9},{25,17},{2,26},{10... | collective-permute-start | bytes 995336 | tf_op jit(solution)/shard_map/ppermute | solution.py:69
  153.6 5.8 %collective-permute-start.11 = (f32[288,256]{1,0:T(8,128)S(1)}, f32[288,256]{1,0:T(8,128)S(1)}, u32[]{:S(2)}, u32[]{:S(2)}) collective-permute-start(f32[288,256]{1,0:T(8,128)S(1)} %shard_map.18), channel_id=1, source_target_pairs={{0,32},{32,0},{1,33},{33,1},{2,34},{34,2},{3,35},{35,3},{4,36},{36... | collective-permute-start | bytes 884744 | tf_op jit(solution)/shard_map/ppermute | solution.py:28

commit v8 on v7

--- a/solution.py
+++ b/solution.py
@@ -33,29 +33,30 @@
     return blocks.swapaxes(0, 1).reshape(nx, n * rows, cols)
 
 
-def product_kernel(right, *refs):
-    *blocks, out = refs
+def product_kernel(blocks, right, out):
     nx = right.shape[0]
     here = lax.axis_index("x")
     out[...] = sum(
-        jnp.dot(block[...], right[lax.rem(here + (nx - hop), nx)], preferred_element_type=F32)
-        for hop, block in enumerate(blocks)
+        jnp.dot(blocks[hop], right[lax.rem(here + (nx - hop), nx)], preferred_element_type=F32)
+        for hop in range(nx)
     )
 
 
-def product(right, *blocks):
-    rows, depth = blocks[0].shape
+def product(blocks, right):
+    _, rows, _ = blocks.shape
     cols = right.shape[2]
-    size = 2 * rows * depth * cols * len(blocks)
-    moved = 2 * right.size + 2 * rows * depth * len(blocks) + 4 * rows * cols
     return pl.pallas_call(
         product_kernel,
         out_shape=jax.ShapeDtypeStruct((rows, cols), F32),
-        in_specs=[pl.BlockSpec(memory_space=pltpu.VMEM)] * (1 + len(blocks)),
+        in_specs=[pl.BlockSpec(memory_space=pltpu.VMEM)] * 2,
         out_specs=pl.BlockSpec(memory_space=pltpu.VMEM),
         compiler_params=pltpu.CompilerParams(vmem_limit_bytes=16 << 20),
-        cost_estimate=pl.CostEstimate(flops=size, bytes_accessed=moved, transcendentals=0),
-    )(right, *blocks)
+        cost_estimate=pl.CostEstimate(
+            flops=2 * blocks.size * cols,
+            bytes_accessed=2 * right.size + 2 * blocks.size + 4 * rows * cols,
+            transcendentals=0,
+        ),
+    )(blocks, right)
 
 
 def on_device(own):
@@ -95,8 +96,10 @@
     above_top, below_bottom = shift_x(top, -1), shift_x(bottom, 1)
     above_bottom, below_top = shift_x(bottom, -1), shift_x(top, 1)
     far_top, far_bottom = shift_x(above_top, -1), shift_x(below_bottom, 1)
-    other = swap_cores(product(right, bottom, below_bottom, far_bottom, above_bottom))
-    second = product(right, top, below_top, far_top, above_top) + other
+    bottoms = jnp.stack([bottom, below_bottom, far_bottom, above_bottom])
+    other = swap_cores(product(bottoms, right))
+    tops = jnp.stack([top, below_top, far_top, above_top])
+    second = product(tops, right) + other
     scale = math.sqrt(COLS)
     return (scale * (3.4445 * own.astype(F32) + second)).astype(BF16)
 

time: 161 us -> 160 us (level)
  starting transfers between devices: 60.2 us -> 57.4 us
  other arithmetic: 1.24 us -> 3.04 us
    ppermute x3, starting transfers between devices: 14.7 us -> 12.6 us  [swap_cores(): return lax.ppermute(block, 'core', [(0, 1), (1, 0)])]
    another operation x0 -> x2, other arithmetic: none -> 1.8 us  [the longest x1 1.5 us: on_device(): tops = jnp.stack([top, below_top, far_top, above_top])]
    ppermute x9, waiting for transfers between devices: 12.6 us -> 14.4 us  [shift_x(): return lax.ppermute(block, 'x', [(i, (i + hop) % nx) for i in range(nx)])]
  transfers between devices with their start and end apart: 14 -> 14, of which waited for: 7 -> 8; matrix products, arithmetic and copies ran while one was open for 1% -> 2% of each run, Pallas kernels for 1% -> 1%
where the time goes in v8:
time: 160 us; the launch traced here: 159 us
  blocking collectives  60.2 us (38%)
  starting transfers between devices  57.4 us (36%)
  waiting for transfers between devices  31.1 us (19%)
  local copies, waits for them, and re-layouts  3.46 us (2%)
  other arithmetic  3.04 us (2%)
  matrix products  2.37 us (1%)
    all_to_all x3, blocking collectives, exchange(): return lax.all_to_all(chunks, axis, 0, 0)  60.2 us
    ppermute x9, starting transfers between devices, shift_x(): return lax.ppermute(block, 'x', [(i, (i + hop) % nx) for i in range(nx)])  27.4 us
    all_to_all x2, starting transfers between devices, exchange(): return lax.all_to_all(chunks, axis, 0, 0)  17.4 us
    all_to_all x2, waiting for transfers between devices, exchange(): return lax.all_to_all(chunks, axis, 0, 0)  15.8 us
    ppermute x9, waiting for transfers between devices, shift_x(): return lax.ppermute(block, 'x', [(i, (i + hop) % nx) for i in range(nx)])  14.4 us
    ppermute x3, starting transfers between devices, swap_cores(): return lax.ppermute(block, 'core', [(0, 1), (1, 0)])  12.6 us
  transfers between devices with their start and end apart: 14, of which 8 were waited for; matrix products, arithmetic and copies ran while one was open for 2% of the time, Pallas kernels for 1%

profile of v8, /device:TPU:1, one launch (start us, length us, event | category | flops | bytes accessed | tf_op | source)
XLA Modules:
  0.0 159.1 jit_solution(4093286459902182931)
XLA Ops:
  0.0 2.0 %broadcast_in_dim.9 = bf16[8,4,72,256]{3,2,1,0:T(8,128)(2,1)} broadcast(bf16[4,72,256]{2,1,0:T(8,128)(2,1)} %bitcast.58), dimensions={1,2,3} | broadcast | bytes 1327104 | tf_op jit(solution)/shard_map/broadcast_in_dim | solution.py:72
  2.0 13.8 %all-to-all-start = ((bf16[32,72,256]{2,1,0:T(8,128)(2,1)}), bf16[32,72,256]{2,1,0:T(8,128)(2,1)S(1)}, u32[]{:S(2)}, u32[]{:S(2)}) async-start(bf16[32,72,256]{2,1,0:T(8,128)(2,1)} %bitcast.5), calls=%async_computation | async-start | bytes 2359296 | tf_op jit(solution)/shard_map/all_to_all | solution.py:15
  15.9 3.1 %collective-permute-start = (bf16[288,256]{1,0:T(8,128)(2,1)S(1)}, bf16[288,256]{1,0:T(8,128)(2,1)S(1)}, u32[]{:S(2)}, u32[]{:S(2)}) collective-permute-start(bf16[288,256]{1,0:T(8,128)(2,1)S(1)} %copy-done), channel_id=1, source_target_pairs={{0,8},{8,16},{16,24},{24,0},{1,9},{9,17},{17,25},{25,1},{2,10},{10... | collective-permute-start | bytes 442376 | tf_op jit(solution)/shard_map/ppermute | solution.py:70
  19.1 4.3 %collective-permute-start.1 = (bf16[288,256]{1,0:T(8,128)(2,1)S(1)}, bf16[288,256]{1,0:T(8,128)(2,1)S(1)}, u32[]{:S(2)}, u32[]{:S(2)}) collective-permute-start(bf16[288,256]{1,0:T(8,128)(2,1)S(1)} %copy-done), channel_id=1, source_target_pairs={{0,16},{8,24},{16,0},{24,8},{1,17},{9,25},{17,1},{25,9},{2,18},{10... | collective-permute-start | bytes 442376 | tf_op jit(solution)/shard_map/ppermute | solution.py:70
  23.4 3.1 %collective-permute-start.2 = (bf16[288,256]{1,0:T(8,128)(2,1)S(1)}, bf16[288,256]{1,0:T(8,128)(2,1)S(1)}, u32[]{:S(2)}, u32[]{:S(2)}) collective-permute-start(bf16[288,256]{1,0:T(8,128)(2,1)S(1)} %copy-done), channel_id=1, source_target_pairs={{0,24},{8,0},{16,8},{24,16},{1,25},{9,1},{17,9},{25,17},{2,26},{10... | collective-permute-start | bytes 442376 | tf_op jit(solution)/shard_map/ppermute | solution.py:70
  26.5 4.8 %collective-permute-done.1 = bf16[288,256]{1,0:T(8,128)(2,1)S(1)} collective-permute-done((bf16[288,256]{1,0:T(8,128)(2,1)S(1)}, bf16[288,256]{1,0:T(8,128)(2,1)S(1)}, u32[]{:S(2)}, u32[]{:S(2)}) %collective-permute-start.1) | collective-permute-done | bytes 147488 | tf_op jit(solution)/shard_map/ppermute | solution.py:70
  31.3 4.5 %collective-permute-done.2 = bf16[288,256]{1,0:T(8,128)(2,1)S(1)} collective-permute-done((bf16[288,256]{1,0:T(8,128)(2,1)S(1)}, bf16[288,256]{1,0:T(8,128)(2,1)S(1)}, u32[]{:S(2)}, u32[]{:S(2)}) %collective-permute-start.2) | collective-permute-done | bytes 147488 | tf_op jit(solution)/shard_map/ppermute | solution.py:70
  35.9 2.5 %collective-permute-start.3 = (bf16[4,288,256]{2,1,0:T(8,128)(2,1)S(1)}, bf16[4,288,256]{2,1,0:T(8,128)(2,1)S(1)}, u32[]{:S(2)}, u32[]{:S(2)}) collective-permute-start(bf16[4,288,256]{2,1,0:T(8,128)(2,1)S(1)} %pad_maximum_fusion.2), channel_id=1, source_target_pairs={{0,32},{32,0},{1,33},{33,1},{2,34},{34,2},{3,35},{35,3},{4,36},{36... | collective-permute-start | bytes 1769480 | tf_op jit(solution)/shard_map/ppermute | solution.py:28
  38.4 6.1 %all-to-all-done = bf16[32,72,256]{2,1,0:T(8,128)(2,1)S(1)} async-done(((bf16[32,72,256]{2,1,0:T(8,128)(2,1)}), bf16[32,72,256]{2,1,0:T(8,128)(2,1)S(1)}, u32[]{:S(2)}, u32[]{:S(2)}) %all-to-all-start) | async-done | bytes 1179680 | tf_op jit(solution)/shard_map/all_to_all | solution.py:15
  44.6 1.1 bitcast_convert_fusion
  45.7 24.3 %all_to_all.25 = bf16[8,72,576]{2,1,0:T(8,128)(2,1)S(1)} all-to-all(bf16[8,72,576]{2,1,0:T(8,128)(2,1)S(1)} %bitcast.63), channel_id=1, replica_groups=mesh['z'=8,'core'=2,'x'=4,'y'=8] {'y'}, dimensions={0} | all-to-all | bytes 1327104 | tf_op jit(solution)/shard_map/all_to_all | solution.py:15
  70.2 20.6 %all_to_all.26 = bf16[8,72,576]{2,1,0:T(8,128)(2,1)S(1)} all-to-all(bf16[8,72,576]{2,1,0:T(8,128)(2,1)S(1)} %broadcast_in_dim.10), channel_id=1, replica_groups=mesh['z'=8,'core'=2,'x'=4,'y'=8] {'y'}, dimensions={0} | all-to-all | bytes 1327104 | tf_op jit(solution)/shard_map/all_to_all | solution.py:15
  90.8 0.6 fusion
  91.5 7.7 %collective-permute-start.4 = (bf16[4,288,256]{2,1,0:T(8,128)(2,1)S(1)}, bf16[4,288,256]{2,1,0:T(8,128)(2,1)S(1)}, u32[]{:S(2)}, u32[]{:S(2)}) collective-permute-start(bf16[4,288,256]{2,1,0:T(8,128)(2,1)S(1)} %fusion), channel_id=1, source_target_pairs={{0,32},{32,0},{1,33},{33,1},{2,34},{34,2},{3,35},{35,3},{4,36},{36... | collective-permute-start | bytes 1769480 | tf_op jit(solution)/shard_map/ppermute | solution.py:28
  99.2 0.6 convolution_bitcast_fusion
  99.8 1.0 collective-permute-done.4
  100.9 15.4 %all_to_all.27 = bf16[4,288,256]{2,1,0:T(8,128)(2,1)S(1)} all-to-all(bf16[4,288,256]{2,1,0:T(8,128)(2,1)S(1)} %add_convert_fusion), channel_id=1, replica_groups=mesh['z'=8,'core'=2,'x'=4,'y'=8] {'x'}, dimensions={0} | all-to-all | bytes 1179648 | tf_op jit(solution)/shard_map/all_to_all | solution.py:15
  116.4 1.1 broadcast_in_dim.11
  117.6 3.6 %all-to-all-start.4 = ((bf16[8,4,72,256]{3,2,1,0:T(8,128)(2,1)}), bf16[8,4,72,256]{3,2,1,0:T(8,128)(2,1)S(1)}, u32[]{:S(2)}, u32[]{:S(2)}) async-start(bf16[8,4,72,256]{3,2,1,0:T(8,128)(2,1)} %broadcast_in_dim.11), calls=%async_computation.4 | async-start | bytes 2359296 | tf_op jit(solution)/shard_map/all_to_all | solution.py:15
  121.1 2.2 %collective-permute-start.8 = (bf16[288,576]{1,0:T(8,128)(2,1)S(1)}, bf16[288,576]{1,0:T(8,128)(2,1)S(1)}, u32[]{:S(2)}, u32[]{:S(2)}) collective-permute-start(bf16[288,576]{1,0:T(8,128)(2,1)S(1)} %bitcast.60), channel_id=1, source_target_pairs={{0,8},{8,16},{16,24},{24,0},{1,9},{9,17},{17,25},{25,1},{2,10},{10... | collective-permute-start | bytes 995336 | tf_op jit(solution)/shard_map/ppermute | solution.py:70
  123.4 4.3 %collective-permute-start.6 = (bf16[288,576]{1,0:T(8,128)(2,1)S(1)}, bf16[288,576]{1,0:T(8,128)(2,1)}, u32[]{:S(2)}, u32[]{:S(2)}) collective-permute-start(bf16[288,576]{1,0:T(8,128)(2,1)S(1)} %bitcast.55), channel_id=1, source_target_pairs={{0,24},{8,0},{16,8},{24,16},{1,25},{9,1},{17,9},{25,17},{2,26},{10... | collective-permute-start | bytes 995336 | tf_op jit(solution)/shard_map/ppermute | solution.py:70
  127.7 1.9 %collective-permute-start.10 = (bf16[288,576]{1,0:T(8,128)(2,1)S(1)}, bf16[288,576]{1,0:T(8,128)(2,1)S(1)}, u32[]{:S(2)}, u32[]{:S(2)}) collective-permute-start(bf16[288,576]{1,0:T(8,128)(2,1)S(1)} %bitcast.61), channel_id=1, source_target_pairs={{0,24},{8,0},{16,8},{24,16},{1,25},{9,1},{17,9},{25,17},{2,26},{10... | collective-permute-start | bytes 995336 | tf_op jit(solution)/shard_map/ppermute | solution.py:70
  129.6 3.0 %collective-permute-done.8 = bf16[288,576]{1,0:T(8,128)(2,1)S(1)} collective-permute-done((bf16[288,576]{1,0:T(8,128)(2,1)S(1)}, bf16[288,576]{1,0:T(8,128)(2,1)S(1)}, u32[]{:S(2)}, u32[]{:S(2)}) %collective-permute-start.8) | collective-permute-done | bytes 331808 | tf_op jit(solution)/shard_map/ppermute | solution.py:70
  132.6 1.9 %collective-permute-start.9 = (bf16[288,576]{1,0:T(8,128)(2,1)S(1)}, bf16[288,576]{1,0:T(8,128)(2,1)S(1)}, u32[]{:S(2)}, u32[]{:S(2)}) collective-permute-start(bf16[288,576]{1,0:T(8,128)(2,1)S(1)} %collective-permute-done.8), channel_id=1, source_target_pairs={{0,8},{8,16},{16,24},{24,0},{1,9},{9,17},{17,25},{25,1},{2,10},{10... | collective-permute-start | bytes 995336 | tf_op jit(solution)/shard_map/ppermute | solution.py:70
  134.5 1.9 %collective-permute-start.5 = (bf16[288,576]{1,0:T(8,128)(2,1)S(1)}, bf16[288,576]{1,0:T(8,128)(2,1)}, u32[]{:S(2)}, u32[]{:S(2)}) collective-permute-start(bf16[288,576]{1,0:T(8,128)(2,1)S(1)} %bitcast.56), channel_id=1, source_target_pairs={{0,8},{8,16},{16,24},{24,0},{1,9},{9,17},{17,25},{25,1},{2,10},{10... | collective-permute-start | bytes 995336 | tf_op jit(solution)/shard_map/ppermute | solution.py:70
  136.5 4.6 %collective-permute-start.7 = (bf16[288,576]{1,0:T(8,128)(2,1)}, bf16[288,576]{1,0:T(8,128)(2,1)}, u32[]{:S(2)}, u32[]{:S(2)}) collective-permute-start(bf16[288,576]{1,0:T(8,128)(2,1)} %collective-permute-done.6), channel_id=1, source_target_pairs={{0,24},{8,0},{16,8},{24,16},{1,25},{9,1},{17,9},{25,17},{2,26},{10... | collective-permute-start | bytes 995336 | tf_op jit(solution)/shard_map/ppermute | solution.py:70
  141.4 1.7 %collective-permute-done.9 = bf16[288,576]{1,0:T(8,128)(2,1)S(1)} collective-permute-done((bf16[288,576]{1,0:T(8,128)(2,1)S(1)}, bf16[288,576]{1,0:T(8,128)(2,1)S(1)}, u32[]{:S(2)}, u32[]{:S(2)}) %collective-permute-start.9) | collective-permute-done | bytes 331808 | tf_op jit(solution)/shard_map/ppermute | solution.py:70
  143.4 9.7 %all-to-all-done.4 = bf16[8,4,72,256]{3,2,1,0:T(8,128)(2,1)S(1)} async-done(((bf16[8,4,72,256]{3,2,1,0:T(8,128)(2,1)}), bf16[8,4,72,256]{3,2,1,0:T(8,128)(2,1)S(1)}, u32[]{:S(2)}, u32[]{:S(2)}) %all-to-all-start.4) | async-done | bytes 1179680 | tf_op jit(solution)/shard_map/all_to_all | solution.py:15
  153.2 0.6 shard_map.18
  153.8 2.4 %collective-permute-start.11 = (f32[288,256]{1,0:T(8,128)S(1)}, f32[288,256]{1,0:T(8,128)S(1)}, u32[]{:S(2)}, u32[]{:S(2)}) collective-permute-start(f32[288,256]{1,0:T(8,128)S(1)} %shard_map.18), channel_id=1, source_target_pairs={{0,32},{32,0},{1,33},{33,1},{2,34},{34,2},{3,35},{35,3},{4,36},{36... | collective-permute-start | bytes 884744 | tf_op jit(solution)/shard_map/ppermute | solution.py:28
  156.2 1.5 pad_maximum_fusion.blocks
  158.4 0.7 fusion.12
  (20 shorter events, 2.1 us)
Async XLA Ops:
  2.0 13.9 %copy-start = (bf16[288,256]{1,0:T(8,128)(2,1)S(1)}, bf16[288,256]{1,0:T(8,128)(2,1)}, u32[]{:S(2)}) copy-start(bf16[288,256]{1,0:T(8,128)(2,1)} %param.1) | copy-start | bytes 442372
  2.0 42.5 %all-to-all-start = ((bf16[32,72,256]{2,1,0:T(8,128)(2,1)}), bf16[32,72,256]{2,1,0:T(8,128)(2,1)S(1)}, u32[]{:S(2)}, u32[]{:S(2)}) async-start(bf16[32,72,256]{2,1,0:T(8,128)(2,1)} %bitcast.5), calls=%async_computation | async-start | bytes 2359296 | tf_op jit(solution)/shard_map/all_to_all | solution.py:15
  15.9 10.6 %collective-permute-start = (bf16[288,256]{1,0:T(8,128)(2,1)S(1)}, bf16[288,256]{1,0:T(8,128)(2,1)S(1)}, u32[]{:S(2)}, u32[]{:S(2)}) collective-permute-start(bf16[288,256]{1,0:T(8,128)(2,1)S(1)} %copy-done), channel_id=1, source_target_pairs={{0,8},{8,16},{16,24},{24,0},{1,9},{9,17},{17,25},{25,1},{2,10},{10... | collective-permute-start | bytes 442376 | tf_op jit(solution)/shard_map/ppermute | solution.py:70
  19.1 12.2 %collective-permute-start.1 = (bf16[288,256]{1,0:T(8,128)(2,1)S(1)}, bf16[288,256]{1,0:T(8,128)(2,1)S(1)}, u32[]{:S(2)}, u32[]{:S(2)}) collective-permute-start(bf16[288,256]{1,0:T(8,128)(2,1)S(1)} %copy-done), channel_id=1, source_target_pairs={{0,16},{8,24},{16,0},{24,8},{1,17},{9,25},{17,1},{25,9},{2,18},{10... | collective-permute-start | bytes 442376 | tf_op jit(solution)/shard_map/ppermute | solution.py:70
  23.4 12.4 %collective-permute-start.2 = (bf16[288,256]{1,0:T(8,128)(2,1)S(1)}, bf16[288,256]{1,0:T(8,128)(2,1)S(1)}, u32[]{:S(2)}, u32[]{:S(2)}) collective-permute-start(bf16[288,256]{1,0:T(8,128)(2,1)S(1)} %copy-done), channel_id=1, source_target_pairs={{0,24},{8,0},{16,8},{24,16},{1,25},{9,1},{17,9},{25,17},{2,26},{10... | collective-permute-start | bytes 442376 | tf_op jit(solution)/shard_map/ppermute | solution.py:70
  35.9 8.7 %collective-permute-start.3 = (bf16[4,288,256]{2,1,0:T(8,128)(2,1)S(1)}, bf16[4,288,256]{2,1,0:T(8,128)(2,1)S(1)}, u32[]{:S(2)}, u32[]{:S(2)}) collective-permute-start(bf16[4,288,256]{2,1,0:T(8,128)(2,1)S(1)} %pad_maximum_fusion.2), channel_id=1, source_target_pairs={{0,32},{32,0},{1,33},{33,1},{2,34},{34,2},{3,35},{35,3},{4,36},{36... | collective-permute-start | bytes 1769480 | tf_op jit(solution)/shard_map/ppermute | solution.py:28
  91.5 9.3 %collective-permute-start.4 = (bf16[4,288,256]{2,1,0:T(8,128)(2,1)S(1)}, bf16[4,288,256]{2,1,0:T(8,128)(2,1)S(1)}, u32[]{:S(2)}, u32[]{:S(2)}) collective-permute-start(bf16[4,288,256]{2,1,0:T(8,128)(2,1)S(1)} %fusion), channel_id=1, source_target_pairs={{0,32},{32,0},{1,33},{33,1},{2,34},{34,2},{3,35},{35,3},{4,36},{36... | collective-permute-start | bytes 1769480 | tf_op jit(solution)/shard_map/ppermute | solution.py:28
  117.6 35.5 %all-to-all-start.4 = ((bf16[8,4,72,256]{3,2,1,0:T(8,128)(2,1)}), bf16[8,4,72,256]{3,2,1,0:T(8,128)(2,1)S(1)}, u32[]{:S(2)}, u32[]{:S(2)}) async-start(bf16[8,4,72,256]{3,2,1,0:T(8,128)(2,1)} %broadcast_in_dim.11), calls=%async_computation.4 | async-start | bytes 2359296 | tf_op jit(solution)/shard_map/all_to_all | solution.py:15
  121.1 11.5 %collective-permute-start.8 = (bf16[288,576]{1,0:T(8,128)(2,1)S(1)}, bf16[288,576]{1,0:T(8,128)(2,1)S(1)}, u32[]{:S(2)}, u32[]{:S(2)}) collective-permute-start(bf16[288,576]{1,0:T(8,128)(2,1)S(1)} %bitcast.60), channel_id=1, source_target_pairs={{0,8},{8,16},{16,24},{24,0},{1,9},{9,17},{17,25},{25,1},{2,10},{10... | collective-permute-start | bytes 995336 | tf_op jit(solution)/shard_map/ppermute | solution.py:70
  123.4 13.1 %collective-permute-start.6 = (bf16[288,576]{1,0:T(8,128)(2,1)S(1)}, bf16[288,576]{1,0:T(8,128)(2,1)}, u32[]{:S(2)}, u32[]{:S(2)}) collective-permute-start(bf16[288,576]{1,0:T(8,128)(2,1)S(1)} %bitcast.55), channel_id=1, source_target_pairs={{0,24},{8,0},{16,8},{24,16},{1,25},{9,1},{17,9},{25,17},{2,26},{10... | collective-permute-start | bytes 995336 | tf_op jit(solution)/shard_map/ppermute | solution.py:70
  127.7 13.7 %collective-permute-start.10 = (bf16[288,576]{1,0:T(8,128)(2,1)S(1)}, bf16[288,576]{1,0:T(8,128)(2,1)S(1)}, u32[]{:S(2)}, u32[]{:S(2)}) collective-permute-start(bf16[288,576]{1,0:T(8,128)(2,1)S(1)} %bitcast.61), channel_id=1, source_target_pairs={{0,24},{8,0},{16,8},{24,16},{1,25},{9,1},{17,9},{25,17},{2,26},{10... | collective-permute-start | bytes 995336 | tf_op jit(solution)/shard_map/ppermute | solution.py:70
  132.6 10.5 %collective-permute-start.9 = (bf16[288,576]{1,0:T(8,128)(2,1)S(1)}, bf16[288,576]{1,0:T(8,128)(2,1)S(1)}, u32[]{:S(2)}, u32[]{:S(2)}) collective-permute-start(bf16[288,576]{1,0:T(8,128)(2,1)S(1)} %collective-permute-done.8), channel_id=1, source_target_pairs={{0,8},{8,16},{16,24},{24,0},{1,9},{9,17},{17,25},{25,1},{2,10},{10... | collective-permute-start | bytes 995336 | tf_op jit(solution)/shard_map/ppermute | solution.py:70
  134.5 21.7 %collective-permute-start.5 = (bf16[288,576]{1,0:T(8,128)(2,1)S(1)}, bf16[288,576]{1,0:T(8,128)(2,1)}, u32[]{:S(2)}, u32[]{:S(2)}) collective-permute-start(bf16[288,576]{1,0:T(8,128)(2,1)S(1)} %bitcast.56), channel_id=1, source_target_pairs={{0,8},{8,16},{16,24},{24,0},{1,9},{9,17},{17,25},{25,1},{2,10},{10... | collective-permute-start | bytes 995336 | tf_op jit(solution)/shard_map/ppermute | solution.py:70
  136.5 19.8 %collective-permute-start.7 = (bf16[288,576]{1,0:T(8,128)(2,1)}, bf16[288,576]{1,0:T(8,128)(2,1)}, u32[]{:S(2)}, u32[]{:S(2)}) collective-permute-start(bf16[288,576]{1,0:T(8,128)(2,1)} %collective-permute-done.6), channel_id=1, source_target_pairs={{0,24},{8,0},{16,8},{24,16},{1,25},{9,1},{17,9},{25,17},{2,26},{10... | collective-permute-start | bytes 995336 | tf_op jit(solution)/shard_map/ppermute | solution.py:70
  153.8 4.6 %collective-permute-start.11 = (f32[288,256]{1,0:T(8,128)S(1)}, f32[288,256]{1,0:T(8,128)S(1)}, u32[]{:S(2)}, u32[]{:S(2)}) collective-permute-start(f32[288,256]{1,0:T(8,128)S(1)} %shard_map.18), channel_id=1, source_target_pairs={{0,32},{32,0},{1,33},{33,1},{2,34},{34,2},{3,35},{35,3},{4,36},{36... | collective-permute-start | bytes 884744 | tf_op jit(solution)/shard_map/ppermute | solution.py:28

commit v9 on v8

--- a/solution.py
+++ b/solution.py
@@ -59,6 +59,74 @@
     )(blocks, right)
 
 
+LANES = 128
+
+
+def gram_kernel(left, right, out):
+    nx, rows, _ = left.shape
+    total = sum(
+        lax.dot_general(left[i], right[i], (((1,), (1,)), ((), ())), preferred_element_type=F32)
+        for i in range(nx)
+    ).astype(BF16)
+    parts, half = out.shape[0], rows // 2
+    share = out.shape[1] - half
+    for part in range(parts):
+        tile, side = part // 2, part % 2
+        out[part, :half, :] = total[side * half : (side + 1) * half, tile * LANES : (tile + 1) * LANES]
+    last = parts // 2 * LANES
+    tail = jnp.concatenate([total[:half, last:], total[half:, last:]], 1)
+    for part in range(parts):
+        if part * share < half:
+            out[part, half:, :] = tail[part * share : (part + 1) * share]
+        else:
+            out[part, half:, :] = jnp.zeros((share, LANES), BF16)
+
+
+def packed_gram(left, right, parts):
+    nx, rows, cols = left.shape
+    share = 48
+    return pl.pallas_call(
+        gram_kernel,
+        out_shape=jax.ShapeDtypeStruct((parts, rows // 2 + share, LANES), BF16),
+        in_specs=[pl.BlockSpec(memory_space=pltpu.VMEM)] * 2,
+        out_specs=pl.BlockSpec(memory_space=pltpu.VMEM),
+        compiler_params=pltpu.CompilerParams(vmem_limit_bytes=24 << 20),
+        cost_estimate=pl.CostEstimate(
+            flops=2 * rows * rows * nx * cols,
+            bytes_accessed=4 * left.size + 2 * rows * rows,
+            transcendentals=0,
+        ),
+    )(left, right)
+
+
+def unpack_kernel(chunks, top, bottom):
+    parts, half = chunks.shape[0], top.shape[0]
+    share = chunks.shape[1] - half
+    for part in range(parts):
+        side, tile = (top, bottom)[part % 2], part // 2
+        side[:, tile * LANES : (tile + 1) * LANES] = chunks[part, :half, :]
+    last = parts // 2 * LANES
+    for part in range(half // share):
+        piece = chunks[part, half:, :]
+        rows = slice(part * share, (part + 1) * share)
+        top[rows, last:] = piece[:, : LANES // 2]
+        bottom[rows, last:] = piece[:, LANES // 2 :]
+
+
+def unpacked(chunks, rows, cols):
+    half = jax.ShapeDtypeStruct((rows // 2, cols), BF16)
+    return pl.pallas_call(
+        unpack_kernel,
+        out_shape=(half, half),
+        in_specs=[pl.BlockSpec(memory_space=pltpu.VMEM)],
+        out_specs=(pl.BlockSpec(memory_space=pltpu.VMEM),) * 2,
+        compiler_params=pltpu.CompilerParams(vmem_limit_bytes=8 << 20),
+        cost_estimate=pl.CostEstimate(
+            flops=0, bytes_accessed=2 * chunks.size + 2 * rows * cols, transcendentals=0
+        ),
+    )(chunks)
+
+
 def on_device(own):
     rows, cols = own.shape
     nx, ny, nz = (lax.axis_size(a) for a in "xyz")
@@ -77,10 +145,8 @@
     wide = jnp.stack([lax.select_n(hop, *blocks) for hop in order])
 
     left = jnp.concatenate([wide, swap_cores(wide)], 1)
-    partial = jnp.einsum("xrc,xjc->rj", left, panel, preferred_element_type=F32)
-    partial = partial.astype(BF16).reshape(ny, 2 * rows // ny, depth)
-    gram = gather(reduce_scatter(partial, "y").astype(BF16), "y").reshape(2 * rows, depth)
-    top, bottom = gram[:rows], gram[rows:]
+    chunk = reduce_scatter(packed_gram(left, panel, ny), "y").astype(BF16)
+    top, bottom = unpacked(gather(chunk, "y"), 2 * rows, depth)
 
     def times(left, right):
         return jnp.einsum("rj,xjc->xrc", left, right, preferred_element_type=F32)

time: 160 us -> 158 us (0.988)
  blocking collectives: 60.2 us -> 58.3 us
    all_to_all x3, blocking collectives: 60.2 us -> 58.3 us  [exchange(): return lax.all_to_all(chunks, axis, 0, 0)]
    ppermute x3, waiting for transfers between devices: 0.98 us -> 2.59 us  [swap_cores(): return lax.ppermute(block, 'core', [(0, 1), (1, 0)])]
  transfers between devices with their start and end apart: 14 -> 14, of which waited for: 8 -> 9; matrix products, arithmetic and copies ran while one was open for 2% -> 2% of each run, Pallas kernels for 1% -> 1%
where the time goes in v9:
time: 158 us; the launch traced here: 157 us
  blocking collectives  58.3 us (37%)
  starting transfers between devices  57.2 us (36%)
  waiting for transfers between devices  31.1 us (20%)
  local copies, waits for them, and re-layouts  3.42 us (2%)
  other arithmetic  3.1 us (2%)
  Pallas kernels  2.5 us (2%)
    all_to_all x3, blocking collectives, exchange(): return lax.all_to_all(chunks, axis, 0, 0)  58.3 us
    ppermute x9, starting transfers between devices, shift_x(): return lax.ppermute(block, 'x', [(i, (i + hop) % nx) for i in range(nx)])  27.3 us
    all_to_all x2, starting transfers between devices, exchange(): return lax.all_to_all(chunks, axis, 0, 0)  17.7 us
    all_to_all x2, waiting for transfers between devices, exchange(): return lax.all_to_all(chunks, axis, 0, 0)  14.3 us
    ppermute x9, waiting for transfers between devices, shift_x(): return lax.ppermute(block, 'x', [(i, (i + hop) % nx) for i in range(nx)])  14.2 us
    ppermute x3, starting transfers between devices, swap_cores(): return lax.ppermute(block, 'core', [(0, 1), (1, 0)])  12.2 us
  transfers between devices with their start and end apart: 14, of which 9 were waited for; matrix products, arithmetic and copies ran while one was open for 2% of the time, Pallas kernels for 1%

profile of v9, /device:TPU:1, one launch (start us, length us, event | category | flops | bytes accessed | tf_op | source)
XLA Modules:
  0.0 157.1 jit_solution(2824469537616765034)
XLA Ops:
  0.0 2.0 %broadcast_in_dim.9 = bf16[8,4,72,256]{3,2,1,0:T(8,128)(2,1)} broadcast(bf16[4,72,256]{2,1,0:T(8,128)(2,1)} %bitcast.50), dimensions={1,2,3} | broadcast | bytes 1327104 | tf_op jit(solution)/shard_map/broadcast_in_dim | solution.py:140
  2.0 13.8 %all-to-all-start = ((bf16[32,72,256]{2,1,0:T(8,128)(2,1)}), bf16[32,72,256]{2,1,0:T(8,128)(2,1)S(1)}, u32[]{:S(2)}, u32[]{:S(2)}) async-start(bf16[32,72,256]{2,1,0:T(8,128)(2,1)} %bitcast.5), calls=%async_computation | async-start | bytes 2359296 | tf_op jit(solution)/shard_map/all_to_all | solution.py:15
  15.9 3.1 %collective-permute-start = (bf16[288,256]{1,0:T(8,128)(2,1)S(1)}, bf16[288,256]{1,0:T(8,128)(2,1)S(1)}, u32[]{:S(2)}, u32[]{:S(2)}) collective-permute-start(bf16[288,256]{1,0:T(8,128)(2,1)S(1)} %copy-done), channel_id=1, source_target_pairs={{0,8},{8,16},{16,24},{24,0},{1,9},{9,17},{17,25},{25,1},{2,10},{10... | collective-permute-start | bytes 442376 | tf_op jit(solution)/shard_map/ppermute | solution.py:138
  19.1 4.3 %collective-permute-start.1 = (bf16[288,256]{1,0:T(8,128)(2,1)S(1)}, bf16[288,256]{1,0:T(8,128)(2,1)S(1)}, u32[]{:S(2)}, u32[]{:S(2)}) collective-permute-start(bf16[288,256]{1,0:T(8,128)(2,1)S(1)} %copy-done), channel_id=1, source_target_pairs={{0,16},{8,24},{16,0},{24,8},{1,17},{9,25},{17,1},{25,9},{2,18},{10... | collective-permute-start | bytes 442376 | tf_op jit(solution)/shard_map/ppermute | solution.py:138
  23.4 3.1 %collective-permute-start.2 = (bf16[288,256]{1,0:T(8,128)(2,1)S(1)}, bf16[288,256]{1,0:T(8,128)(2,1)S(1)}, u32[]{:S(2)}, u32[]{:S(2)}) collective-permute-start(bf16[288,256]{1,0:T(8,128)(2,1)S(1)} %copy-done), channel_id=1, source_target_pairs={{0,24},{8,0},{16,8},{24,16},{1,25},{9,1},{17,9},{25,17},{2,26},{10... | collective-permute-start | bytes 442376 | tf_op jit(solution)/shard_map/ppermute | solution.py:138
  26.5 4.8 %collective-permute-done.1 = bf16[288,256]{1,0:T(8,128)(2,1)S(1)} collective-permute-done((bf16[288,256]{1,0:T(8,128)(2,1)S(1)}, bf16[288,256]{1,0:T(8,128)(2,1)S(1)}, u32[]{:S(2)}, u32[]{:S(2)}) %collective-permute-start.1) | collective-permute-done | bytes 147488 | tf_op jit(solution)/shard_map/ppermute | solution.py:138
  31.3 4.5 %collective-permute-done.2 = bf16[288,256]{1,0:T(8,128)(2,1)S(1)} collective-permute-done((bf16[288,256]{1,0:T(8,128)(2,1)S(1)}, bf16[288,256]{1,0:T(8,128)(2,1)S(1)}, u32[]{:S(2)}, u32[]{:S(2)}) %collective-permute-start.2) | collective-permute-done | bytes 147488 | tf_op jit(solution)/shard_map/ppermute | solution.py:138
  35.9 2.5 %collective-permute-start.3 = (bf16[4,288,256]{2,1,0:T(8,128)(2,1)S(1)}, bf16[4,288,256]{2,1,0:T(8,128)(2,1)S(1)}, u32[]{:S(2)}, u32[]{:S(2)}) collective-permute-start(bf16[4,288,256]{2,1,0:T(8,128)(2,1)S(1)} %pad_maximum_fusion.3), channel_id=1, source_target_pairs={{0,32},{32,0},{1,33},{33,1},{2,34},{34,2},{3,35},{35,3},{4,36},{36... | collective-permute-start | bytes 1769480 | tf_op jit(solution)/shard_map/ppermute | solution.py:28
  38.4 1.6 %collective-permute-done.3 = bf16[4,288,256]{2,1,0:T(8,128)(2,1)S(1)} collective-permute-done((bf16[4,288,256]{2,1,0:T(8,128)(2,1)S(1)}, bf16[4,288,256]{2,1,0:T(8,128)(2,1)S(1)}, u32[]{:S(2)}, u32[]{:S(2)}) %collective-permute-start.3) | collective-permute-done | bytes 589856 | tf_op jit(solution)/shard_map/ppermute | solution.py:28
  40.1 4.4 %all-to-all-done = bf16[32,72,256]{2,1,0:T(8,128)(2,1)S(1)} async-done(((bf16[32,72,256]{2,1,0:T(8,128)(2,1)}), bf16[32,72,256]{2,1,0:T(8,128)(2,1)S(1)}, u32[]{:S(2)}, u32[]{:S(2)}) %all-to-all-start) | async-done | bytes 1179680 | tf_op jit(solution)/shard_map/all_to_all | solution.py:15
  44.6 1.1 shard_map.17
  45.8 23.7 %all_to_all.25 = bf16[8,336,128]{2,1,0:T(8,128)(2,1)S(1)} all-to-all(bf16[8,336,128]{2,1,0:T(8,128)(2,1)S(1)} %shard_map.17), channel_id=1, replica_groups=mesh['z'=8,'core'=2,'x'=4,'y'=8] {'y'}, dimensions={0} | all-to-all | bytes 1376256 | tf_op jit(solution)/shard_map/all_to_all | solution.py:15
  69.7 19.6 %all_to_all.26.chunks = bf16[8,336,128]{2,1,0:T(8,128)(2,1)S(1)} all-to-all(bf16[8,336,128]{2,1,0:T(8,128)(2,1)S(1)} %broadcast_in_dim.10), channel_id=1, replica_groups=mesh['z'=8,'core'=2,'x'=4,'y'=8] {'y'}, dimensions={0} | all-to-all | bytes 1376256 | tf_op jit(solution)/shard_map/all_to_all | solution.py:15
  89.4 0.6 fusion
  90.1 7.3 %collective-permute-start.4 = (bf16[4,288,256]{2,1,0:T(8,128)(2,1)S(1)}, bf16[4,288,256]{2,1,0:T(8,128)(2,1)S(1)}, u32[]{:S(2)}, u32[]{:S(2)}) collective-permute-start(bf16[4,288,256]{2,1,0:T(8,128)(2,1)S(1)} %fusion), channel_id=1, source_target_pairs={{0,32},{32,0},{1,33},{33,1},{2,34},{34,2},{3,35},{35,3},{4,36},{36... | collective-permute-start | bytes 1769480 | tf_op jit(solution)/shard_map/ppermute | solution.py:28
  97.4 0.6 convolution_bitcast_fusion
  98.0 1.0 collective-permute-done.4
  99.1 14.9 %all_to_all.27 = bf16[4,288,256]{2,1,0:T(8,128)(2,1)S(1)} all-to-all(bf16[4,288,256]{2,1,0:T(8,128)(2,1)S(1)} %add_convert_fusion), channel_id=1, replica_groups=mesh['z'=8,'core'=2,'x'=4,'y'=8] {'x'}, dimensions={0} | all-to-all | bytes 1179648 | tf_op jit(solution)/shard_map/all_to_all | solution.py:15
  114.2 1.1 broadcast_in_dim.11
  115.3 3.8 %all-to-all-start.4 = ((bf16[8,4,72,256]{3,2,1,0:T(8,128)(2,1)}), bf16[8,4,72,256]{3,2,1,0:T(8,128)(2,1)S(1)}, u32[]{:S(2)}, u32[]{:S(2)}) async-start(bf16[8,4,72,256]{3,2,1,0:T(8,128)(2,1)} %broadcast_in_dim.11), calls=%async_computation.4 | async-start | bytes 2359296 | tf_op jit(solution)/shard_map/all_to_all | solution.py:15
  119.1 2.2 %collective-permute-start.8 = (bf16[288,576]{1,0:T(8,128)(2,1)S(1)}, bf16[288,576]{1,0:T(8,128)(2,1)S(1)}, u32[]{:S(2)}, u32[]{:S(2)}) collective-permute-start(bf16[288,576]{1,0:T(8,128)(2,1)S(1)} %get-tuple-element.14), channel_id=1, source_target_pairs={{0,8},{8,16},{16,24},{24,0},{1,9},{9,17},{17,25},{25,1},{2,10},{10... | collective-permute-start | bytes 995336 | tf_op jit(solution)/shard_map/ppermute | solution.py:138
  121.3 4.3 %collective-permute-start.6 = (bf16[288,576]{1,0:T(8,128)(2,1)S(1)}, bf16[288,576]{1,0:T(8,128)(2,1)}, u32[]{:S(2)}, u32[]{:S(2)}) collective-permute-start(bf16[288,576]{1,0:T(8,128)(2,1)S(1)} %get-tuple-element.12), channel_id=1, source_target_pairs={{0,24},{8,0},{16,8},{24,16},{1,25},{9,1},{17,9},{25,17},{2,26},{10... | collective-permute-start | bytes 995336 | tf_op jit(solution)/shard_map/ppermute | solution.py:138
  125.6 1.9 %collective-permute-start.10 = (bf16[288,576]{1,0:T(8,128)(2,1)S(1)}, bf16[288,576]{1,0:T(8,128)(2,1)S(1)}, u32[]{:S(2)}, u32[]{:S(2)}) collective-permute-start(bf16[288,576]{1,0:T(8,128)(2,1)S(1)} %get-tuple-element.14), channel_id=1, source_target_pairs={{0,24},{8,0},{16,8},{24,16},{1,25},{9,1},{17,9},{25,17},{2,26},{10... | collective-permute-start | bytes 995336 | tf_op jit(solution)/shard_map/ppermute | solution.py:138
  127.6 2.9 %collective-permute-done.8 = bf16[288,576]{1,0:T(8,128)(2,1)S(1)} collective-permute-done((bf16[288,576]{1,0:T(8,128)(2,1)S(1)}, bf16[288,576]{1,0:T(8,128)(2,1)S(1)}, u32[]{:S(2)}, u32[]{:S(2)}) %collective-permute-start.8) | collective-permute-done | bytes 331808 | tf_op jit(solution)/shard_map/ppermute | solution.py:138
  130.5 1.9 %collective-permute-start.9 = (bf16[288,576]{1,0:T(8,128)(2,1)S(1)}, bf16[288,576]{1,0:T(8,128)(2,1)S(1)}, u32[]{:S(2)}, u32[]{:S(2)}) collective-permute-start(bf16[288,576]{1,0:T(8,128)(2,1)S(1)} %collective-permute-done.8), channel_id=1, source_target_pairs={{0,8},{8,16},{16,24},{24,0},{1,9},{9,17},{17,25},{25,1},{2,10},{10... | collective-permute-start | bytes 995336 | tf_op jit(solution)/shard_map/ppermute | solution.py:138
  132.4 1.9 %collective-permute-start.5 = (bf16[288,576]{1,0:T(8,128)(2,1)S(1)}, bf16[288,576]{1,0:T(8,128)(2,1)}, u32[]{:S(2)}, u32[]{:S(2)}) collective-permute-start(bf16[288,576]{1,0:T(8,128)(2,1)S(1)} %get-tuple-element.12), channel_id=1, source_target_pairs={{0,8},{8,16},{16,24},{24,0},{1,9},{9,17},{17,25},{25,1},{2,10},{10... | collective-permute-start | bytes 995336 | tf_op jit(solution)/shard_map/ppermute | solution.py:138
  134.4 4.6 %collective-permute-start.7 = (bf16[288,576]{1,0:T(8,128)(2,1)}, bf16[288,576]{1,0:T(8,128)(2,1)}, u32[]{:S(2)}, u32[]{:S(2)}) collective-permute-start(bf16[288,576]{1,0:T(8,128)(2,1)} %collective-permute-done.6), channel_id=1, source_target_pairs={{0,24},{8,0},{16,8},{24,16},{1,25},{9,1},{17,9},{25,17},{2,26},{10... | collective-permute-start | bytes 995336 | tf_op jit(solution)/shard_map/ppermute | solution.py:138
  139.3 1.6 %collective-permute-done.9 = bf16[288,576]{1,0:T(8,128)(2,1)S(1)} collective-permute-done((bf16[288,576]{1,0:T(8,128)(2,1)S(1)}, bf16[288,576]{1,0:T(8,128)(2,1)S(1)}, u32[]{:S(2)}, u32[]{:S(2)}) %collective-permute-start.9) | collective-permute-done | bytes 331808 | tf_op jit(solution)/shard_map/ppermute | solution.py:138
  141.3 9.9 %all-to-all-done.4 = bf16[8,4,72,256]{3,2,1,0:T(8,128)(2,1)S(1)} async-done(((bf16[8,4,72,256]{3,2,1,0:T(8,128)(2,1)}), bf16[8,4,72,256]{3,2,1,0:T(8,128)(2,1)S(1)}, u32[]{:S(2)}, u32[]{:S(2)}) %all-to-all-start.4) | async-done | bytes 1179680 | tf_op jit(solution)/shard_map/all_to_all | solution.py:15
  151.8 2.4 %collective-permute-start.11 = (f32[288,256]{1,0:T(8,128)S(1)}, f32[288,256]{1,0:T(8,128)S(1)}, u32[]{:S(2)}, u32[]{:S(2)}) collective-permute-start(f32[288,256]{1,0:T(8,128)S(1)} %shard_map.20), channel_id=1, source_target_pairs={{0,32},{32,0},{1,33},{33,1},{2,34},{34,2},{3,35},{35,3},{4,36},{36... | collective-permute-start | bytes 884744 | tf_op jit(solution)/shard_map/ppermute | solution.py:28
  154.3 1.5 pad_maximum_fusion.blocks
  156.4 0.7 fusion.5
  (21 shorter events, 2.9 us)
Async XLA Ops:
  2.0 13.9 %copy-start = (bf16[288,256]{1,0:T(8,128)(2,1)S(1)}, bf16[288,256]{1,0:T(8,128)(2,1)}, u32[]{:S(2)}) copy-start(bf16[288,256]{1,0:T(8,128)(2,1)} %param.1) | copy-start | bytes 442372
  2.0 42.5 %all-to-all-start = ((bf16[32,72,256]{2,1,0:T(8,128)(2,1)}), bf16[32,72,256]{2,1,0:T(8,128)(2,1)S(1)}, u32[]{:S(2)}, u32[]{:S(2)}) async-start(bf16[32,72,256]{2,1,0:T(8,128)(2,1)} %bitcast.5), calls=%async_computation | async-start | bytes 2359296 | tf_op jit(solution)/shard_map/all_to_all | solution.py:15
  15.9 10.6 %collective-permute-start = (bf16[288,256]{1,0:T(8,128)(2,1)S(1)}, bf16[288,256]{1,0:T(8,128)(2,1)S(1)}, u32[]{:S(2)}, u32[]{:S(2)}) collective-permute-start(bf16[288,256]{1,0:T(8,128)(2,1)S(1)} %copy-done), channel_id=1, source_target_pairs={{0,8},{8,16},{16,24},{24,0},{1,9},{9,17},{17,25},{25,1},{2,10},{10... | collective-permute-start | bytes 442376 | tf_op jit(solution)/shard_map/ppermute | solution.py:138
  19.1 12.2 %collective-permute-start.1 = (bf16[288,256]{1,0:T(8,128)(2,1)S(1)}, bf16[288,256]{1,0:T(8,128)(2,1)S(1)}, u32[]{:S(2)}, u32[]{:S(2)}) collective-permute-start(bf16[288,256]{1,0:T(8,128)(2,1)S(1)} %copy-done), channel_id=1, source_target_pairs={{0,16},{8,24},{16,0},{24,8},{1,17},{9,25},{17,1},{25,9},{2,18},{10... | collective-permute-start | bytes 442376 | tf_op jit(solution)/shard_map/ppermute | solution.py:138
  23.4 12.4 %collective-permute-start.2 = (bf16[288,256]{1,0:T(8,128)(2,1)S(1)}, bf16[288,256]{1,0:T(8,128)(2,1)S(1)}, u32[]{:S(2)}, u32[]{:S(2)}) collective-permute-start(bf16[288,256]{1,0:T(8,128)(2,1)S(1)} %copy-done), channel_id=1, source_target_pairs={{0,24},{8,0},{16,8},{24,16},{1,25},{9,1},{17,9},{25,17},{2,26},{10... | collective-permute-start | bytes 442376 | tf_op jit(solution)/shard_map/ppermute | solution.py:138
  35.9 4.1 %collective-permute-start.3 = (bf16[4,288,256]{2,1,0:T(8,128)(2,1)S(1)}, bf16[4,288,256]{2,1,0:T(8,128)(2,1)S(1)}, u32[]{:S(2)}, u32[]{:S(2)}) collective-permute-start(bf16[4,288,256]{2,1,0:T(8,128)(2,1)S(1)} %pad_maximum_fusion.3), channel_id=1, source_target_pairs={{0,32},{32,0},{1,33},{33,1},{2,34},{34,2},{3,35},{35,3},{4,36},{36... | collective-permute-start | bytes 1769480 | tf_op jit(solution)/shard_map/ppermute | solution.py:28
  90.1 8.9 %collective-permute-start.4 = (bf16[4,288,256]{2,1,0:T(8,128)(2,1)S(1)}, bf16[4,288,256]{2,1,0:T(8,128)(2,1)S(1)}, u32[]{:S(2)}, u32[]{:S(2)}) collective-permute-start(bf16[4,288,256]{2,1,0:T(8,128)(2,1)S(1)} %fusion), channel_id=1, source_target_pairs={{0,32},{32,0},{1,33},{33,1},{2,34},{34,2},{3,35},{35,3},{4,36},{36... | collective-permute-start | bytes 1769480 | tf_op jit(solution)/shard_map/ppermute | solution.py:28
  115.3 35.8 %all-to-all-start.4 = ((bf16[8,4,72,256]{3,2,1,0:T(8,128)(2,1)}), bf16[8,4,72,256]{3,2,1,0:T(8,128)(2,1)S(1)}, u32[]{:S(2)}, u32[]{:S(2)}) async-start(bf16[8,4,72,256]{3,2,1,0:T(8,128)(2,1)} %broadcast_in_dim.11), calls=%async_computation.4 | async-start | bytes 2359296 | tf_op jit(solution)/shard_map/all_to_all | solution.py:15
  119.1 11.4 %collective-permute-start.8 = (bf16[288,576]{1,0:T(8,128)(2,1)S(1)}, bf16[288,576]{1,0:T(8,128)(2,1)S(1)}, u32[]{:S(2)}, u32[]{:S(2)}) collective-permute-start(bf16[288,576]{1,0:T(8,128)(2,1)S(1)} %get-tuple-element.14), channel_id=1, source_target_pairs={{0,8},{8,16},{16,24},{24,0},{1,9},{9,17},{17,25},{25,1},{2,10},{10... | collective-permute-start | bytes 995336 | tf_op jit(solution)/shard_map/ppermute | solution.py:138
  121.3 13.0 %collective-permute-start.6 = (bf16[288,576]{1,0:T(8,128)(2,1)S(1)}, bf16[288,576]{1,0:T(8,128)(2,1)}, u32[]{:S(2)}, u32[]{:S(2)}) collective-permute-start(bf16[288,576]{1,0:T(8,128)(2,1)S(1)} %get-tuple-element.12), channel_id=1, source_target_pairs={{0,24},{8,0},{16,8},{24,16},{1,25},{9,1},{17,9},{25,17},{2,26},{10... | collective-permute-start | bytes 995336 | tf_op jit(solution)/shard_map/ppermute | solution.py:138
  125.6 13.7 %collective-permute-start.10 = (bf16[288,576]{1,0:T(8,128)(2,1)S(1)}, bf16[288,576]{1,0:T(8,128)(2,1)S(1)}, u32[]{:S(2)}, u32[]{:S(2)}) collective-permute-start(bf16[288,576]{1,0:T(8,128)(2,1)S(1)} %get-tuple-element.14), channel_id=1, source_target_pairs={{0,24},{8,0},{16,8},{24,16},{1,25},{9,1},{17,9},{25,17},{2,26},{10... | collective-permute-start | bytes 995336 | tf_op jit(solution)/shard_map/ppermute | solution.py:138
  130.5 10.4 %collective-permute-start.9 = (bf16[288,576]{1,0:T(8,128)(2,1)S(1)}, bf16[288,576]{1,0:T(8,128)(2,1)S(1)}, u32[]{:S(2)}, u32[]{:S(2)}) collective-permute-start(bf16[288,576]{1,0:T(8,128)(2,1)S(1)} %collective-permute-done.8), channel_id=1, source_target_pairs={{0,8},{8,16},{16,24},{24,0},{1,9},{9,17},{17,25},{25,1},{2,10},{10... | collective-permute-start | bytes 995336 | tf_op jit(solution)/shard_map/ppermute | solution.py:138
  132.4 21.8 %collective-permute-start.5 = (bf16[288,576]{1,0:T(8,128)(2,1)S(1)}, bf16[288,576]{1,0:T(8,128)(2,1)}, u32[]{:S(2)}, u32[]{:S(2)}) collective-permute-start(bf16[288,576]{1,0:T(8,128)(2,1)S(1)} %get-tuple-element.12), channel_id=1, source_target_pairs={{0,8},{8,16},{16,24},{24,0},{1,9},{9,17},{17,25},{25,1},{2,10},{10... | collective-permute-start | bytes 995336 | tf_op jit(solution)/shard_map/ppermute | solution.py:138
  134.4 19.9 %collective-permute-start.7 = (bf16[288,576]{1,0:T(8,128)(2,1)}, bf16[288,576]{1,0:T(8,128)(2,1)}, u32[]{:S(2)}, u32[]{:S(2)}) collective-permute-start(bf16[288,576]{1,0:T(8,128)(2,1)} %collective-permute-done.6), channel_id=1, source_target_pairs={{0,24},{8,0},{16,8},{24,16},{1,25},{9,1},{17,9},{25,17},{2,26},{10... | collective-permute-start | bytes 995336 | tf_op jit(solution)/shard_map/ppermute | solution.py:138
  151.8 4.6 %collective-permute-start.11 = (f32[288,256]{1,0:T(8,128)S(1)}, f32[288,256]{1,0:T(8,128)S(1)}, u32[]{:S(2)}, u32[]{:S(2)}) collective-permute-start(f32[288,256]{1,0:T(8,128)S(1)} %shard_map.20), channel_id=1, source_target_pairs={{0,32},{32,0},{1,33},{33,1},{2,34},{34,2},{3,35},{35,3},{4,36},{36... | collective-permute-start | bytes 884744 | tf_op jit(solution)/shard_map/ppermute | solution.py:28

commit v10 on v9

--- a/solution.py
+++ b/solution.py
@@ -33,30 +33,32 @@
     return blocks.swapaxes(0, 1).reshape(nx, n * rows, cols)
 
 
-def product_kernel(blocks, right, out):
+def product_kernel(right, *refs):
+    *stacks, out = refs
     nx = right.shape[0]
     here = lax.axis_index("x")
+    blocks = [stacks[0].at[hop] for hop in range(nx)] if len(stacks) == 1 else stacks
     out[...] = sum(
-        jnp.dot(blocks[hop], right[lax.rem(here + (nx - hop), nx)], preferred_element_type=F32)
-        for hop in range(nx)
+        jnp.dot(block[...], right[lax.rem(here + (nx - hop), nx)], preferred_element_type=F32)
+        for hop, block in enumerate(blocks)
     )
 
 
-def product(blocks, right):
-    _, rows, _ = blocks.shape
-    cols = right.shape[2]
+def product(stacks, right):
+    rows, cols = stacks[0].shape[-2], right.shape[2]
+    size = sum(stack.size for stack in stacks)
     return pl.pallas_call(
         product_kernel,
         out_shape=jax.ShapeDtypeStruct((rows, cols), F32),
-        in_specs=[pl.BlockSpec(memory_space=pltpu.VMEM)] * 2,
+        in_specs=[pl.BlockSpec(memory_space=pltpu.VMEM)] * (1 + len(stacks)),
         out_specs=pl.BlockSpec(memory_space=pltpu.VMEM),
         compiler_params=pltpu.CompilerParams(vmem_limit_bytes=16 << 20),
         cost_estimate=pl.CostEstimate(
-            flops=2 * blocks.size * cols,
-            bytes_accessed=2 * right.size + 2 * blocks.size + 4 * rows * cols,
+            flops=2 * size * cols,
+            bytes_accessed=2 * right.size + 2 * size + 4 * rows * cols,
             transcendentals=0,
         ),
-    )(blocks, right)
+    )(right, *stacks)
 
 
 LANES = 128
@@ -163,9 +165,8 @@
     above_bottom, below_top = shift_x(bottom, -1), shift_x(top, 1)
     far_top, far_bottom = shift_x(above_top, -1), shift_x(below_bottom, 1)
     bottoms = jnp.stack([bottom, below_bottom, far_bottom, above_bottom])
-    other = swap_cores(product(bottoms, right))
-    tops = jnp.stack([top, below_top, far_top, above_top])
-    second = product(tops, right) + other
+    other = swap_cores(product((bottoms,), right))
+    second = product((top, below_top, far_top, above_top), right) + other
     scale = math.sqrt(COLS)
     return (scale * (3.4445 * own.astype(F32) + second)).astype(BF16)
 

time: 158 us -> 159 us (level)
  starting transfers between devices: 57.2 us -> 59.8 us
  waiting for transfers between devices: 31.1 us -> 29.5 us
    all_to_all x2, waiting for transfers between devices: 14.3 us -> 11.2 us  [exchange(): return lax.all_to_all(chunks, axis, 0, 0)]
    ppermute x3, starting transfers between devices: 12.2 us -> 14.4 us  [swap_cores(): return lax.ppermute(block, 'core', [(0, 1), (1, 0)])]
  transfers between devices with their start and end apart: 14 -> 14, of which waited for: 9 -> 10; matrix products, arithmetic and copies ran while one was open for 2% -> 2% of each run, Pallas kernels for 1% -> 1%
where the time goes in v10:
time: 159 us; the launch traced here: 158 us
  starting transfers between devices  59.8 us (38%)
  blocking collectives  58.3 us (37%)
  waiting for transfers between devices  29.5 us (19%)
  local copies, waits for them, and re-layouts  4.65 us (3%)
  Pallas kernels  2.5 us (2%)
  other arithmetic  1.61 us (1%)
    all_to_all x3, blocking collectives, exchange(): return lax.all_to_all(chunks, axis, 0, 0)  58.3 us
    ppermute x9, starting transfers between devices, shift_x(): return lax.ppermute(block, 'x', [(i, (i + hop) % nx) for i in range(nx)])  27.3 us
    all_to_all x2, starting transfers between devices, exchange(): return lax.all_to_all(chunks, axis, 0, 0)  18.1 us
    ppermute x9, waiting for transfers between devices, shift_x(): return lax.ppermute(block, 'x', [(i, (i + hop) % nx) for i in range(nx)])  15.1 us
    ppermute x3, starting transfers between devices, swap_cores(): return lax.ppermute(block, 'core', [(0, 1), (1, 0)])  14.4 us
    all_to_all x2, waiting for transfers between devices, exchange(): return lax.all_to_all(chunks, axis, 0, 0)  11.2 us
  transfers between devices with their start and end apart: 14, of which 10 were waited for; matrix products, arithmetic and copies ran while one was open for 2% of the time, Pallas kernels for 1%

profile of v10, /device:TPU:1, one launch (start us, length us, event | category | flops | bytes accessed | tf_op | source)
XLA Modules:
  0.0 157.8 jit_solution(11013006585494970641)
XLA Ops:
  0.0 2.0 %broadcast_in_dim.9 = bf16[8,4,72,256]{3,2,1,0:T(8,128)(2,1)} broadcast(bf16[4,72,256]{2,1,0:T(8,128)(2,1)} %bitcast.44), dimensions={1,2,3} | broadcast | bytes 1327104 | tf_op jit(solution)/shard_map/broadcast_in_dim | solution.py:142
  2.0 13.8 %all-to-all-start = ((bf16[32,72,256]{2,1,0:T(8,128)(2,1)}), bf16[32,72,256]{2,1,0:T(8,128)(2,1)S(1)}, u32[]{:S(2)}, u32[]{:S(2)}) async-start(bf16[32,72,256]{2,1,0:T(8,128)(2,1)} %bitcast.5), calls=%async_computation | async-start | bytes 2359296 | tf_op jit(solution)/shard_map/all_to_all | solution.py:15
  15.9 3.1 %collective-permute-start = (bf16[288,256]{1,0:T(8,128)(2,1)S(1)}, bf16[288,256]{1,0:T(8,128)(2,1)S(1)}, u32[]{:S(2)}, u32[]{:S(2)}) collective-permute-start(bf16[288,256]{1,0:T(8,128)(2,1)S(1)} %copy-done), channel_id=1, source_target_pairs={{0,8},{8,16},{16,24},{24,0},{1,9},{9,17},{17,25},{25,1},{2,10},{10... | collective-permute-start | bytes 442376 | tf_op jit(solution)/shard_map/ppermute | solution.py:140
  19.1 4.3 %collective-permute-start.1 = (bf16[288,256]{1,0:T(8,128)(2,1)S(1)}, bf16[288,256]{1,0:T(8,128)(2,1)S(1)}, u32[]{:S(2)}, u32[]{:S(2)}) collective-permute-start(bf16[288,256]{1,0:T(8,128)(2,1)S(1)} %copy-done), channel_id=1, source_target_pairs={{0,16},{8,24},{16,0},{24,8},{1,17},{9,25},{17,1},{25,9},{2,18},{10... | collective-permute-start | bytes 442376 | tf_op jit(solution)/shard_map/ppermute | solution.py:140
  23.4 3.1 %collective-permute-start.2 = (bf16[288,256]{1,0:T(8,128)(2,1)S(1)}, bf16[288,256]{1,0:T(8,128)(2,1)S(1)}, u32[]{:S(2)}, u32[]{:S(2)}) collective-permute-start(bf16[288,256]{1,0:T(8,128)(2,1)S(1)} %copy-done), channel_id=1, source_target_pairs={{0,24},{8,0},{16,8},{24,16},{1,25},{9,1},{17,9},{25,17},{2,26},{10... | collective-permute-start | bytes 442376 | tf_op jit(solution)/shard_map/ppermute | solution.py:140
  26.5 4.8 %collective-permute-done.1 = bf16[288,256]{1,0:T(8,128)(2,1)S(1)} collective-permute-done((bf16[288,256]{1,0:T(8,128)(2,1)S(1)}, bf16[288,256]{1,0:T(8,128)(2,1)S(1)}, u32[]{:S(2)}, u32[]{:S(2)}) %collective-permute-start.1) | collective-permute-done | bytes 147488 | tf_op jit(solution)/shard_map/ppermute | solution.py:140
  31.3 4.5 %collective-permute-done.2 = bf16[288,256]{1,0:T(8,128)(2,1)S(1)} collective-permute-done((bf16[288,256]{1,0:T(8,128)(2,1)S(1)}, bf16[288,256]{1,0:T(8,128)(2,1)S(1)}, u32[]{:S(2)}, u32[]{:S(2)}) %collective-permute-start.2) | collective-permute-done | bytes 147488 | tf_op jit(solution)/shard_map/ppermute | solution.py:140
  35.9 2.5 %collective-permute-start.3 = (bf16[4,288,256]{2,1,0:T(8,128)(2,1)S(1)}, bf16[4,288,256]{2,1,0:T(8,128)(2,1)S(1)}, u32[]{:S(2)}, u32[]{:S(2)}) collective-permute-start(bf16[4,288,256]{2,1,0:T(8,128)(2,1)S(1)} %pad_maximum_fusion.2), channel_id=1, source_target_pairs={{0,32},{32,0},{1,33},{33,1},{2,34},{34,2},{3,35},{35,3},{4,36},{36... | collective-permute-start | bytes 1769480 | tf_op jit(solution)/shard_map/ppermute | solution.py:28
  38.4 1.6 %collective-permute-done.3 = bf16[4,288,256]{2,1,0:T(8,128)(2,1)S(1)} collective-permute-done((bf16[4,288,256]{2,1,0:T(8,128)(2,1)S(1)}, bf16[4,288,256]{2,1,0:T(8,128)(2,1)S(1)}, u32[]{:S(2)}, u32[]{:S(2)}) %collective-permute-start.3) | collective-permute-done | bytes 589856 | tf_op jit(solution)/shard_map/ppermute | solution.py:28
  40.1 4.4 %all-to-all-done = bf16[32,72,256]{2,1,0:T(8,128)(2,1)S(1)} async-done(((bf16[32,72,256]{2,1,0:T(8,128)(2,1)}), bf16[32,72,256]{2,1,0:T(8,128)(2,1)S(1)}, u32[]{:S(2)}, u32[]{:S(2)}) %all-to-all-start) | async-done | bytes 1179680 | tf_op jit(solution)/shard_map/all_to_all | solution.py:15
  44.6 1.1 shard_map.17
  45.8 23.7 %all_to_all.25 = bf16[8,336,128]{2,1,0:T(8,128)(2,1)S(1)} all-to-all(bf16[8,336,128]{2,1,0:T(8,128)(2,1)S(1)} %shard_map.17), channel_id=1, replica_groups=mesh['z'=8,'core'=2,'x'=4,'y'=8] {'y'}, dimensions={0} | all-to-all | bytes 1376256 | tf_op jit(solution)/shard_map/all_to_all | solution.py:15
  69.7 19.6 %all_to_all.26.chunks = bf16[8,336,128]{2,1,0:T(8,128)(2,1)S(1)} all-to-all(bf16[8,336,128]{2,1,0:T(8,128)(2,1)S(1)} %broadcast_in_dim.10), channel_id=1, replica_groups=mesh['z'=8,'core'=2,'x'=4,'y'=8] {'y'}, dimensions={0} | all-to-all | bytes 1376256 | tf_op jit(solution)/shard_map/all_to_all | solution.py:15
  89.4 0.6 fusion
  90.1 7.3 %collective-permute-start.4 = (bf16[4,288,256]{2,1,0:T(8,128)(2,1)S(1)}, bf16[4,288,256]{2,1,0:T(8,128)(2,1)S(1)}, u32[]{:S(2)}, u32[]{:S(2)}) collective-permute-start(bf16[4,288,256]{2,1,0:T(8,128)(2,1)S(1)} %fusion), channel_id=1, source_target_pairs={{0,32},{32,0},{1,33},{33,1},{2,34},{34,2},{3,35},{35,3},{4,36},{36... | collective-permute-start | bytes 1769480 | tf_op jit(solution)/shard_map/ppermute | solution.py:28
  97.4 0.6 convolution_bitcast_fusion
  98.0 1.0 collective-permute-done.4
  99.1 14.9 %all_to_all.27 = bf16[4,288,256]{2,1,0:T(8,128)(2,1)S(1)} all-to-all(bf16[4,288,256]{2,1,0:T(8,128)(2,1)S(1)} %add_convert_fusion), channel_id=1, replica_groups=mesh['z'=8,'core'=2,'x'=4,'y'=8] {'x'}, dimensions={0} | all-to-all | bytes 1179648 | tf_op jit(solution)/shard_map/all_to_all | solution.py:15
  114.2 1.1 broadcast_in_dim.11
  115.3 4.3 %all-to-all-start.4 = ((bf16[8,4,72,256]{3,2,1,0:T(8,128)(2,1)}), bf16[8,4,72,256]{3,2,1,0:T(8,128)(2,1)}, u32[]{:S(2)}, u32[]{:S(2)}) async-start(bf16[8,4,72,256]{3,2,1,0:T(8,128)(2,1)} %broadcast_in_dim.11), calls=%async_computation.4 | async-start | bytes 2359296 | tf_op jit(solution)/shard_map/all_to_all | solution.py:15
  119.5 2.2 %collective-permute-start.8 = (bf16[288,576]{1,0:T(8,128)(2,1)S(1)}, bf16[288,576]{1,0:T(8,128)(2,1)S(1)}, u32[]{:S(2)}, u32[]{:S(2)}) collective-permute-start(bf16[288,576]{1,0:T(8,128)(2,1)S(1)} %get-tuple-element.14), channel_id=1, source_target_pairs={{0,8},{8,16},{16,24},{24,0},{1,9},{9,17},{17,25},{25,1},{2,10},{10... | collective-permute-start | bytes 995336 | tf_op jit(solution)/shard_map/ppermute | solution.py:140
  121.8 4.3 %collective-permute-start.6 = (bf16[288,576]{1,0:T(8,128)(2,1)S(1)}, bf16[288,576]{1,0:T(8,128)(2,1)S(1)}, u32[]{:S(2)}, u32[]{:S(2)}) collective-permute-start(bf16[288,576]{1,0:T(8,128)(2,1)S(1)} %get-tuple-element.13.refs_0_), channel_id=1, source_target_pairs={{0,24},{8,0},{16,8},{24,16},{1,25},{9,1},{17,9},{25,17},{2,26},{10... | collective-permute-start | bytes 995336 | tf_op jit(solution)/shard_map/ppermute | solution.py:140
  126.1 1.9 %collective-permute-start.10 = (bf16[288,576]{1,0:T(8,128)(2,1)S(1)}, bf16[288,576]{1,0:T(8,128)(2,1)S(1)}, u32[]{:S(2)}, u32[]{:S(2)}) collective-permute-start(bf16[288,576]{1,0:T(8,128)(2,1)S(1)} %get-tuple-element.14), channel_id=1, source_target_pairs={{0,24},{8,0},{16,8},{24,16},{1,25},{9,1},{17,9},{25,17},{2,26},{10... | collective-permute-start | bytes 995336 | tf_op jit(solution)/shard_map/ppermute | solution.py:140
  128.0 3.3 %collective-permute-done.8 = bf16[288,576]{1,0:T(8,128)(2,1)S(1)} collective-permute-done((bf16[288,576]{1,0:T(8,128)(2,1)S(1)}, bf16[288,576]{1,0:T(8,128)(2,1)S(1)}, u32[]{:S(2)}, u32[]{:S(2)}) %collective-permute-start.8) | collective-permute-done | bytes 331808 | tf_op jit(solution)/shard_map/ppermute | solution.py:140
  131.3 1.9 %collective-permute-start.9 = (bf16[288,576]{1,0:T(8,128)(2,1)S(1)}, bf16[288,576]{1,0:T(8,128)(2,1)S(1)}, u32[]{:S(2)}, u32[]{:S(2)}) collective-permute-start(bf16[288,576]{1,0:T(8,128)(2,1)S(1)} %collective-permute-done.8), channel_id=1, source_target_pairs={{0,8},{8,16},{16,24},{24,0},{1,9},{9,17},{17,25},{25,1},{2,10},{10... | collective-permute-start | bytes 995336 | tf_op jit(solution)/shard_map/ppermute | solution.py:140
  133.2 1.9 %collective-permute-start.5 = (bf16[288,576]{1,0:T(8,128)(2,1)S(1)}, bf16[288,576]{1,0:T(8,128)(2,1)S(1)}, u32[]{:S(2)}, u32[]{:S(2)}) collective-permute-start(bf16[288,576]{1,0:T(8,128)(2,1)S(1)} %get-tuple-element.13.refs_0_), channel_id=1, source_target_pairs={{0,8},{8,16},{16,24},{24,0},{1,9},{9,17},{17,25},{25,1},{2,10},{10... | collective-permute-start | bytes 995336 | tf_op jit(solution)/shard_map/ppermute | solution.py:140
  135.2 4.6 %collective-permute-start.7 = (bf16[288,576]{1,0:T(8,128)(2,1)S(1)}, bf16[288,576]{1,0:T(8,128)(2,1)S(1)}, u32[]{:S(2)}, u32[]{:S(2)}) collective-permute-start(bf16[288,576]{1,0:T(8,128)(2,1)S(1)} %collective-permute-done.6.refs_3_), channel_id=1, source_target_pairs={{0,24},{8,0},{16,8},{24,16},{1,25},{9,1},{17,9},{25,17},{2,26},{10... | collective-permute-start | bytes 995336 | tf_op jit(solution)/shard_map/ppermute | solution.py:140
  140.0 2.2 %collective-permute-done.9 = bf16[288,576]{1,0:T(8,128)(2,1)S(1)} collective-permute-done((bf16[288,576]{1,0:T(8,128)(2,1)S(1)}, bf16[288,576]{1,0:T(8,128)(2,1)S(1)}, u32[]{:S(2)}, u32[]{:S(2)}) %collective-permute-start.9) | collective-permute-done | bytes 331808 | tf_op jit(solution)/shard_map/ppermute | solution.py:140
  142.6 6.8 %all-to-all-done.4 = bf16[8,4,72,256]{3,2,1,0:T(8,128)(2,1)} async-done(((bf16[8,4,72,256]{3,2,1,0:T(8,128)(2,1)}), bf16[8,4,72,256]{3,2,1,0:T(8,128)(2,1)}, u32[]{:S(2)}, u32[]{:S(2)}) %all-to-all-start.4) | async-done | bytes 1179680 | tf_op jit(solution)/shard_map/all_to_all | solution.py:15
  149.4 1.3 copy.4
  151.4 4.6 %collective-permute-start.11 = (f32[288,256]{1,0:T(8,128)S(1)}, f32[288,256]{1,0:T(8,128)S(1)}, u32[]{:S(2)}, u32[]{:S(2)}) collective-permute-start(f32[288,256]{1,0:T(8,128)S(1)} %shard_map.20), channel_id=1, source_target_pairs={{0,32},{32,0},{1,33},{33,1},{2,34},{34,2},{3,35},{35,3},{4,36},{36... | collective-permute-start | bytes 884744 | tf_op jit(solution)/shard_map/ppermute | solution.py:28
  157.1 0.7 fusion.5
  (20 shorter events, 3.2 us)
Async XLA Ops:
  2.0 13.9 %copy-start = (bf16[288,256]{1,0:T(8,128)(2,1)S(1)}, bf16[288,256]{1,0:T(8,128)(2,1)}, u32[]{:S(2)}) copy-start(bf16[288,256]{1,0:T(8,128)(2,1)} %param.1) | copy-start | bytes 442372
  2.0 42.5 %all-to-all-start = ((bf16[32,72,256]{2,1,0:T(8,128)(2,1)}), bf16[32,72,256]{2,1,0:T(8,128)(2,1)S(1)}, u32[]{:S(2)}, u32[]{:S(2)}) async-start(bf16[32,72,256]{2,1,0:T(8,128)(2,1)} %bitcast.5), calls=%async_computation | async-start | bytes 2359296 | tf_op jit(solution)/shard_map/all_to_all | solution.py:15
  15.9 10.6 %collective-permute-start = (bf16[288,256]{1,0:T(8,128)(2,1)S(1)}, bf16[288,256]{1,0:T(8,128)(2,1)S(1)}, u32[]{:S(2)}, u32[]{:S(2)}) collective-permute-start(bf16[288,256]{1,0:T(8,128)(2,1)S(1)} %copy-done), channel_id=1, source_target_pairs={{0,8},{8,16},{16,24},{24,0},{1,9},{9,17},{17,25},{25,1},{2,10},{10... | collective-permute-start | bytes 442376 | tf_op jit(solution)/shard_map/ppermute | solution.py:140
  19.1 12.2 %collective-permute-start.1 = (bf16[288,256]{1,0:T(8,128)(2,1)S(1)}, bf16[288,256]{1,0:T(8,128)(2,1)S(1)}, u32[]{:S(2)}, u32[]{:S(2)}) collective-permute-start(bf16[288,256]{1,0:T(8,128)(2,1)S(1)} %copy-done), channel_id=1, source_target_pairs={{0,16},{8,24},{16,0},{24,8},{1,17},{9,25},{17,1},{25,9},{2,18},{10... | collective-permute-start | bytes 442376 | tf_op jit(solution)/shard_map/ppermute | solution.py:140
  23.4 12.4 %collective-permute-start.2 = (bf16[288,256]{1,0:T(8,128)(2,1)S(1)}, bf16[288,256]{1,0:T(8,128)(2,1)S(1)}, u32[]{:S(2)}, u32[]{:S(2)}) collective-permute-start(bf16[288,256]{1,0:T(8,128)(2,1)S(1)} %copy-done), channel_id=1, source_target_pairs={{0,24},{8,0},{16,8},{24,16},{1,25},{9,1},{17,9},{25,17},{2,26},{10... | collective-permute-start | bytes 442376 | tf_op jit(solution)/shard_map/ppermute | solution.py:140
  35.9 4.1 %collective-permute-start.3 = (bf16[4,288,256]{2,1,0:T(8,128)(2,1)S(1)}, bf16[4,288,256]{2,1,0:T(8,128)(2,1)S(1)}, u32[]{:S(2)}, u32[]{:S(2)}) collective-permute-start(bf16[4,288,256]{2,1,0:T(8,128)(2,1)S(1)} %pad_maximum_fusion.2), channel_id=1, source_target_pairs={{0,32},{32,0},{1,33},{33,1},{2,34},{34,2},{3,35},{35,3},{4,36},{36... | collective-permute-start | bytes 1769480 | tf_op jit(solution)/shard_map/ppermute | solution.py:28
  90.1 8.9 %collective-permute-start.4 = (bf16[4,288,256]{2,1,0:T(8,128)(2,1)S(1)}, bf16[4,288,256]{2,1,0:T(8,128)(2,1)S(1)}, u32[]{:S(2)}, u32[]{:S(2)}) collective-permute-start(bf16[4,288,256]{2,1,0:T(8,128)(2,1)S(1)} %fusion), channel_id=1, source_target_pairs={{0,32},{32,0},{1,33},{33,1},{2,34},{34,2},{3,35},{35,3},{4,36},{36... | collective-permute-start | bytes 1769480 | tf_op jit(solution)/shard_map/ppermute | solution.py:28
  115.3 34.1 %all-to-all-start.4 = ((bf16[8,4,72,256]{3,2,1,0:T(8,128)(2,1)}), bf16[8,4,72,256]{3,2,1,0:T(8,128)(2,1)}, u32[]{:S(2)}, u32[]{:S(2)}) async-start(bf16[8,4,72,256]{3,2,1,0:T(8,128)(2,1)} %broadcast_in_dim.11), calls=%async_computation.4 | async-start | bytes 2359296 | tf_op jit(solution)/shard_map/all_to_all | solution.py:15
  119.5 11.8 %collective-permute-start.8 = (bf16[288,576]{1,0:T(8,128)(2,1)S(1)}, bf16[288,576]{1,0:T(8,128)(2,1)S(1)}, u32[]{:S(2)}, u32[]{:S(2)}) collective-permute-start(bf16[288,576]{1,0:T(8,128)(2,1)S(1)} %get-tuple-element.14), channel_id=1, source_target_pairs={{0,8},{8,16},{16,24},{24,0},{1,9},{9,17},{17,25},{25,1},{2,10},{10... | collective-permute-start | bytes 995336 | tf_op jit(solution)/shard_map/ppermute | solution.py:140
  121.8 13.4 %collective-permute-start.6 = (bf16[288,576]{1,0:T(8,128)(2,1)S(1)}, bf16[288,576]{1,0:T(8,128)(2,1)S(1)}, u32[]{:S(2)}, u32[]{:S(2)}) collective-permute-start(bf16[288,576]{1,0:T(8,128)(2,1)S(1)} %get-tuple-element.13.refs_0_), channel_id=1, source_target_pairs={{0,24},{8,0},{16,8},{24,16},{1,25},{9,1},{17,9},{25,17},{2,26},{10... | collective-permute-start | bytes 995336 | tf_op jit(solution)/shard_map/ppermute | solution.py:140
  126.1 14.0 %collective-permute-start.10 = (bf16[288,576]{1,0:T(8,128)(2,1)S(1)}, bf16[288,576]{1,0:T(8,128)(2,1)S(1)}, u32[]{:S(2)}, u32[]{:S(2)}) collective-permute-start(bf16[288,576]{1,0:T(8,128)(2,1)S(1)} %get-tuple-element.14), channel_id=1, source_target_pairs={{0,24},{8,0},{16,8},{24,16},{1,25},{9,1},{17,9},{25,17},{2,26},{10... | collective-permute-start | bytes 995336 | tf_op jit(solution)/shard_map/ppermute | solution.py:140
  131.3 10.9 %collective-permute-start.9 = (bf16[288,576]{1,0:T(8,128)(2,1)S(1)}, bf16[288,576]{1,0:T(8,128)(2,1)S(1)}, u32[]{:S(2)}, u32[]{:S(2)}) collective-permute-start(bf16[288,576]{1,0:T(8,128)(2,1)S(1)} %collective-permute-done.8), channel_id=1, source_target_pairs={{0,8},{8,16},{16,24},{24,0},{1,9},{9,17},{17,25},{25,1},{2,10},{10... | collective-permute-start | bytes 995336 | tf_op jit(solution)/shard_map/ppermute | solution.py:140
  133.2 22.7 %collective-permute-start.5 = (bf16[288,576]{1,0:T(8,128)(2,1)S(1)}, bf16[288,576]{1,0:T(8,128)(2,1)S(1)}, u32[]{:S(2)}, u32[]{:S(2)}) collective-permute-start(bf16[288,576]{1,0:T(8,128)(2,1)S(1)} %get-tuple-element.13.refs_0_), channel_id=1, source_target_pairs={{0,8},{8,16},{16,24},{24,0},{1,9},{9,17},{17,25},{25,1},{2,10},{10... | collective-permute-start | bytes 995336 | tf_op jit(solution)/shard_map/ppermute | solution.py:140
  135.2 20.8 %collective-permute-start.7 = (bf16[288,576]{1,0:T(8,128)(2,1)S(1)}, bf16[288,576]{1,0:T(8,128)(2,1)S(1)}, u32[]{:S(2)}, u32[]{:S(2)}) collective-permute-start(bf16[288,576]{1,0:T(8,128)(2,1)S(1)} %collective-permute-done.6.refs_3_), channel_id=1, source_target_pairs={{0,24},{8,0},{16,8},{24,16},{1,25},{9,1},{17,9},{25,17},{2,26},{10... | collective-permute-start | bytes 995336 | tf_op jit(solution)/shard_map/ppermute | solution.py:140
  151.4 5.8 %collective-permute-start.11 = (f32[288,256]{1,0:T(8,128)S(1)}, f32[288,256]{1,0:T(8,128)S(1)}, u32[]{:S(2)}, u32[]{:S(2)}) collective-permute-start(f32[288,256]{1,0:T(8,128)S(1)} %shard_map.20), channel_id=1, source_target_pairs={{0,32},{32,0},{1,33},{33,1},{2,34},{34,2},{3,35},{35,3},{4,36},{36... | collective-permute-start | bytes 884744 | tf_op jit(solution)/shard_map/ppermute | solution.py:28
